TPU v7x, 32 devices: a whole 2x2x4 slice. The times are simulated.
32 devices in a mesh: replica: 2 (over y), blk: 4 (over z), contract: 4 (over x, core).
Axes of the slice: x: 2, y: 2, z: 4, core: 2. Of those that a mesh axis runs over, the one named last changes fastest.
Arguments:
- tokens: bfloat16 [128, 8192], P(('replica', 'blk'), 'contract'), parts along dimension 0, may hold values from -6 to 6
- gate_weight: bfloat16 [8192, 28672], P('contract', 'blk'), may hold values from -0.0625 to 0.0625
- up_weight: bfloat16 [8192, 28672], P('contract', 'blk'), may hold values from -0.0625 to 0.0625
- down_weight: bfloat16 [28672, 8192], P('blk', 'contract'), may hold values from -0.03125 to 0.03125
Outputs:
- mixed: bfloat16 [128, 8192], P(('replica', 'blk'), 'contract'), parts along dimension 0
There are 2 independent parts, one for each index of `replica`. A program takes and returns all parts, laid end to end along the dimension named above; an argument that names none is the same for every part. Nothing has to cross between parts.
All inputs are finite; a program needn't handle non-finite values.
Results may differ from a plain program's by a relative error of at most 0.0049.
Values may be sent and summed in bfloat16 or wider, within the bound.
No kernel may reach another device: no remote copies, remote signals or barrier semaphores. Data moves between devices by JAX's collectives and lax.ppermute only.
A program may use at most 192 MiB of HBM per device.

v0:
```python
import jax
import jax.numpy as jnp
from jax import lax
from jax.sharding import PartitionSpec as P


def activate(summed, width):
    return (jax.nn.silu(summed[:, :width]) * summed[:, width:]).astype(jnp.bfloat16)


def shards(tokens, gate_weight, up_weight, down_weight):
    width = gate_weight.shape[1]
    piece = lax.all_gather(tokens, "blk", axis=0, tiled=True)
    gate_part = jnp.dot(piece, gate_weight, preferred_element_type=jnp.float32)
    up_part = jnp.dot(piece, up_weight, preferred_element_type=jnp.float32)
    partial_sums = jnp.concatenate((gate_part, up_part), axis=1)
    summed = lax.psum(partial_sums, "contract")
    hidden = activate(summed, width)
    mixed = lax.psum_scatter(
        jnp.dot(hidden, down_weight, preferred_element_type=jnp.float32),
        "blk",
        scatter_dimension=0,
        tiled=True,
    )
    return mixed.astype(jnp.bfloat16)


def solution(mesh):
    placed = (
        P(("replica", "blk"), "contract"),
        P("contract", "blk"),
        P("contract", "blk"),
        P("blk", "contract"),
    )
    return jax.shard_map(
        shards,
        mesh=mesh,
        in_specs=placed,
        out_specs=P(("replica", "blk"), "contract"),
        check_vma=False,
    )
```

profile of v0, /device:TPU:0, one launch (start us, length us, event | category | flops | bytes accessed | tf_op | source)
XLA Modules:
  0.0 173.9 jit_solution(9673391708477872775)
XLA Ops:
  6.5 0.0 all-reduce.2.cloned.1.call-start
  6.5 15.8 %all_gather.3 = bf16[64,2048]{1,0:T(8,128)(2,1)S(1)} all-gather(bf16[16,2048]{1,0:T(8,128)(2,1)} %param.4), channel_id=1, replica_groups=mesh['replica'=2,'blk'=4,'contract'=4] {'blk'}, dimensions={0}, use_global_device_ids=true | all-gather | bytes 327680 | tf_op jit(solution)/shard_map/all_gather | solution.py:13
  22.4 12.0 %fusion.6 = f32[64,7168]{1,0:T(8,128)S(1)} fusion(bf16[64,2048]{1,0:T(8,128)(2,1)S(1)} %all_gather.3, bf16[2048,7168]{1,0:T(8,128)(2,1)} %param.6), kind=kOutput, calls=%fused_computation.7 | convolution fusion | flops 1879048192 | bytes 31457280 | tf_op jit(solution)/shard_map/dot_general | solution.py:15
  34.4 12.0 %fusion.5 = f32[64,7168]{1,0:T(8,128)S(1)} fusion(bf16[64,2048]{1,0:T(8,128)(2,1)S(1)} %all_gather.3, bf16[2048,7168]{1,0:T(8,128)(2,1)} %param.5), kind=kOutput, calls=%fused_computation.6 | convolution fusion | flops 1879048192 | bytes 31457280 | tf_op jit(solution)/shard_map/dot_general | solution.py:14
  46.4 2.1 %pad_maximum_fusion = f32[64,14336]{1,0:T(8,128)} fusion(f32[64,7168]{1,0:T(8,128)S(1)} %fusion.6, f32[64,7168]{1,0:T(8,128)S(1)} %fusion.5), kind=kLoop, calls=%fused_computation | loop fusion | flops 917504 | bytes 7340032 | tf_op jit(solution)/shard_map/concatenate | solution.py:16
  48.4 0.0 all-reduce.2.cloned.1.call-update
  48.5 0.0 reduce-scatter.2.cloned.1.call-start
  48.5 78.6 %all-reduce.2.cloned.1.call-done = f32[64,14336]{1,0:T(8,128)} async-done(((f32[64,14336]{1,0:T(8,128)}), f32[64,14336]{1,0:T(8,128)}) %all-reduce.2.cloned.1.call-update) | async-done | bytes 3670032 | tf_op jit(solution)/shard_map/psum | solution.py:17
  127.1 16.5 %fusion.1 = f32[64,2048]{1,0:T(8,128)} fusion(bf16[7168,2048]{1,0:T(8,128)(2,1)} %param.7, f32[64,14336]{1,0:T(8,128)} %all-reduce.2.cloned.1.call-done), kind=kOutput, calls=%fused_computation.3 | convolution fusion | flops 1881800704 | bytes 33554432 | tf_op jit(solution)/shard_map/dot_general | solution.py:20
  143.6 0.0 reduce-scatter.2.cloned.1.call-update
  143.6 21.9 %reduce-scatter.2.cloned.1.call-done = f32[16,2048]{1,0:T(8,128)} async-done(((f32[64,2048]{1,0:T(8,128)}), f32[16,2048]{1,0:T(8,128)}) %reduce-scatter.2.cloned.1.call-update) | async-done | bytes 131088 | tf_op jit(solution)/shard_map/reduce_scatter | solution.py:19
  165.6 1.5 convert_element_type.7
Async XLA Ops:
  6.5 120.6 %all-reduce.2.cloned.1.call-start = ((), (), s32[]{:S(2)}) async-start(), calls=%async_computation.1 | async-start | bytes 7340032 | tf_op jit(solution)/shard_map/psum | solution.py:17
  48.5 117.1 %reduce-scatter.2.cloned.1.call-start = ((), (), s32[]{:S(2)}) async-start(), calls=%async_computation.2 | async-start | bytes 655360 | tf_op jit(solution)/shard_map/reduce_scatter | solution.py:19
Sparse Core Ops, SparseCore 0:
  48.6 78.5 all-reduce.1
  143.8 21.7 reduce-scatter.1
where the time goes:
time: 174 us
  waiting for transfers between devices  101 us (58%)
  matrix products  40.5 us (23%)
  blocking collectives  15.8 us (9%)
  between operations  13.4 us (8%)
  other arithmetic  3.63 us (2%)
    psum x1, waiting for transfers between devices, shards(): summed = lax.psum(partial_sums, 'contract')  78.6 us
    reduce_scatter x1, waiting for transfers between devices, shards(): lax.psum_scatter(jnp.dot(hidden, down_weight, preferred_element_type=jnp....  21.9 us
    dot_general x1, matrix products, shards(): jnp.dot(hidden, down_weight, preferred_element_type=jnp.float32)  16.5 us
    all_gather x1, blocking collectives, shards(): piece = lax.all_gather(tokens, 'blk', axis=0, tiled=True)  15.8 us
    dot_general x1, matrix products, shards(): gate_part = jnp.dot(piece, gate_weight, preferred_element_type=jnp.float32)  12 us
    dot_general x1, matrix products, shards(): up_part = jnp.dot(piece, up_weight, preferred_element_type=jnp.float32)  12 us
  transfers between devices with their start and end apart: 2, of which 2 were waited for; matrix products, arithmetic and copies ran while one was open for 0% of the time, Pallas kernels for 0%

commit v1 on v0

v1 whole, which is shorter than its diff:
```python
import functools

import jax
import jax.numpy as jnp
from jax import lax
from jax.experimental import pallas as pl
from jax.experimental.pallas import tpu as pltpu
from jax.sharding import PartitionSpec as P

BF16, F32 = jnp.bfloat16, jnp.float32
MIB = 2**20
CHUNKS = 2
VMEM, ANY = pl.BlockSpec(memory_space=pltpu.VMEM), pl.BlockSpec(memory_space=pl.ANY)


def tile_of(width, most):
    return max(t for t in range(128, most + 1, 128) if width % t == 0)


def reverse(value, count):
    out, bit = 0, 1
    while bit < count:
        out = out * 2 + (value // bit) % 2
        bit *= 2
    return out


def swap(x, axis, count, bit):
    return lax.ppermute(x, axis, [(i, i ^ bit) for i in range(count)])


def stream(sources, buffers, sems, tiles, use):
    depth = sems.shape[0]
    ahead = min(depth, tiles)

    def copies(tile, slot):
        return [
            pltpu.make_async_copy(source(tile), buffer.at[slot], sems.at[slot, i])
            for i, (source, buffer) in enumerate(zip(sources, buffers))
        ]

    for tile in range(ahead):
        for copy in copies(tile, tile):
            copy.start()

    def step(tile, carry):
        slot = lax.rem(tile, depth)
        for copy in copies(tile, slot):
            copy.wait()
        use(tile, slot)

        @pl.when(tile + depth < tiles)
        def _():
            for copy in copies(tile + depth, slot):
                copy.start()

        return carry

    lax.fori_loop(0, tiles, step, 0)


def gate_up_kernel(slots, groups, start, n, bn, *refs):
    pieces = refs[:slots]
    gate, up, keep, send, x, gate_buf, up_buf, sems = refs[slots:]
    block, half = pieces[0].shape[0], keep.shape[0]
    me, per = lax.axis_index("contract"), slots // groups
    for s in range(slots):
        place = reverse(s, slots)
        group = reverse(me ^ (place // per), groups)
        row = pl.multiple_of((group * per + place % per) * block, 16)
        x[pl.ds(row, block), :] = pieces[s][...]

    def source(weight):
        return lambda tile: weight.at[:, pl.ds(pl.multiple_of(start + tile * bn, 128), bn)]

    def use(tile, slot):
        for base, buf in ((0, gate_buf), (n, up_buf)):
            part = jnp.dot(x[...], buf[slot], preferred_element_type=F32)
            columns = pl.ds(pl.multiple_of(base + tile * bn, 128), bn)
            keep[:, columns] = part[:half]
            send[:, columns] = part[half:]

    stream([source(gate), source(up)], [gate_buf, up_buf], sems, n // bn, use)


def gate_up(pieces, gate, up, groups, start, n):
    slots, (block, depth) = len(pieces), pieces[0].shape
    rows, bn, ring = slots * block, tile_of(n, 512), 3
    return pl.pallas_call(
        functools.partial(gate_up_kernel, slots, groups, start, n, bn),
        out_shape=[jax.ShapeDtypeStruct((rows // 2, 2 * n), F32)] * 2,
        in_specs=[VMEM] * slots + [ANY, ANY],
        out_specs=[VMEM, VMEM],
        scratch_shapes=[
            pltpu.VMEM((rows, depth), BF16),
            pltpu.VMEM((ring, depth, bn), BF16),
            pltpu.VMEM((ring, depth, bn), BF16),
            pltpu.SemaphoreType.DMA((ring, 2)),
        ],
        compiler_params=pltpu.CompilerParams(vmem_limit_bytes=30 * MIB),
        cost_estimate=pl.CostEstimate(
            flops=4 * rows * depth * n, bytes_accessed=4 * depth * n, transcendentals=0
        ),
        name="gate_up",
    )(*pieces, gate, up)


def down_kernel(groups, start, bn, last, *refs):
    pieces, refs = refs[:groups], refs[groups:]
    down, refs = refs[0], refs[1:]
    total = None
    if start:
        total, refs = refs[0], refs[1:]
    outs, (hidden, buf, sems) = refs[:-3], refs[-3:]
    share, n = pieces[0].shape
    me = lax.axis_index("contract")
    for j in range(groups):
        row = pl.multiple_of((me ^ j) * share, 16)
        hidden[pl.ds(row, share), :] = pieces[j][...]

    def source(tile):
        return down.at[pl.ds(start, n), pl.ds(pl.multiple_of(tile * bn, 128), bn)]

    def use(tile, slot):
        columns = pl.ds(pl.multiple_of(tile * bn, 128), bn)
        part = jnp.dot(hidden[...], buf[slot], preferred_element_type=F32)
        if total is not None:
            part = part + total[:, columns]
        if last:
            half = outs[0].shape[0]
            outs[0][:, columns] = part[:half]
            outs[1][:, columns] = part[half:].astype(outs[1].dtype)
        else:
            outs[0][:, columns] = part

    stream([source], [buf], sems, down.shape[1] // bn, use)


def down_part(pieces, down, total, start, last, sent):
    groups, (share, n), width = len(pieces), pieces[0].shape, down.shape[1]
    rows, bn, ring = groups * share, tile_of(width, 256), 3
    if last:
        out_shape = [
            jax.ShapeDtypeStruct((rows // 2, width), F32),
            jax.ShapeDtypeStruct((rows // 2, width), sent),
        ]
    else:
        out_shape = [jax.ShapeDtypeStruct((rows, width), F32)]
    given = [] if total is None else [total]
    return pl.pallas_call(
        functools.partial(down_kernel, groups, start, bn, last),
        out_shape=out_shape,
        in_specs=[VMEM] * groups + [ANY] + [VMEM] * len(given),
        out_specs=[VMEM] * len(out_shape),
        scratch_shapes=[
            pltpu.VMEM((rows, n), BF16),
            pltpu.VMEM((ring, n, bn), BF16),
            pltpu.SemaphoreType.DMA((ring, 1)),
        ],
        compiler_params=pltpu.CompilerParams(vmem_limit_bytes=30 * MIB),
        cost_estimate=pl.CostEstimate(
            flops=2 * rows * n * width, bytes_accessed=2 * n * width, transcendentals=0
        ),
        name="down",
    )(*pieces, down, *given)


def gather_tokens(tokens, count):
    pieces, bit = {0: tokens}, count // 2
    while bit:
        pieces.update({s | bit: swap(p, "blk", count, bit) for s, p in list(pieces.items())})
        bit //= 2
    return [pieces[s] for s in range(count)]


def hidden_of(keep, send, groups, n):
    got = swap(send, "contract", groups, 1)
    quarter = keep.shape[0] // 2
    own = keep[:quarter] + got[:quarter]
    away = (keep[quarter:] + got[quarter:]).astype(BF16)
    summed = own + swap(away, "contract", groups, 2).astype(F32)
    mine = (jax.nn.silu(summed[:, :n]) * summed[:, n:]).astype(BF16)
    across = swap(mine, "contract", groups, 2)
    return [
        mine,
        swap(mine, "contract", groups, 1),
        across,
        swap(across, "contract", groups, 1),
    ]


def shards(slots, groups, tokens, gate, up, down):
    pieces = gather_tokens(tokens, slots)
    width = gate.shape[1]
    chunks = CHUNKS if width % (CHUNKS * 128) == 0 else 1
    n = width // chunks
    sent = BF16 if slots <= 4 else F32
    parts = [gate_up(pieces, gate, up, groups, k * n, n) for k in range(chunks)]
    hidden = [hidden_of(keep, send, groups, n) for keep, send in parts]
    total = None
    for k in range(chunks):
        out = down_part(hidden[k], down, total, k * n, k == chunks - 1, sent)
        total = out[0]
    keep, send = out
    bit = 1
    while True:
        keep = keep + swap(send, "blk", slots, bit).astype(F32)
        bit *= 2
        if bit == slots:
            return keep.astype(BF16)
        half = keep.shape[0] // 2
        keep, send = keep[:half], keep[half:].astype(sent)


def solution(mesh):
    placed = (
        P(("replica", "blk"), "contract"),
        P("contract", "blk"),
        P("contract", "blk"),
        P("blk", "contract"),
    )
    return jax.shard_map(
        functools.partial(shards, mesh.shape["blk"], mesh.shape["contract"]),
        mesh=mesh,
        in_specs=placed,
        out_specs=P(("replica", "blk"), "contract"),
        check_vma=False,
    )
```

time: 174 us -> 79.5 us (0.46)
  waiting for transfers between devices: 101 us -> 22.7 us
  matrix products: 40.5 us -> 0 us
  Pallas kernels: 0 us -> 34.4 us
  starting transfers between devices: 0.04 us -> 20.2 us
  blocking collectives: 15.8 us -> 0 us
  between operations: 13.4 us -> 0.11 us
  other arithmetic: 3.63 us -> 1.02 us
    psum x1 -> x0, waiting for transfers between devices: 78.6 us -> none  [shards(): summed = lax.psum(partial_sums, 'contract')]
    dot_general x3 -> x0, matrix products: 40.5 us -> none  [the longest x1 16.5 us: shards(): jnp.dot(hidden, down_weight, preferred_element_type=jnp.float32)]
    pallas_call x0 -> x4, Pallas kernels: none -> 34.4 us  [the longest x2 21.5 us: gate_up(): pl.pallas_call(functools.partial(gate_up_kernel, slots, groups, start, n,...]
    ppermute x0 -> x15, waiting for transfers between devices: none -> 22.7 us  [swap(): return lax.ppermute(x, axis, [(i, i ^ bit) for i in range(count)])]
    reduce_scatter x1 -> x0, waiting for transfers between devices: 21.9 us -> none  [shards(): lax.psum_scatter(jnp.dot(hidden, down_weight, preferred_element_type=jnp....]
    ppermute x0 -> x15, starting transfers between devices: none -> 20.2 us  [swap(): return lax.ppermute(x, axis, [(i, i ^ bit) for i in range(count)])]
    all_gather x1 -> x0, blocking collectives: 15.8 us -> none  [shards(): piece = lax.all_gather(tokens, 'blk', axis=0, tiled=True)]
    concatenate x1 -> x0, other arithmetic: 2.09 us -> none  [shards(): partial_sums = jnp.concatenate((gate_part, up_part), axis=1)]
  transfers between devices with their start and end apart: 2 -> 15, of which waited for: 2 -> 8; matrix products, arithmetic and copies ran while one was open for 0% -> 0% of each run, Pallas kernels for 0% -> 22%
where the time goes in v1:
time: 79.5 us; the launch traced here: 79.3 us
  Pallas kernels  34.4 us (43%)
  waiting for transfers between devices  22.7 us (29%)
  starting transfers between devices  20.2 us (25%)
  other arithmetic  1.02 us (1%)
  local copies, waits for them, and re-layouts  0.85 us (1%)
    ppermute x15, waiting for transfers between devices, swap(): return lax.ppermute(x, axis, [(i, i ^ bit) for i in range(count)])  22.7 us
    pallas_call x2, Pallas kernels, gate_up(): pl.pallas_call(functools.partial(gate_up_kernel, slots, groups, start, n,...  21.5 us
    ppermute x15, starting transfers between devices, swap(): return lax.ppermute(x, axis, [(i, i ^ bit) for i in range(count)])  20.2 us
    pallas_call x2, Pallas kernels, down_part(): pl.pallas_call(functools.partial(down_kernel, groups, start, bn, last), o...  12.9 us
  transfers between devices with their start and end apart: 15, of which 8 were waited for; matrix products, arithmetic and copies ran while one was open for 0% of the time, Pallas kernels for 22%

profile of v1, /device:TPU:0, one launch (start us, length us, event | category | flops | bytes accessed | tf_op | source)
XLA Modules:
  0.0 79.3 jit_solution(14373163869940272275)
XLA Ops:
  0.0 4.0 %collective-permute-start.1 = (bf16[16,2048]{1,0:T(8,128)(2,1)}, bf16[16,2048]{1,0:T(8,128)(2,1)S(1)}, u32[]{:S(2)}, u32[]{:S(2)}) collective-permute-start(bf16[16,2048]{1,0:T(8,128)(2,1)} %refs_0_.3), channel_id=1, source_target_pairs={{0,8},{4,12},{8,0},{12,4},{1,9},{5,13},{9,1},{13,5},{2,10},{6,14},... | collective-permute-start | bytes 196616 | tf_op jit(solution)/shard_map/ppermute | solution.py:29
  4.0 1.6 %collective-permute-start = (bf16[16,2048]{1,0:T(8,128)(2,1)}, bf16[16,2048]{1,0:T(8,128)(2,1)S(1)}, u32[]{:S(2)}, u32[]{:S(2)}) collective-permute-start(bf16[16,2048]{1,0:T(8,128)(2,1)} %refs_0_.3), channel_id=1, source_target_pairs={{0,4},{4,0},{8,12},{12,8},{1,5},{5,1},{9,13},{13,9},{2,6},{6,2},{1... | collective-permute-start | bytes 196616 | tf_op jit(solution)/shard_map/ppermute | solution.py:29
  5.6 1.7 %collective-permute-done.1.refs_2_ = bf16[16,2048]{1,0:T(8,128)(2,1)S(1)} collective-permute-done((bf16[16,2048]{1,0:T(8,128)(2,1)}, bf16[16,2048]{1,0:T(8,128)(2,1)S(1)}, u32[]{:S(2)}, u32[]{:S(2)}) %collective-permute-start.1) | collective-permute-done | bytes 65568 | tf_op jit(solution)/shard_map/ppermute | solution.py:29
  7.3 1.4 %collective-permute-start.2 = (bf16[16,2048]{1,0:T(8,128)(2,1)S(1)}, bf16[16,2048]{1,0:T(8,128)(2,1)S(1)}, u32[]{:S(2)}, u32[]{:S(2)}) collective-permute-start(bf16[16,2048]{1,0:T(8,128)(2,1)S(1)} %collective-permute-done.1.refs_2_), channel_id=1, source_target_pairs={{0,4},{4,0},{8,12},{12,8},{1,5},{5,1},{9,13},{13,9},{2,6},{6,2},{1... | collective-permute-start | bytes 196616 | tf_op jit(solution)/shard_map/ppermute | solution.py:29
  8.7 2.9 %collective-permute-done.2.refs_3_ = bf16[16,2048]{1,0:T(8,128)(2,1)S(1)} collective-permute-done((bf16[16,2048]{1,0:T(8,128)(2,1)S(1)}, bf16[16,2048]{1,0:T(8,128)(2,1)S(1)}, u32[]{:S(2)}, u32[]{:S(2)}) %collective-permute-start.2) | collective-permute-done | bytes 65568 | tf_op jit(solution)/shard_map/ppermute | solution.py:29
  11.6 0.8 %copy-done = bf16[16,2048]{1,0:T(8,128)(2,1)S(1)} copy-done((bf16[16,2048]{1,0:T(8,128)(2,1)S(1)}, bf16[16,2048]{1,0:T(8,128)(2,1)}, u32[]{:S(2)}) %copy-start) | copy-done | bytes 65560
  12.4 10.8 %gate_up.3 = (f32[32,7168]{1,0:T(8,128)S(1)}, f32[32,7168]{1,0:T(8,128)S(1)}) custom-call(bf16[16,2048]{1,0:T(8,128)(2,1)S(1)} %copy-done, bf16[16,2048]{1,0:T(8,128)(2,1)S(1)} %collective-permute-done.refs_1_, bf16[16,2048]{1,0:T(8,128)(2,1)S(1)} %collective-permute-done.1.refs_2_, bf16[16,2048]{1,0:T(8,128)(2,1)S(1)} %collective-permute-done.2.refs_3_, ...), custom_call_target="tpu_custom_call" | custom-call | flops 1879048192 | bytes 29360128 | tf_op jit(solution)/shard_map/gate_up/pallas_call | solution.py:89
  23.2 0.1 collective-permute-start.8
  23.2 10.8 %gate_up.2 = (f32[32,7168]{1,0:T(8,128)S(1)}, f32[32,7168]{1,0:T(8,128)S(1)}) custom-call(bf16[16,2048]{1,0:T(8,128)(2,1)S(1)} %copy-done, bf16[16,2048]{1,0:T(8,128)(2,1)S(1)} %collective-permute-done.refs_1_, bf16[16,2048]{1,0:T(8,128)(2,1)S(1)} %collective-permute-done.1.refs_2_, bf16[16,2048]{1,0:T(8,128)(2,1)S(1)} %collective-permute-done.2.refs_3_, ...), custom_call_target="tpu_custom_call" | custom-call | flops 1879048192 | bytes 29360128 | tf_op jit(solution)/shard_map/gate_up/pallas_call | solution.py:89
  34.0 0.6 collective-permute-start.3
  34.6 0.0 collective-permute-done.8
  34.6 1.9 %collective-permute-start.9 = (bf16[16,7168]{1,0:T(8,128)(2,1)S(1)}, bf16[16,7168]{1,0:T(8,128)(2,1)S(1)}, u32[]{:S(2)}, u32[]{:S(2)}) collective-permute-start(bf16[16,7168]{1,0:T(8,128)(2,1)S(1)} %fusion), channel_id=1, source_target_pairs={{0,2},{1,3},{2,0},{3,1},{4,6},{5,7},{6,4},{7,5},{8,10},{9,11},{10,... | collective-permute-start | bytes 688136 | tf_op jit(solution)/shard_map/ppermute | solution.py:29
  36.5 0.1 collective-permute-done.3
  36.7 1.9 %collective-permute-start.4 = (bf16[16,7168]{1,0:T(8,128)(2,1)S(1)}, bf16[16,7168]{1,0:T(8,128)(2,1)S(1)}, u32[]{:S(2)}, u32[]{:S(2)}) collective-permute-start(bf16[16,7168]{1,0:T(8,128)(2,1)S(1)} %fusion.2), channel_id=1, source_target_pairs={{0,2},{1,3},{2,0},{3,1},{4,6},{5,7},{6,4},{7,5},{8,10},{9,11},{10,... | collective-permute-start | bytes 688136 | tf_op jit(solution)/shard_map/ppermute | solution.py:29
  38.6 4.5 %collective-permute-done.9 = bf16[16,7168]{1,0:T(8,128)(2,1)S(1)} collective-permute-done((bf16[16,7168]{1,0:T(8,128)(2,1)S(1)}, bf16[16,7168]{1,0:T(8,128)(2,1)S(1)}, u32[]{:S(2)}, u32[]{:S(2)}) %collective-permute-start.9) | collective-permute-done | bytes 229408 | tf_op jit(solution)/shard_map/ppermute | solution.py:29
  43.1 0.1 fusion.1
  43.2 0.1 fusion.4.refs_0_
  43.3 1.9 %collective-permute-start.11 = (bf16[16,3584]{1,0:T(8,128)(2,1)S(1)}, bf16[16,3584]{1,0:T(8,128)(2,1)S(1)}, u32[]{:S(2)}, u32[]{:S(2)}) collective-permute-start(bf16[16,3584]{1,0:T(8,128)(2,1)S(1)} %fusion.4.refs_0_), channel_id=1, source_target_pairs={{0,2},{1,3},{2,0},{3,1},{4,6},{5,7},{6,4},{7,5},{8,10},{9,11},{10,... | collective-permute-start | bytes 344072 | tf_op jit(solution)/shard_map/ppermute | solution.py:29
  45.2 2.8 %collective-permute-done.4 = bf16[16,7168]{1,0:T(8,128)(2,1)S(1)} collective-permute-done((bf16[16,7168]{1,0:T(8,128)(2,1)S(1)}, bf16[16,7168]{1,0:T(8,128)(2,1)S(1)}, u32[]{:S(2)}, u32[]{:S(2)}) %collective-permute-start.4) | collective-permute-done | bytes 229408 | tf_op jit(solution)/shard_map/ppermute | solution.py:29
  48.0 0.1 fusion.3
  48.1 0.1 fusion.5.refs_0_
  48.2 1.9 %collective-permute-start.6 = (bf16[16,3584]{1,0:T(8,128)(2,1)S(1)}, bf16[16,3584]{1,0:T(8,128)(2,1)S(1)}, u32[]{:S(2)}, u32[]{:S(2)}) collective-permute-start(bf16[16,3584]{1,0:T(8,128)(2,1)S(1)} %fusion.5.refs_0_), channel_id=1, source_target_pairs={{0,2},{1,3},{2,0},{3,1},{4,6},{5,7},{6,4},{7,5},{8,10},{9,11},{10,... | collective-permute-start | bytes 344072 | tf_op jit(solution)/shard_map/ppermute | solution.py:29
  50.1 0.5 collective-permute-start.12
  50.6 0.0 collective-permute-start.5
  50.6 2.4 %collective-permute-done.6.refs_2_ = bf16[16,3584]{1,0:T(8,128)(2,1)S(1)} collective-permute-done((bf16[16,3584]{1,0:T(8,128)(2,1)S(1)}, bf16[16,3584]{1,0:T(8,128)(2,1)S(1)}, u32[]{:S(2)}, u32[]{:S(2)}) %collective-permute-start.6) | collective-permute-done | bytes 114720 | tf_op jit(solution)/shard_map/ppermute | solution.py:29
  53.1 6.5 %down.2.refs_5_ = f32[64,2048]{1,0:T(8,128)S(1)} custom-call(bf16[16,3584]{1,0:T(8,128)(2,1)S(1)} %fusion.4.refs_0_, bf16[16,3584]{1,0:T(8,128)(2,1)S(1)} %collective-permute-done.10.refs_1_, bf16[16,3584]{1,0:T(8,128)(2,1)S(1)} %collective-permute-done.11.refs_2_, bf16[16,3584]{1,0:T(8,128)(2,1)S(1)} %collective-permute-done.12.refs_3_, ...), custom_call_target="tpu_custom_call" | custom-call | flops 939524096 | bytes 14680064 | tf_op jit(solution)/shard_map/down/pallas_call | solution.py:150
  59.6 6.5 %down.3 = (f32[32,2048]{1,0:T(8,128)S(1)}, bf16[32,2048]{1,0:T(8,128)(2,1)S(1)}) custom-call(bf16[16,3584]{1,0:T(8,128)(2,1)S(1)} %fusion.5.refs_0_, bf16[16,3584]{1,0:T(8,128)(2,1)S(1)} %collective-permute-done.5.refs_1_, bf16[16,3584]{1,0:T(8,128)(2,1)S(1)} %collective-permute-done.6.refs_2_, bf16[16,3584]{1,0:T(8,128)(2,1)S(1)} %collective-permute-done.7.refs_3_, ...), custom_call_target="tpu_custom_call" | custom-call | flops 939524096 | bytes 14680064 | tf_op jit(solution)/shard_map/down/pallas_call | solution.py:150
  66.0 1.5 %collective-permute-start.13 = (bf16[32,2048]{1,0:T(8,128)(2,1)S(1)}, bf16[32,2048]{1,0:T(8,128)(2,1)S(1)}, u32[]{:S(2)}, u32[]{:S(2)}) collective-permute-start(bf16[32,2048]{1,0:T(8,128)(2,1)S(1)} %get-tuple-element.16), channel_id=1, source_target_pairs={{0,4},{4,0},{8,12},{12,8},{1,5},{5,1},{9,13},{13,9},{2,6},{6,2},{1... | collective-permute-start | bytes 393224 | tf_op jit(solution)/shard_map/ppermute | solution.py:29
  67.5 4.5 %collective-permute-done.13 = bf16[32,2048]{1,0:T(8,128)(2,1)S(1)} collective-permute-done((bf16[32,2048]{1,0:T(8,128)(2,1)S(1)}, bf16[32,2048]{1,0:T(8,128)(2,1)S(1)}, u32[]{:S(2)}, u32[]{:S(2)}) %collective-permute-start.13) | collective-permute-done | bytes 131104 | tf_op jit(solution)/shard_map/ppermute | solution.py:29
  72.0 2.9 %collective-permute-start.14 = (bf16[16,2048]{1,0:T(8,128)(2,1)S(1)}, bf16[16,2048]{1,0:T(8,128)(2,1)S(1)}, u32[]{:S(2)}, u32[]{:S(2)}) collective-permute-start(bf16[16,2048]{1,0:T(8,128)(2,1)S(1)} %slice.95), channel_id=1, source_target_pairs={{0,8},{4,12},{8,0},{12,4},{1,9},{5,13},{9,1},{13,5},{2,10},{6,14},... | collective-permute-start | bytes 196616 | tf_op jit(solution)/shard_map/ppermute | solution.py:29
  74.9 3.7 %collective-permute-done.14 = bf16[16,2048]{1,0:T(8,128)(2,1)S(1)} collective-permute-done((bf16[16,2048]{1,0:T(8,128)(2,1)S(1)}, bf16[16,2048]{1,0:T(8,128)(2,1)S(1)}, u32[]{:S(2)}, u32[]{:S(2)}) %collective-permute-start.14) | collective-permute-done | bytes 65568 | tf_op jit(solution)/shard_map/ppermute | solution.py:29
  78.7 0.6 fusion.6
  (13 shorter events, 0.1 us)
Async XLA Ops:
  0.0 7.3 %collective-permute-start.1 = (bf16[16,2048]{1,0:T(8,128)(2,1)}, bf16[16,2048]{1,0:T(8,128)(2,1)S(1)}, u32[]{:S(2)}, u32[]{:S(2)}) collective-permute-start(bf16[16,2048]{1,0:T(8,128)(2,1)} %refs_0_.3), channel_id=1, source_target_pairs={{0,8},{4,12},{8,0},{12,4},{1,9},{5,13},{9,1},{13,5},{2,10},{6,14},... | collective-permute-start | bytes 196616 | tf_op jit(solution)/shard_map/ppermute | solution.py:29
  4.0 4.6 %collective-permute-start = (bf16[16,2048]{1,0:T(8,128)(2,1)}, bf16[16,2048]{1,0:T(8,128)(2,1)S(1)}, u32[]{:S(2)}, u32[]{:S(2)}) collective-permute-start(bf16[16,2048]{1,0:T(8,128)(2,1)} %refs_0_.3), channel_id=1, source_target_pairs={{0,4},{4,0},{8,12},{12,8},{1,5},{5,1},{9,13},{13,9},{2,6},{6,2},{1... | collective-permute-start | bytes 196616 | tf_op jit(solution)/shard_map/ppermute | solution.py:29
  7.3 4.3 %collective-permute-start.2 = (bf16[16,2048]{1,0:T(8,128)(2,1)S(1)}, bf16[16,2048]{1,0:T(8,128)(2,1)S(1)}, u32[]{:S(2)}, u32[]{:S(2)}) collective-permute-start(bf16[16,2048]{1,0:T(8,128)(2,1)S(1)} %collective-permute-done.1.refs_2_), channel_id=1, source_target_pairs={{0,4},{4,0},{8,12},{12,8},{1,5},{5,1},{9,13},{13,9},{2,6},{6,2},{1... | collective-permute-start | bytes 196616 | tf_op jit(solution)/shard_map/ppermute | solution.py:29
  11.6 0.8 %copy-start = (bf16[16,2048]{1,0:T(8,128)(2,1)S(1)}, bf16[16,2048]{1,0:T(8,128)(2,1)}, u32[]{:S(2)}) copy-start(bf16[16,2048]{1,0:T(8,128)(2,1)} %refs_0_.3) | copy-start | bytes 196612
  23.2 11.4 %collective-permute-start.8 = (f32[32,7168]{1,0:T(8,128)S(1)}, f32[32,7168]{1,0:T(8,128)S(1)}, u32[]{:S(2)}, u32[]{:S(2)}) collective-permute-start(f32[32,7168]{1,0:T(8,128)S(1)} %get-tuple-element.14), channel_id=1, source_target_pairs={{0,1},{1,0},{2,3},{3,2},{4,5},{5,4},{6,7},{7,6},{8,9},{9,8},{10,11... | collective-permute-start | bytes 2752520 | tf_op jit(solution)/shard_map/ppermute | solution.py:29
  34.0 2.7 %collective-permute-start.3 = (f32[32,7168]{1,0:T(8,128)S(1)}, f32[32,7168]{1,0:T(8,128)S(1)}, u32[]{:S(2)}, u32[]{:S(2)}) collective-permute-start(f32[32,7168]{1,0:T(8,128)S(1)} %get-tuple-element.12), channel_id=1, source_target_pairs={{0,1},{1,0},{2,3},{3,2},{4,5},{5,4},{6,7},{7,6},{8,9},{9,8},{10,11... | collective-permute-start | bytes 2752520 | tf_op jit(solution)/shard_map/ppermute | solution.py:29
  34.6 8.5 %collective-permute-start.9 = (bf16[16,7168]{1,0:T(8,128)(2,1)S(1)}, bf16[16,7168]{1,0:T(8,128)(2,1)S(1)}, u32[]{:S(2)}, u32[]{:S(2)}) collective-permute-start(bf16[16,7168]{1,0:T(8,128)(2,1)S(1)} %fusion), channel_id=1, source_target_pairs={{0,2},{1,3},{2,0},{3,1},{4,6},{5,7},{6,4},{7,5},{8,10},{9,11},{10,... | collective-permute-start | bytes 688136 | tf_op jit(solution)/shard_map/ppermute | solution.py:29
  36.7 11.3 %collective-permute-start.4 = (bf16[16,7168]{1,0:T(8,128)(2,1)S(1)}, bf16[16,7168]{1,0:T(8,128)(2,1)S(1)}, u32[]{:S(2)}, u32[]{:S(2)}) collective-permute-start(bf16[16,7168]{1,0:T(8,128)(2,1)S(1)} %fusion.2), channel_id=1, source_target_pairs={{0,2},{1,3},{2,0},{3,1},{4,6},{5,7},{6,4},{7,5},{8,10},{9,11},{10,... | collective-permute-start | bytes 688136 | tf_op jit(solution)/shard_map/ppermute | solution.py:29
  43.3 6.9 %collective-permute-start.11 = (bf16[16,3584]{1,0:T(8,128)(2,1)S(1)}, bf16[16,3584]{1,0:T(8,128)(2,1)S(1)}, u32[]{:S(2)}, u32[]{:S(2)}) collective-permute-start(bf16[16,3584]{1,0:T(8,128)(2,1)S(1)} %fusion.4.refs_0_), channel_id=1, source_target_pairs={{0,2},{1,3},{2,0},{3,1},{4,6},{5,7},{6,4},{7,5},{8,10},{9,11},{10,... | collective-permute-start | bytes 344072 | tf_op jit(solution)/shard_map/ppermute | solution.py:29
  48.2 4.9 %collective-permute-start.6 = (bf16[16,3584]{1,0:T(8,128)(2,1)S(1)}, bf16[16,3584]{1,0:T(8,128)(2,1)S(1)}, u32[]{:S(2)}, u32[]{:S(2)}) collective-permute-start(bf16[16,3584]{1,0:T(8,128)(2,1)S(1)} %fusion.5.refs_0_), channel_id=1, source_target_pairs={{0,2},{1,3},{2,0},{3,1},{4,6},{5,7},{6,4},{7,5},{8,10},{9,11},{10,... | collective-permute-start | bytes 344072 | tf_op jit(solution)/shard_map/ppermute | solution.py:29
  50.1 2.9 %collective-permute-start.10 = (bf16[16,3584]{1,0:T(8,128)(2,1)S(1)}, bf16[16,3584]{1,0:T(8,128)(2,1)S(1)}, u32[]{:S(2)}, u32[]{:S(2)}) collective-permute-start(bf16[16,3584]{1,0:T(8,128)(2,1)S(1)} %fusion.4.refs_0_), channel_id=1, source_target_pairs={{0,1},{1,0},{2,3},{3,2},{4,5},{5,4},{6,7},{7,6},{8,9},{9,8},{10,11... | collective-permute-start | bytes 344072 | tf_op jit(solution)/shard_map/ppermute | solution.py:29
  50.1 2.9 %collective-permute-start.12 = (bf16[16,3584]{1,0:T(8,128)(2,1)S(1)}, bf16[16,3584]{1,0:T(8,128)(2,1)S(1)}, u32[]{:S(2)}, u32[]{:S(2)}) collective-permute-start(bf16[16,3584]{1,0:T(8,128)(2,1)S(1)} %collective-permute-done.11.refs_2_), channel_id=1, source_target_pairs={{0,1},{1,0},{2,3},{3,2},{4,5},{5,4},{6,7},{7,6},{8,9},{9,8},{10,11... | collective-permute-start | bytes 344072 | tf_op jit(solution)/shard_map/ppermute | solution.py:29
  50.6 8.9 %collective-permute-start.5 = (bf16[16,3584]{1,0:T(8,128)(2,1)S(1)}, bf16[16,3584]{1,0:T(8,128)(2,1)S(1)}, u32[]{:S(2)}, u32[]{:S(2)}) collective-permute-start(bf16[16,3584]{1,0:T(8,128)(2,1)S(1)} %fusion.5.refs_0_), channel_id=1, source_target_pairs={{0,1},{1,0},{2,3},{3,2},{4,5},{5,4},{6,7},{7,6},{8,9},{9,8},{10,11... | collective-permute-start | bytes 344072 | tf_op jit(solution)/shard_map/ppermute | solution.py:29
  53.0 6.5 %collective-permute-start.7 = (bf16[16,3584]{1,0:T(8,128)(2,1)S(1)}, bf16[16,3584]{1,0:T(8,128)(2,1)S(1)}, u32[]{:S(2)}, u32[]{:S(2)}) collective-permute-start(bf16[16,3584]{1,0:T(8,128)(2,1)S(1)} %collective-permute-done.6.refs_2_), channel_id=1, source_target_pairs={{0,1},{1,0},{2,3},{3,2},{4,5},{5,4},{6,7},{7,6},{8,9},{9,8},{10,11... | collective-permute-start | bytes 344072 | tf_op jit(solution)/shard_map/ppermute | solution.py:29
  66.0 6.0 %collective-permute-start.13 = (bf16[32,2048]{1,0:T(8,128)(2,1)S(1)}, bf16[32,2048]{1,0:T(8,128)(2,1)S(1)}, u32[]{:S(2)}, u32[]{:S(2)}) collective-permute-start(bf16[32,2048]{1,0:T(8,128)(2,1)S(1)} %get-tuple-element.16), channel_id=1, source_target_pairs={{0,4},{4,0},{8,12},{12,8},{1,5},{5,1},{9,13},{13,9},{2,6},{6,2},{1... | collective-permute-start | bytes 393224 | tf_op jit(solution)/shard_map/ppermute | solution.py:29
  72.0 6.6 %collective-permute-start.14 = (bf16[16,2048]{1,0:T(8,128)(2,1)S(1)}, bf16[16,2048]{1,0:T(8,128)(2,1)S(1)}, u32[]{:S(2)}, u32[]{:S(2)}) collective-permute-start(bf16[16,2048]{1,0:T(8,128)(2,1)S(1)} %slice.95), channel_id=1, source_target_pairs={{0,8},{4,12},{8,0},{12,4},{1,9},{5,13},{9,1},{13,5},{2,10},{6,14},... | collective-permute-start | bytes 196616 | tf_op jit(solution)/shard_map/ppermute | solution.py:29

commit v2 on v0

v2 whole, which is shorter than its diff:
```python
import functools

import jax
import jax.numpy as jnp
from jax import lax
from jax.experimental import pallas as pl
from jax.experimental.pallas import tpu as pltpu
from jax.sharding import PartitionSpec as P

BF16, F32 = jnp.bfloat16, jnp.float32
MIB = 2**20
SPLIT = (4, 4)
VMEM, ANY = pl.BlockSpec(memory_space=pltpu.VMEM), pl.BlockSpec(memory_space=pl.ANY)
LONG = pl.CostEstimate(flops=20_000_000_000, bytes_accessed=1000, transcendentals=0)


def tile_of(width, most):
    return max(t for t in range(128, most + 1, 128) if width % t == 0)


def reverse(value, count):
    out, bit = 0, 1
    while bit < count:
        out = out * 2 + (value // bit) % 2
        bit *= 2
    return out


def swap(x, axis, count, bit):
    return lax.ppermute(x, axis, [(i, i ^ bit) for i in range(count)])


def local(kernel, outs, *given, name, limit=8 * MIB, cost=None):
    arrays = [a[0] if isinstance(a, list) else a for a in given]
    return pl.pallas_call(
        kernel,
        out_shape=[jax.ShapeDtypeStruct(*o) for o in outs],
        in_specs=[ANY if isinstance(a, list) else VMEM for a in given],
        out_specs=[VMEM] * len(outs),
        compiler_params=pltpu.CompilerParams(vmem_limit_bytes=limit),
        cost_estimate=cost,
        name=name,
    )(*arrays)


def head(tokens):
    def kernel(given, out):
        out[...] = given[...]

    return local(kernel, [(tokens.shape, BF16)], tokens, name="head", cost=LONG)[0]


def gate_up_kernel(slots, groups, waits, start, n, bn, *refs):
    pieces, refs = refs[:slots], refs[slots + waits :]
    gate, up, keep, send, x, buffers, sems = refs
    block, half = pieces[0].shape[0], keep.shape[0]
    tiles, ring = n // bn, sems.shape[0]

    def copy(tile):
        columns = pl.ds(start + tile * bn, bn)
        slot = tile % ring
        return pltpu.make_async_copy(up.at[:, columns], buffers.at[slot], sems.at[slot])

    for tile in range(min(ring, tiles)):
        copy(tile).start()
    me, per = lax.axis_index("contract"), slots // groups
    for s in range(slots):
        place = reverse(s, slots)
        group = reverse(me ^ (place // per), groups)
        row = pl.multiple_of((group * per + place % per) * block, 16)
        x[pl.ds(row, block), :] = pieces[s][...]

    def put(column, part):
        keep[:, pl.ds(column, bn)] = part[:half]
        send[:, pl.ds(column, bn)] = part[half:]

    for tile in range(tiles):
        at = tile * bn
        put(at, jnp.dot(x[...], gate[:, pl.ds(start + at, bn)], preferred_element_type=F32))
        copy(tile).wait()
        put(n + at, jnp.dot(x[...], buffers[tile % ring], preferred_element_type=F32))
        if tile + ring < tiles:
            copy(tile + ring).start()


def gate_up(pieces, waits, gate, up, groups, start, n):
    slots, (block, depth) = len(pieces), pieces[0].shape
    rows, bn, ring = slots * block, tile_of(n, 512), 4
    return pl.pallas_call(
        functools.partial(gate_up_kernel, slots, groups, len(waits), start, n, bn),
        out_shape=[jax.ShapeDtypeStruct((rows // 2, 2 * n), F32)] * 2,
        in_specs=[VMEM] * slots + [ANY] * len(waits) + [VMEM, ANY],
        out_specs=[VMEM, VMEM],
        scratch_shapes=[
            pltpu.VMEM((rows, depth), BF16),
            pltpu.VMEM((ring, depth, bn), BF16),
            pltpu.SemaphoreType.DMA((ring,)),
        ],
        compiler_params=pltpu.CompilerParams(vmem_limit_bytes=14 * MIB),
        cost_estimate=pl.CostEstimate(
            flops=4 * rows * depth * n, bytes_accessed=4 * depth * n, transcendentals=0
        ),
        name="gate_up",
    )(*pieces, *waits, gate, up)


def fold(keep, got, cost=None):
    def kernel(keep, got, own, away):
        quarter = own.shape[0]
        own[...] = keep[:quarter] + got[:quarter]
        away[...] = (keep[quarter:] + got[quarter:]).astype(BF16)

    rows, width = keep.shape
    shape = (rows // 2, width)
    return local(kernel, [(shape, F32), (shape, BF16)], keep, got, name="fold", cost=cost)


def activate(own, got):
    def kernel(own, got, out):
        n = out.shape[1]
        gate = own[:, :n] + got[:, :n].astype(F32)
        up = own[:, n:] + got[:, n:].astype(F32)
        out[...] = (jax.nn.silu(gate) * up).astype(BF16)

    rows, width = own.shape
    return local(kernel, [((rows, width // 2), BF16)], own, got, name="activate", cost=LONG)[0]


def down_kernel(chunks, groups, start, bn, places, *refs):
    pieces, refs = refs[: chunks * groups], refs[chunks * groups :]
    down, refs = refs[0], refs[1:]
    total = None
    if start:
        total, refs = refs[0], refs[1:]
    outs, hidden = refs[:-1], refs[-1]
    me, column = lax.axis_index("contract"), 0
    for k in range(chunks):
        share, n = pieces[k * groups].shape
        for j in range(groups):
            row = pl.multiple_of((me ^ j) * share, 16)
            hidden[pl.ds(row, share), pl.ds(column, n)] = pieces[k * groups + j][...]
        column += n
    for column in range(0, down.shape[1], bn):
        columns = pl.ds(column, bn)
        weight = down[pl.ds(start, hidden.shape[1]), columns]
        part = jnp.dot(hidden[...], weight, preferred_element_type=F32)
        if total is not None:
            part = part + total[:, columns]
        for out, (row, count) in zip(outs, places):
            out[:, columns] = part[row : row + count].astype(out.dtype)


def down_part(pieces, down, total, start, places):
    groups, share, n, width = len(pieces[0]), pieces[0][0].shape[0], sum(p[0].shape[1] for p in pieces), down.shape[1]
    rows, bn = groups * share, tile_of(width, 512)
    given = [] if total is None else [total]
    return pl.pallas_call(
        functools.partial(down_kernel, len(pieces), groups, start, bn, [p[:2] for p in places]),
        out_shape=[jax.ShapeDtypeStruct((count, width), kind) for _, count, kind in places],
        in_specs=[VMEM] * (groups * len(pieces)) + [VMEM] + [VMEM] * len(given),
        out_specs=[VMEM] * len(places),
        scratch_shapes=[pltpu.VMEM((rows, n), BF16)],
        compiler_params=pltpu.CompilerParams(vmem_limit_bytes=8 * MIB),
        cost_estimate=pl.CostEstimate(
            flops=2 * rows * n * width, bytes_accessed=2 * n * width, transcendentals=0
        ),
        name="down",
    )(*(q for p in pieces for q in p), down, *given)


def gather_tokens(tokens, count):
    pieces, bit = {0: tokens}, count // 2
    while bit:
        pieces.update({s | bit: swap(p, "blk", count, bit) for s, p in list(pieces.items())})
        bit //= 2
    return [pieces[s] for s in range(count)]


def shards(slots, groups, tokens, gate, up, down):
    rows, width = slots * tokens.shape[0], gate.shape[1]
    gate = pltpu.with_memory_space_constraint(gate, pltpu.VMEM)
    up = pltpu.with_memory_space_constraint(up, pltpu.HBM)
    down = pltpu.with_memory_space_constraint(down, pltpu.VMEM)
    pieces = gather_tokens(head(tokens), slots)
    unit = sum(SPLIT) * 128
    sizes = [width // sum(SPLIT) * s for s in SPLIT] if width % unit == 0 else [width]
    starts = [sum(sizes[:k]) for k in range(len(sizes))]
    waits, folded = [], []
    for k, (start, n) in enumerate(zip(starts, sizes)):
        keep, send = gate_up(pieces, waits, gate, up, groups, start, n)
        got = swap(send, "contract", groups, 1)
        folded.append(fold(keep, got))
        waits = [folded[-1][1]]
    if slots <= 4:
        block = tokens.shape[0]
        places = [(reverse(s, slots) * block, block, BF16 if s else F32) for s in range(slots)]
    else:
        places = [(0, rows // 2, F32), (rows // 2, rows // 2, F32)]
    hiddens = []
    for k, (own, away) in enumerate(folded):
        mine = activate(own, swap(away, "contract", groups, 2))
        across = swap(mine, "contract", groups, 2)
        hidden = [mine, swap(mine, "contract", groups, 1), across, swap(across, "contract", groups, 1)]
        hiddens.append(hidden)
    out = down_part(hiddens, down, None, 0, places)
    if slots <= 4:
        return sum((swap(out[s], "blk", slots, s).astype(F32) for s in range(1, slots)), out[0]).astype(BF16)
    keep, send = out
    bit = 1
    while True:
        keep = keep + swap(send, "blk", slots, bit)
        bit *= 2
        if bit == slots:
            return keep.astype(BF16)
        half = keep.shape[0] // 2
        keep, send = keep[:half], keep[half:]


def solution(mesh):
    placed = (
        P(("replica", "blk"), "contract"),
        P("contract", "blk"),
        P("contract", "blk"),
        P("blk", "contract"),
    )
    return jax.shard_map(
        functools.partial(shards, mesh.shape["blk"], mesh.shape["contract"]),
        mesh=mesh,
        in_specs=placed,
        out_specs=P(("replica", "blk"), "contract"),
        check_vma=False,
    )
```

time: 174 us -> 66.1 us (0.38)
  waiting for transfers between devices: 101 us -> 24.2 us
  matrix products: 40.5 us -> 0 us
  Pallas kernels: 0 us -> 20 us
  starting transfers between devices: 0.04 us -> 20 us
  blocking collectives: 15.8 us -> 0 us
  between operations: 13.4 us -> 0.13 us
  other arithmetic: 3.63 us -> 0.66 us
    psum x1 -> x0, waiting for transfers between devices: 78.6 us -> none  [shards(): summed = lax.psum(partial_sums, 'contract')]
    dot_general x3 -> x0, matrix products: 40.5 us -> none  [the longest x1 16.5 us: shards(): jnp.dot(hidden, down_weight, preferred_element_type=jnp.float32)]
    ppermute x0 -> x16, waiting for transfers between devices: none -> 24.2 us  [swap(): return lax.ppermute(x, axis, [(i, i ^ bit) for i in range(count)])]
    reduce_scatter x1 -> x0, waiting for transfers between devices: 21.9 us -> none  [shards(): lax.psum_scatter(jnp.dot(hidden, down_weight, preferred_element_type=jnp....]
    ppermute x0 -> x16, starting transfers between devices: none -> 20 us  [swap(): return lax.ppermute(x, axis, [(i, i ^ bit) for i in range(count)])]
    pallas_call x0 -> x8, Pallas kernels: none -> 20 us  [the longest x2 14.4 us: gate_up(): pl.pallas_call(functools.partial(gate_up_kernel, slots, groups, len(waits...]
    all_gather x1 -> x0, blocking collectives: 15.8 us -> none  [shards(): piece = lax.all_gather(tokens, 'blk', axis=0, tiled=True)]
    concatenate x1 -> x0, other arithmetic: 2.09 us -> none  [shards(): partial_sums = jnp.concatenate((gate_part, up_part), axis=1)]
  transfers between devices with their start and end apart: 2 -> 16, of which waited for: 2 -> 10; matrix products, arithmetic and copies ran while one was open for 0% -> 0% of each run, Pallas kernels for 0% -> 0%
where the time goes in v2:
time: 66.1 us; the launch traced here: 66 us
  waiting for transfers between devices  24.2 us (37%)
  Pallas kernels  20 us (30%)
  starting transfers between devices  20 us (30%)
  local copies, waits for them, and re-layouts  1.02 us (2%)
    ppermute x16, waiting for transfers between devices, swap(): return lax.ppermute(x, axis, [(i, i ^ bit) for i in range(count)])  24.2 us
    ppermute x16, starting transfers between devices, swap(): return lax.ppermute(x, axis, [(i, i ^ bit) for i in range(count)])  20 us
    pallas_call x2, Pallas kernels, gate_up(): pl.pallas_call(functools.partial(gate_up_kernel, slots, groups, len(waits...  14.4 us
    pallas_call x1, Pallas kernels, down_part(): pl.pallas_call(functools.partial(down_kernel, len(pieces), groups, start,...  5.26 us
  transfers between devices with their start and end apart: 16, of which 10 were waited for; matrix products, arithmetic and copies ran while one was open for 0% of the time, Pallas kernels for 0%

profile of v2, /device:TPU:0, one launch (start us, length us, event | category | flops | bytes accessed | tf_op | source)
XLA Modules:
  0.0 66.0 jit_solution(13040046925060305014)
XLA Ops:
  0.0 1.0 %copy-done.1 = bf16[16,2048]{1,0:T(8,128)(2,1)S(1)} copy-done((bf16[16,2048]{1,0:T(8,128)(2,1)S(1)}, bf16[16,2048]{1,0:T(8,128)(2,1)}, u32[]{:S(2)}) %copy-start.1) | copy-done | bytes 65560
  1.0 4.0 %collective-permute-start.1 = (bf16[16,2048]{1,0:T(8,128)(2,1)S(1)}, bf16[16,2048]{1,0:T(8,128)(2,1)S(1)}, u32[]{:S(2)}, u32[]{:S(2)}) collective-permute-start(bf16[16,2048]{1,0:T(8,128)(2,1)S(1)} %head.1.refs_0_), channel_id=1, source_target_pairs={{0,8},{4,12},{8,0},{12,4},{1,9},{5,13},{9,1},{13,5},{2,10},{6,14},... | collective-permute-start | bytes 196616 | tf_op jit(solution)/shard_map/ppermute | solution.py:30
  5.0 1.6 %collective-permute-start = (bf16[16,2048]{1,0:T(8,128)(2,1)S(1)}, bf16[16,2048]{1,0:T(8,128)(2,1)S(1)}, u32[]{:S(2)}, u32[]{:S(2)}) collective-permute-start(bf16[16,2048]{1,0:T(8,128)(2,1)S(1)} %head.1.refs_0_), channel_id=1, source_target_pairs={{0,4},{4,0},{8,12},{12,8},{1,5},{5,1},{9,13},{13,9},{2,6},{6,2},{1... | collective-permute-start | bytes 196616 | tf_op jit(solution)/shard_map/ppermute | solution.py:30
  6.6 1.5 %collective-permute-done.1.refs_2_ = bf16[16,2048]{1,0:T(8,128)(2,1)S(1)} collective-permute-done((bf16[16,2048]{1,0:T(8,128)(2,1)S(1)}, bf16[16,2048]{1,0:T(8,128)(2,1)S(1)}, u32[]{:S(2)}, u32[]{:S(2)}) %collective-permute-start.1) | collective-permute-done | bytes 65568 | tf_op jit(solution)/shard_map/ppermute | solution.py:30
  8.1 1.4 %collective-permute-start.2 = (bf16[16,2048]{1,0:T(8,128)(2,1)S(1)}, bf16[16,2048]{1,0:T(8,128)(2,1)S(1)}, u32[]{:S(2)}, u32[]{:S(2)}) collective-permute-start(bf16[16,2048]{1,0:T(8,128)(2,1)S(1)} %collective-permute-done.1.refs_2_), channel_id=1, source_target_pairs={{0,4},{4,0},{8,12},{12,8},{1,5},{5,1},{9,13},{13,9},{2,6},{6,2},{1... | collective-permute-start | bytes 196616 | tf_op jit(solution)/shard_map/ppermute | solution.py:30
  9.5 2.9 %collective-permute-done.2.refs_3_ = bf16[16,2048]{1,0:T(8,128)(2,1)S(1)} collective-permute-done((bf16[16,2048]{1,0:T(8,128)(2,1)S(1)}, bf16[16,2048]{1,0:T(8,128)(2,1)S(1)}, u32[]{:S(2)}, u32[]{:S(2)}) %collective-permute-start.2) | collective-permute-done | bytes 65568 | tf_op jit(solution)/shard_map/ppermute | solution.py:30
  12.4 7.2 %gate_up.2 = (f32[32,7168]{1,0:T(8,128)S(1)}, f32[32,7168]{1,0:T(8,128)S(1)}) custom-call(bf16[16,2048]{1,0:T(8,128)(2,1)S(1)} %head.1.refs_0_, bf16[16,2048]{1,0:T(8,128)(2,1)S(1)} %collective-permute-done.refs_1_, bf16[16,2048]{1,0:T(8,128)(2,1)S(1)} %collective-permute-done.1.refs_2_, bf16[16,2048]{1,0:T(8,128)(2,1)S(1)} %collective-permute-done.2.refs_3_, ...), custom_call_target="tpu_custom_call" | custom-call | flops 1879048192 | bytes 29360128 | tf_op jit(solution)/shard_map/gate_up/pallas_call | solution.py:89
  19.6 0.1 collective-permute-start.3
  19.6 2.5 %collective-permute-done.3.got = f32[32,7168]{1,0:T(8,128)S(1)} collective-permute-done((f32[32,7168]{1,0:T(8,128)S(1)}, f32[32,7168]{1,0:T(8,128)S(1)}, u32[]{:S(2)}, u32[]{:S(2)}) %collective-permute-start.3) | collective-permute-done | bytes 917536 | tf_op jit(solution)/shard_map/ppermute | solution.py:30
  22.1 0.1 fold.2
  22.2 7.2 %gate_up.3 = (f32[32,7168]{1,0:T(8,128)S(1)}, f32[32,7168]{1,0:T(8,128)S(1)}) custom-call(bf16[16,2048]{1,0:T(8,128)(2,1)S(1)} %head.1.refs_0_, bf16[16,2048]{1,0:T(8,128)(2,1)S(1)} %collective-permute-done.refs_1_, bf16[16,2048]{1,0:T(8,128)(2,1)S(1)} %collective-permute-done.1.refs_2_, bf16[16,2048]{1,0:T(8,128)(2,1)S(1)} %collective-permute-done.2.refs_3_, ...), custom_call_target="tpu_custom_call" | custom-call | flops 1879048192 | bytes 29360128 | tf_op jit(solution)/shard_map/gate_up/pallas_call | solution.py:89
  29.4 0.2 collective-permute-start.8
  29.6 1.9 %collective-permute-start.4 = (bf16[16,7168]{1,0:T(8,128)(2,1)S(1)}, bf16[16,7168]{1,0:T(8,128)(2,1)S(1)}, u32[]{:S(2)}, u32[]{:S(2)}) collective-permute-start(bf16[16,7168]{1,0:T(8,128)(2,1)S(1)} %get-tuple-element.20.refs_4_), channel_id=1, source_target_pairs={{0,2},{1,3},{2,0},{3,1},{4,6},{5,7},{6,4},{7,5},{8,10},{9,11},{10,... | collective-permute-start | bytes 688136 | tf_op jit(solution)/shard_map/ppermute | solution.py:30
  31.5 0.5 collective-permute-done.8.got
  32.0 0.1 fold.3
  32.0 1.9 %collective-permute-start.9 = (bf16[16,7168]{1,0:T(8,128)(2,1)S(1)}, bf16[16,7168]{1,0:T(8,128)(2,1)S(1)}, u32[]{:S(2)}, u32[]{:S(2)}) collective-permute-start(bf16[16,7168]{1,0:T(8,128)(2,1)S(1)} %get-tuple-element.24), channel_id=1, source_target_pairs={{0,2},{1,3},{2,0},{3,1},{4,6},{5,7},{6,4},{7,5},{8,10},{9,11},{10,... | collective-permute-start | bytes 688136 | tf_op jit(solution)/shard_map/ppermute | solution.py:30
  34.0 4.1 %collective-permute-done.4.got = bf16[16,7168]{1,0:T(8,128)(2,1)S(1)} collective-permute-done((bf16[16,7168]{1,0:T(8,128)(2,1)S(1)}, bf16[16,7168]{1,0:T(8,128)(2,1)S(1)}, u32[]{:S(2)}, u32[]{:S(2)}) %collective-permute-start.4) | collective-permute-done | bytes 229408 | tf_op jit(solution)/shard_map/ppermute | solution.py:30
  38.0 0.1 activate.2.refs_0_
  38.1 1.9 %collective-permute-start.6 = (bf16[16,3584]{1,0:T(8,128)(2,1)S(1)}, bf16[16,3584]{1,0:T(8,128)(2,1)S(1)}, u32[]{:S(2)}, u32[]{:S(2)}) collective-permute-start(bf16[16,3584]{1,0:T(8,128)(2,1)S(1)} %activate.2.refs_0_), channel_id=1, source_target_pairs={{0,2},{1,3},{2,0},{3,1},{4,6},{5,7},{6,4},{7,5},{8,10},{9,11},{10,... | collective-permute-start | bytes 344072 | tf_op jit(solution)/shard_map/ppermute | solution.py:30
  40.1 2.9 %collective-permute-done.9.got = bf16[16,7168]{1,0:T(8,128)(2,1)S(1)} collective-permute-done((bf16[16,7168]{1,0:T(8,128)(2,1)S(1)}, bf16[16,7168]{1,0:T(8,128)(2,1)S(1)}, u32[]{:S(2)}, u32[]{:S(2)}) %collective-permute-start.9) | collective-permute-done | bytes 229408 | tf_op jit(solution)/shard_map/ppermute | solution.py:30
  43.0 0.1 activate.3.refs_4_
  43.0 1.9 %collective-permute-start.11 = (bf16[16,3584]{1,0:T(8,128)(2,1)S(1)}, bf16[16,3584]{1,0:T(8,128)(2,1)S(1)}, u32[]{:S(2)}, u32[]{:S(2)}) collective-permute-start(bf16[16,3584]{1,0:T(8,128)(2,1)S(1)} %activate.3.refs_4_), channel_id=1, source_target_pairs={{0,2},{1,3},{2,0},{3,1},{4,6},{5,7},{6,4},{7,5},{8,10},{9,11},{10,... | collective-permute-start | bytes 344072 | tf_op jit(solution)/shard_map/ppermute | solution.py:30
  45.0 0.0 collective-permute-done.6.refs_2_
  45.0 0.5 collective-permute-start.7
  45.5 2.4 %collective-permute-done.11.refs_6_ = bf16[16,3584]{1,0:T(8,128)(2,1)S(1)} collective-permute-done((bf16[16,3584]{1,0:T(8,128)(2,1)S(1)}, bf16[16,3584]{1,0:T(8,128)(2,1)S(1)}, u32[]{:S(2)}, u32[]{:S(2)}) %collective-permute-start.11) | collective-permute-done | bytes 114720 | tf_op jit(solution)/shard_map/ppermute | solution.py:30
  47.9 1.3 %collective-permute-done.12.refs_7_ = bf16[16,3584]{1,0:T(8,128)(2,1)S(1)} collective-permute-done((bf16[16,3584]{1,0:T(8,128)(2,1)S(1)}, bf16[16,3584]{1,0:T(8,128)(2,1)S(1)}, u32[]{:S(2)}, u32[]{:S(2)}) %collective-permute-start.12) | collective-permute-done | bytes 114720 | tf_op jit(solution)/shard_map/ppermute | solution.py:30
  49.3 5.3 %down.1 = (f32[16,2048]{1,0:T(8,128)S(1)}, bf16[16,2048]{1,0:T(8,128)(2,1)S(1)}, bf16[16,2048]{1,0:T(8,128)(2,1)S(1)}, bf16[16,2048]{1,0:T(8,128)(2,1)S(1)}) custom-call(bf16[16,3584]{1,0:T(8,128)(2,1)S(1)} %activate.2.refs_0_, bf16[16,3584]{1,0:T(8,128)(2,1)S(1)} %collective-permute-done.5.refs_1_, bf16[16,3584]{1,0:T(8,128)(2,1)S(1)} %collective-permute-done.6.refs_2_, ...), custom_call_target="tpu_custom_call" | custom-call | flops 1879048192 | bytes 29360128 | tf_op jit(solution)/shard_map/down/pallas_call | solution.py:157
  54.5 1.5 %collective-permute-start.13 = (bf16[16,2048]{1,0:T(8,128)(2,1)S(1)}, bf16[16,2048]{1,0:T(8,128)(2,1)S(1)}, u32[]{:S(2)}, u32[]{:S(2)}) collective-permute-start(bf16[16,2048]{1,0:T(8,128)(2,1)S(1)} %get-tuple-element.26), channel_id=1, source_target_pairs={{0,4},{4,0},{8,12},{12,8},{1,5},{5,1},{9,13},{13,9},{2,6},{6,2},{1... | collective-permute-start | bytes 196616 | tf_op jit(solution)/shard_map/ppermute | solution.py:30
  56.0 3.2 %collective-permute-start.14 = (bf16[16,2048]{1,0:T(8,128)(2,1)S(1)}, bf16[16,2048]{1,0:T(8,128)(2,1)S(1)}, u32[]{:S(2)}, u32[]{:S(2)}) collective-permute-start(bf16[16,2048]{1,0:T(8,128)(2,1)S(1)} %get-tuple-element.27), channel_id=1, source_target_pairs={{0,8},{4,12},{8,0},{12,4},{1,9},{5,13},{9,1},{13,5},{2,10},{6,14},... | collective-permute-start | bytes 196616 | tf_op jit(solution)/shard_map/ppermute | solution.py:30
  59.2 4.0 %collective-permute-done.14 = bf16[16,2048]{1,0:T(8,128)(2,1)S(1)} collective-permute-done((bf16[16,2048]{1,0:T(8,128)(2,1)S(1)}, bf16[16,2048]{1,0:T(8,128)(2,1)S(1)}, u32[]{:S(2)}, u32[]{:S(2)}) %collective-permute-start.14) | collective-permute-done | bytes 65568 | tf_op jit(solution)/shard_map/ppermute | solution.py:30
  63.2 2.1 %collective-permute-done.15 = bf16[16,2048]{1,0:T(8,128)(2,1)S(1)} collective-permute-done((bf16[16,2048]{1,0:T(8,128)(2,1)S(1)}, bf16[16,2048]{1,0:T(8,128)(2,1)S(1)}, u32[]{:S(2)}, u32[]{:S(2)}) %collective-permute-start.15) | collective-permute-done | bytes 65568 | tf_op jit(solution)/shard_map/ppermute | solution.py:30
  65.3 0.7 %add_convert_fusion = bf16[16,2048]{1,0:T(8,128)(2,1)} fusion(bf16[16,2048]{1,0:T(8,128)(2,1)S(1)} %collective-permute-done.15, bf16[16,2048]{1,0:T(8,128)(2,1)S(1)} %collective-permute-done.14, f32[16,2048]{1,0:T(8,128)S(1)} %get-tuple-element.25, bf16[16,2048]{1,0:T(8,128)(2,1)S(1)} %collective-permute-done.13), kind=kLoop, calls=%fused_computation | loop fusion | flops 229376 | bytes 393216 | tf_op jit(solution)/shard_map/convert_element_type | solution.py:207
  (28 shorter events, 0.1 us)
Async XLA Ops:
  0.0 12.4 %copy-start = (bf16[2048,7168]{1,0:T(8,128)(2,1)S(1)}, bf16[2048,7168]{1,0:T(8,128)(2,1)}, u32[]{:S(2)}) copy-start(bf16[2048,7168]{1,0:T(8,128)(2,1)} %refs_5_.3) | copy-start | bytes 88080384
  0.0 1.0 %copy-start.1 = (bf16[16,2048]{1,0:T(8,128)(2,1)S(1)}, bf16[16,2048]{1,0:T(8,128)(2,1)}, u32[]{:S(2)}) copy-start(bf16[16,2048]{1,0:T(8,128)(2,1)} %given.1) | copy-start | bytes 196612
  1.0 7.1 %collective-permute-start.1 = (bf16[16,2048]{1,0:T(8,128)(2,1)S(1)}, bf16[16,2048]{1,0:T(8,128)(2,1)S(1)}, u32[]{:S(2)}, u32[]{:S(2)}) collective-permute-start(bf16[16,2048]{1,0:T(8,128)(2,1)S(1)} %head.1.refs_0_), channel_id=1, source_target_pairs={{0,8},{4,12},{8,0},{12,4},{1,9},{5,13},{9,1},{13,5},{2,10},{6,14},... | collective-permute-start | bytes 196616 | tf_op jit(solution)/shard_map/ppermute | solution.py:30
  5.0 4.4 %collective-permute-start = (bf16[16,2048]{1,0:T(8,128)(2,1)S(1)}, bf16[16,2048]{1,0:T(8,128)(2,1)S(1)}, u32[]{:S(2)}, u32[]{:S(2)}) collective-permute-start(bf16[16,2048]{1,0:T(8,128)(2,1)S(1)} %head.1.refs_0_), channel_id=1, source_target_pairs={{0,4},{4,0},{8,12},{12,8},{1,5},{5,1},{9,13},{13,9},{2,6},{6,2},{1... | collective-permute-start | bytes 196616 | tf_op jit(solution)/shard_map/ppermute | solution.py:30
  8.1 4.3 %collective-permute-start.2 = (bf16[16,2048]{1,0:T(8,128)(2,1)S(1)}, bf16[16,2048]{1,0:T(8,128)(2,1)S(1)}, u32[]{:S(2)}, u32[]{:S(2)}) collective-permute-start(bf16[16,2048]{1,0:T(8,128)(2,1)S(1)} %collective-permute-done.1.refs_2_), channel_id=1, source_target_pairs={{0,4},{4,0},{8,12},{12,8},{1,5},{5,1},{9,13},{13,9},{2,6},{6,2},{1... | collective-permute-start | bytes 196616 | tf_op jit(solution)/shard_map/ppermute | solution.py:30
  19.6 2.5 %collective-permute-start.3 = (f32[32,7168]{1,0:T(8,128)S(1)}, f32[32,7168]{1,0:T(8,128)S(1)}, u32[]{:S(2)}, u32[]{:S(2)}) collective-permute-start(f32[32,7168]{1,0:T(8,128)S(1)} %get-tuple-element.18), channel_id=1, source_target_pairs={{0,1},{1,0},{2,3},{3,2},{4,5},{5,4},{6,7},{7,6},{8,9},{9,8},{10,11... | collective-permute-start | bytes 2752520 | tf_op jit(solution)/shard_map/ppermute | solution.py:30
  29.4 2.5 %collective-permute-start.8 = (f32[32,7168]{1,0:T(8,128)S(1)}, f32[32,7168]{1,0:T(8,128)S(1)}, u32[]{:S(2)}, u32[]{:S(2)}) collective-permute-start(f32[32,7168]{1,0:T(8,128)S(1)} %get-tuple-element.22), channel_id=1, source_target_pairs={{0,1},{1,0},{2,3},{3,2},{4,5},{5,4},{6,7},{7,6},{8,9},{9,8},{10,11... | collective-permute-start | bytes 2752520 | tf_op jit(solution)/shard_map/ppermute | solution.py:30
  29.6 8.4 %collective-permute-start.4 = (bf16[16,7168]{1,0:T(8,128)(2,1)S(1)}, bf16[16,7168]{1,0:T(8,128)(2,1)S(1)}, u32[]{:S(2)}, u32[]{:S(2)}) collective-permute-start(bf16[16,7168]{1,0:T(8,128)(2,1)S(1)} %get-tuple-element.20.refs_4_), channel_id=1, source_target_pairs={{0,2},{1,3},{2,0},{3,1},{4,6},{5,7},{6,4},{7,5},{8,10},{9,11},{10,... | collective-permute-start | bytes 688136 | tf_op jit(solution)/shard_map/ppermute | solution.py:30
  32.0 10.9 %collective-permute-start.9 = (bf16[16,7168]{1,0:T(8,128)(2,1)S(1)}, bf16[16,7168]{1,0:T(8,128)(2,1)S(1)}, u32[]{:S(2)}, u32[]{:S(2)}) collective-permute-start(bf16[16,7168]{1,0:T(8,128)(2,1)S(1)} %get-tuple-element.24), channel_id=1, source_target_pairs={{0,2},{1,3},{2,0},{3,1},{4,6},{5,7},{6,4},{7,5},{8,10},{9,11},{10,... | collective-permute-start | bytes 688136 | tf_op jit(solution)/shard_map/ppermute | solution.py:30
  38.0 11.2 %slice-start = ((s8[29360128]{0:T(1024)(128)(4,1)}), s8[4194304]{0:T(1024)(128)(4,1)S(1)}, s32[]{:S(2)}) async-start(s8[29360128]{0:T(1024)(128)(4,1)} %bitcast), calls=%async_computation | async-start | bytes 8388608
  38.0 11.2 %slice-start.1 = ((s8[29360128]{0:T(1024)(128)(4,1)}), s8[4194304]{0:T(1024)(128)(4,1)S(1)}, s32[]{:S(2)}) async-start(s8[29360128]{0:T(1024)(128)(4,1)} %bitcast), calls=%async_computation.1 | async-start | bytes 8388608
  38.0 11.2 %slice-start.2 = ((s8[29360128]{0:T(1024)(128)(4,1)}), s8[4194304]{0:T(1024)(128)(4,1)S(1)}, s32[]{:S(2)}) async-start(s8[29360128]{0:T(1024)(128)(4,1)} %bitcast), calls=%async_computation.2 | async-start | bytes 8388608
  38.0 11.2 %slice-start.3 = ((s8[29360128]{0:T(1024)(128)(4,1)}), s8[4194304]{0:T(1024)(128)(4,1)S(1)}, s32[]{:S(2)}) async-start(s8[29360128]{0:T(1024)(128)(4,1)} %bitcast), calls=%async_computation.3 | async-start | bytes 8388608
  38.1 6.9 %collective-permute-start.6 = (bf16[16,3584]{1,0:T(8,128)(2,1)S(1)}, bf16[16,3584]{1,0:T(8,128)(2,1)S(1)}, u32[]{:S(2)}, u32[]{:S(2)}) collective-permute-start(bf16[16,3584]{1,0:T(8,128)(2,1)S(1)} %activate.2.refs_0_), channel_id=1, source_target_pairs={{0,2},{1,3},{2,0},{3,1},{4,6},{5,7},{6,4},{7,5},{8,10},{9,11},{10,... | collective-permute-start | bytes 344072 | tf_op jit(solution)/shard_map/ppermute | solution.py:30
  42.9 6.3 %slice-start.4 = ((s8[29360128]{0:T(1024)(128)(4,1)}), s8[4194304]{0:T(1024)(128)(4,1)S(1)}, s32[]{:S(2)}) async-start(s8[29360128]{0:T(1024)(128)(4,1)} %bitcast), calls=%async_computation.4 | async-start | bytes 8388608
  42.9 6.3 %slice-start.5 = ((s8[29360128]{0:T(1024)(128)(4,1)}), s8[4194304]{0:T(1024)(128)(4,1)S(1)}, s32[]{:S(2)}) async-start(s8[29360128]{0:T(1024)(128)(4,1)} %bitcast), calls=%async_computation.5 | async-start | bytes 8388608
  43.0 6.3 %slice-start.6 = ((s8[29360128]{0:T(1024)(128)(4,1)}), s8[4194304]{0:T(1024)(128)(4,1)S(1)}, s32[]{:S(2)}) async-start(s8[29360128]{0:T(1024)(128)(4,1)} %bitcast), calls=%async_computation.6 | async-start | bytes 8388608
  43.0 4.9 %collective-permute-start.11 = (bf16[16,3584]{1,0:T(8,128)(2,1)S(1)}, bf16[16,3584]{1,0:T(8,128)(2,1)S(1)}, u32[]{:S(2)}, u32[]{:S(2)}) collective-permute-start(bf16[16,3584]{1,0:T(8,128)(2,1)S(1)} %activate.3.refs_4_), channel_id=1, source_target_pairs={{0,2},{1,3},{2,0},{3,1},{4,6},{5,7},{6,4},{7,5},{8,10},{9,11},{10,... | collective-permute-start | bytes 344072 | tf_op jit(solution)/shard_map/ppermute | solution.py:30
  45.0 2.9 %collective-permute-start.5 = (bf16[16,3584]{1,0:T(8,128)(2,1)S(1)}, bf16[16,3584]{1,0:T(8,128)(2,1)S(1)}, u32[]{:S(2)}, u32[]{:S(2)}) collective-permute-start(bf16[16,3584]{1,0:T(8,128)(2,1)S(1)} %activate.2.refs_0_), channel_id=1, source_target_pairs={{0,1},{1,0},{2,3},{3,2},{4,5},{5,4},{6,7},{7,6},{8,9},{9,8},{10,11... | collective-permute-start | bytes 344072 | tf_op jit(solution)/shard_map/ppermute | solution.py:30
  45.0 2.9 %collective-permute-start.7 = (bf16[16,3584]{1,0:T(8,128)(2,1)S(1)}, bf16[16,3584]{1,0:T(8,128)(2,1)S(1)}, u32[]{:S(2)}, u32[]{:S(2)}) collective-permute-start(bf16[16,3584]{1,0:T(8,128)(2,1)S(1)} %collective-permute-done.6.refs_2_), channel_id=1, source_target_pairs={{0,1},{1,0},{2,3},{3,2},{4,5},{5,4},{6,7},{7,6},{8,9},{9,8},{10,11... | collective-permute-start | bytes 344072 | tf_op jit(solution)/shard_map/ppermute | solution.py:30
  45.5 2.4 %collective-permute-start.10 = (bf16[16,3584]{1,0:T(8,128)(2,1)S(1)}, bf16[16,3584]{1,0:T(8,128)(2,1)S(1)}, u32[]{:S(2)}, u32[]{:S(2)}) collective-permute-start(bf16[16,3584]{1,0:T(8,128)(2,1)S(1)} %activate.3.refs_4_), channel_id=1, source_target_pairs={{0,1},{1,0},{2,3},{3,2},{4,5},{5,4},{6,7},{7,6},{8,9},{9,8},{10,11... | collective-permute-start | bytes 344072 | tf_op jit(solution)/shard_map/ppermute | solution.py:30
  47.9 1.3 %collective-permute-start.12 = (bf16[16,3584]{1,0:T(8,128)(2,1)S(1)}, bf16[16,3584]{1,0:T(8,128)(2,1)S(1)}, u32[]{:S(2)}, u32[]{:S(2)}) collective-permute-start(bf16[16,3584]{1,0:T(8,128)(2,1)S(1)} %collective-permute-done.11.refs_6_), channel_id=1, source_target_pairs={{0,1},{1,0},{2,3},{3,2},{4,5},{5,4},{6,7},{7,6},{8,9},{9,8},{10,11... | collective-permute-start | bytes 344072 | tf_op jit(solution)/shard_map/ppermute | solution.py:30
  54.5 4.6 %collective-permute-start.13 = (bf16[16,2048]{1,0:T(8,128)(2,1)S(1)}, bf16[16,2048]{1,0:T(8,128)(2,1)S(1)}, u32[]{:S(2)}, u32[]{:S(2)}) collective-permute-start(bf16[16,2048]{1,0:T(8,128)(2,1)S(1)} %get-tuple-element.26), channel_id=1, source_target_pairs={{0,4},{4,0},{8,12},{12,8},{1,5},{5,1},{9,13},{13,9},{2,6},{6,2},{1... | collective-permute-start | bytes 196616 | tf_op jit(solution)/shard_map/ppermute | solution.py:30
  56.0 7.2 %collective-permute-start.14 = (bf16[16,2048]{1,0:T(8,128)(2,1)S(1)}, bf16[16,2048]{1,0:T(8,128)(2,1)S(1)}, u32[]{:S(2)}, u32[]{:S(2)}) collective-permute-start(bf16[16,2048]{1,0:T(8,128)(2,1)S(1)} %get-tuple-element.27), channel_id=1, source_target_pairs={{0,8},{4,12},{8,0},{12,4},{1,9},{5,13},{9,1},{13,5},{2,10},{6,14},... | collective-permute-start | bytes 196616 | tf_op jit(solution)/shard_map/ppermute | solution.py:30
  59.2 6.2 %collective-permute-start.15 = (bf16[16,2048]{1,0:T(8,128)(2,1)S(1)}, bf16[16,2048]{1,0:T(8,128)(2,1)S(1)}, u32[]{:S(2)}, u32[]{:S(2)}) collective-permute-start(bf16[16,2048]{1,0:T(8,128)(2,1)S(1)} %get-tuple-element.28), channel_id=1, source_target_pairs={{0,12},{4,8},{8,4},{12,0},{1,13},{5,9},{9,5},{13,1},{2,14},{6,10},... | collective-permute-start | bytes 196616 | tf_op jit(solution)/shard_map/ppermute | solution.py:30

commit v3 on v2

--- a/solution.py
+++ b/solution.py
@@ -9,7 +9,7 @@
 
 BF16, F32 = jnp.bfloat16, jnp.float32
 MIB = 2**20
-SPLIT = (4, 4)
+SPLIT = (8, 6)
 VMEM, ANY = pl.BlockSpec(memory_space=pltpu.VMEM), pl.BlockSpec(memory_space=pl.ANY)
 LONG = pl.CostEstimate(flops=20_000_000_000, bytes_accessed=1000, transcendentals=0)
 
@@ -74,11 +74,16 @@
         keep[:, pl.ds(column, bn)] = part[:half]
         send[:, pl.ds(column, bn)] = part[half:]
 
-    for tile in range(tiles):
-        at = tile * bn
-        put(at, jnp.dot(x[...], gate[:, pl.ds(start + at, bn)], preferred_element_type=F32))
+    lead = min(2, tiles)
+    for step in range(tiles + lead):
+        if step < tiles:
+            weight = gate[:, pl.ds(start + step * bn, bn)]
+            put(step * bn, jnp.dot(x[...], weight, preferred_element_type=F32))
+        tile = step - lead
+        if tile < 0:
+            continue
         copy(tile).wait()
-        put(n + at, jnp.dot(x[...], buffers[tile % ring], preferred_element_type=F32))
+        put(n + tile * bn, jnp.dot(x[...], buffers[tile % ring], preferred_element_type=F32))
         if tile + ring < tiles:
             copy(tile + ring).start()
 
@@ -104,15 +109,16 @@
     )(*pieces, *waits, gate, up)
 
 
-def fold(keep, got, cost=None):
-    def kernel(keep, got, own, away):
+def fold(keep, got, waits, cost=None):
+    def kernel(keep, got, *refs):
+        own, away = refs[-2:]
         quarter = own.shape[0]
         own[...] = keep[:quarter] + got[:quarter]
         away[...] = (keep[quarter:] + got[quarter:]).astype(BF16)
 
     rows, width = keep.shape
     shape = (rows // 2, width)
-    return local(kernel, [(shape, F32), (shape, BF16)], keep, got, name="fold", cost=cost)
+    return local(kernel, [(shape, F32), (shape, BF16)], keep, got, *([w] for w in waits), name="fold", cost=cost)
 
 
 def activate(own, got):
@@ -126,11 +132,11 @@
     return local(kernel, [((rows, width // 2), BF16)], own, got, name="activate", cost=LONG)[0]
 
 
-def down_kernel(chunks, groups, start, bn, places, *refs):
+def down_kernel(chunks, groups, start, bn, places, summed, *refs):
     pieces, refs = refs[: chunks * groups], refs[chunks * groups :]
     down, refs = refs[0], refs[1:]
     total = None
-    if start:
+    if summed:
         total, refs = refs[0], refs[1:]
     outs, hidden = refs[:-1], refs[-1]
     me, column = lax.axis_index("contract"), 0
@@ -155,7 +161,7 @@
     rows, bn = groups * share, tile_of(width, 512)
     given = [] if total is None else [total]
     return pl.pallas_call(
-        functools.partial(down_kernel, len(pieces), groups, start, bn, [p[:2] for p in places]),
+        functools.partial(down_kernel, len(pieces), groups, start, bn, [p[:2] for p in places], bool(given)),
         out_shape=[jax.ShapeDtypeStruct((count, width), kind) for _, count, kind in places],
         in_specs=[VMEM] * (groups * len(pieces)) + [VMEM] + [VMEM] * len(given),
         out_specs=[VMEM] * len(places),
@@ -169,6 +175,8 @@
 
 
 def gather_tokens(tokens, count):
+    if count <= 4:
+        return [tokens] + [swap(tokens, "blk", count, s) for s in range(1, count)]
     pieces, bit = {0: tokens}, count // 2
     while bit:
         pieces.update({s | bit: swap(p, "blk", count, bit) for s, p in list(pieces.items())})
@@ -180,31 +188,32 @@
     rows, width = slots * tokens.shape[0], gate.shape[1]
     gate = pltpu.with_memory_space_constraint(gate, pltpu.VMEM)
     up = pltpu.with_memory_space_constraint(up, pltpu.HBM)
-    down = pltpu.with_memory_space_constraint(down, pltpu.VMEM)
     pieces = gather_tokens(head(tokens), slots)
     unit = sum(SPLIT) * 128
     sizes = [width // sum(SPLIT) * s for s in SPLIT] if width % unit == 0 else [width]
     starts = [sum(sizes[:k]) for k in range(len(sizes))]
-    waits, folded = [], []
+    waits, mines = [], []
     for k, (start, n) in enumerate(zip(starts, sizes)):
         keep, send = gate_up(pieces, waits, gate, up, groups, start, n)
         got = swap(send, "contract", groups, 1)
-        folded.append(fold(keep, got))
-        waits = [folded[-1][1]]
+        own, away = fold(keep, got, mines[-1:])
+        waits = [away]
+        mine = activate(own, swap(away, "contract", groups, 2))
+        mines.append(mine)
     if slots <= 4:
         block = tokens.shape[0]
         places = [(reverse(s, slots) * block, block, BF16 if s else F32) for s in range(slots)]
     else:
         places = [(0, rows // 2, F32), (rows // 2, rows // 2, F32)]
     hiddens = []
-    for k, (own, away) in enumerate(folded):
-        mine = activate(own, swap(away, "contract", groups, 2))
+    for mine in mines:
         across = swap(mine, "contract", groups, 2)
         hidden = [mine, swap(mine, "contract", groups, 1), across, swap(across, "contract", groups, 1)]
         hiddens.append(hidden)
-    out = down_part(hiddens, down, None, 0, places)
+    held = pltpu.with_memory_space_constraint(down, pltpu.VMEM)
+    out = down_part(hiddens, held, None, 0, places)
     if slots <= 4:
-        return sum((swap(out[s], "blk", slots, s).astype(F32) for s in range(1, slots)), out[0]).astype(BF16)
+        return sum((swap(out[s], "blk", slots, s).astype(F32) for s in reversed(range(1, slots))), out[0]).astype(BF16)
     keep, send = out
     bit = 1
     while True:

time: 66.1 us -> 60.5 us (0.915)
  starting transfers between devices: 20 us -> 15 us
  Pallas kernels: 20 us -> 18.5 us
  waiting for transfers between devices: 24.2 us -> 25 us
    ppermute x16, starting transfers between devices: 20 us -> 15 us  [swap(): return lax.ppermute(x, axis, [(i, i ^ bit) for i in range(count)])]
    pallas_call x2, Pallas kernels: 14.4 us -> 12.9 us  [gate_up(): pl.pallas_call(functools.partial(gate_up_kernel, slots, groups, len(waits...]
    ppermute x16, waiting for transfers between devices: 24.2 us -> 25 us  [swap(): return lax.ppermute(x, axis, [(i, i ^ bit) for i in range(count)])]
  transfers between devices with their start and end apart: 16 -> 16, of which waited for: 10 -> 11; matrix products, arithmetic and copies ran while one was open for 0% -> 0% of each run, Pallas kernels for 0% -> 10%
where the time goes in v3:
time: 60.5 us; the launch traced here: 60.4 us
  waiting for transfers between devices  25 us (41%)
  Pallas kernels  18.5 us (31%)
  starting transfers between devices  15 us (25%)
  local copies, waits for them, and re-layouts  1.02 us (2%)
  other arithmetic  0.67 us (1%)
    ppermute x16, waiting for transfers between devices, swap(): return lax.ppermute(x, axis, [(i, i ^ bit) for i in range(count)])  25 us
    ppermute x16, starting transfers between devices, swap(): return lax.ppermute(x, axis, [(i, i ^ bit) for i in range(count)])  15 us
    pallas_call x2, Pallas kernels, gate_up(): pl.pallas_call(functools.partial(gate_up_kernel, slots, groups, len(waits...  12.9 us
    pallas_call x1, Pallas kernels, down_part(): pl.pallas_call(functools.partial(down_kernel, len(pieces), groups, start,...  5.26 us
  transfers between devices with their start and end apart: 16, of which 11 were waited for; matrix products, arithmetic and copies ran while one was open for 0% of the time, Pallas kernels for 10%

profile of v3, /device:TPU:0, one launch (start us, length us, event | category | flops | bytes accessed | tf_op | source)
XLA Modules:
  0.0 60.4 jit_solution(12861454169513210972)
XLA Ops:
  0.0 1.0 %copy-done.1 = bf16[16,2048]{1,0:T(8,128)(2,1)S(1)} copy-done((bf16[16,2048]{1,0:T(8,128)(2,1)S(1)}, bf16[16,2048]{1,0:T(8,128)(2,1)}, u32[]{:S(2)}) %copy-start.1) | copy-done | bytes 65560
  1.0 5.0 %collective-permute-start.2 = (bf16[16,2048]{1,0:T(8,128)(2,1)S(1)}, bf16[16,2048]{1,0:T(8,128)(2,1)S(1)}, u32[]{:S(2)}, u32[]{:S(2)}) collective-permute-start(bf16[16,2048]{1,0:T(8,128)(2,1)S(1)} %head.1.refs_0_), channel_id=1, source_target_pairs={{0,12},{4,8},{8,4},{12,0},{1,13},{5,9},{9,5},{13,1},{2,14},{6,10},... | collective-permute-start | bytes 196616 | tf_op jit(solution)/shard_map/ppermute | solution.py:30
  6.0 0.0 collective-permute-start.1
  6.1 0.6 %collective-permute-start = (bf16[16,2048]{1,0:T(8,128)(2,1)S(1)}, bf16[16,2048]{1,0:T(8,128)(2,1)S(1)}, u32[]{:S(2)}, u32[]{:S(2)}) collective-permute-start(bf16[16,2048]{1,0:T(8,128)(2,1)S(1)} %head.1.refs_0_), channel_id=1, source_target_pairs={{0,4},{4,0},{8,12},{12,8},{1,5},{5,1},{9,13},{13,9},{2,6},{6,2},{1... | collective-permute-start | bytes 196616 | tf_op jit(solution)/shard_map/ppermute | solution.py:30
  6.7 1.9 %collective-permute-done.2.refs_3_ = bf16[16,2048]{1,0:T(8,128)(2,1)S(1)} collective-permute-done((bf16[16,2048]{1,0:T(8,128)(2,1)S(1)}, bf16[16,2048]{1,0:T(8,128)(2,1)S(1)}, u32[]{:S(2)}, u32[]{:S(2)}) %collective-permute-start.2) | collective-permute-done | bytes 65568 | tf_op jit(solution)/shard_map/ppermute | solution.py:30
  8.6 3.0 %collective-permute-done.1.refs_2_ = bf16[16,2048]{1,0:T(8,128)(2,1)S(1)} collective-permute-done((bf16[16,2048]{1,0:T(8,128)(2,1)S(1)}, bf16[16,2048]{1,0:T(8,128)(2,1)S(1)}, u32[]{:S(2)}, u32[]{:S(2)}) %collective-permute-start.1) | collective-permute-done | bytes 65568 | tf_op jit(solution)/shard_map/ppermute | solution.py:30
  11.7 7.3 %gate_up.2 = (f32[32,8192]{1,0:T(8,128)S(1)}, f32[32,8192]{1,0:T(8,128)S(1)}) custom-call(bf16[16,2048]{1,0:T(8,128)(2,1)S(1)} %head.1.refs_0_, bf16[16,2048]{1,0:T(8,128)(2,1)S(1)} %collective-permute-done.refs_1_, bf16[16,2048]{1,0:T(8,128)(2,1)S(1)} %collective-permute-done.1.refs_2_, bf16[16,2048]{1,0:T(8,128)(2,1)S(1)} %collective-permute-done.2.refs_3_, ...), custom_call_target="tpu_custom_call" | custom-call | flops 2147483648 | bytes 33554432 | tf_op jit(solution)/shard_map/gate_up/pallas_call | solution.py:94
  19.0 0.1 collective-permute-start.3
  19.1 2.6 %collective-permute-done.3.got = f32[32,8192]{1,0:T(8,128)S(1)} collective-permute-done((f32[32,8192]{1,0:T(8,128)S(1)}, f32[32,8192]{1,0:T(8,128)S(1)}, u32[]{:S(2)}, u32[]{:S(2)}) %collective-permute-start.3) | collective-permute-done | bytes 1048608 | tf_op jit(solution)/shard_map/ppermute | solution.py:30
  21.7 0.1 fold.2
  21.8 1.6 %collective-permute-start.4 = (bf16[16,8192]{1,0:T(8,128)(2,1)S(1)}, bf16[16,8192]{1,0:T(8,128)(2,1)S(1)}, u32[]{:S(2)}, u32[]{:S(2)}) collective-permute-start(bf16[16,8192]{1,0:T(8,128)(2,1)S(1)} %get-tuple-element.20.refs_4_), channel_id=1, source_target_pairs={{0,2},{1,3},{2,0},{3,1},{4,6},{5,7},{6,4},{7,5},{8,10},{9,11},{10,... | collective-permute-start | bytes 786440 | tf_op jit(solution)/shard_map/ppermute | solution.py:30
  23.4 5.6 %gate_up.3 = (f32[32,6144]{1,0:T(8,128)S(1)}, f32[32,6144]{1,0:T(8,128)S(1)}) custom-call(bf16[16,2048]{1,0:T(8,128)(2,1)S(1)} %head.1.refs_0_, bf16[16,2048]{1,0:T(8,128)(2,1)S(1)} %collective-permute-done.refs_1_, bf16[16,2048]{1,0:T(8,128)(2,1)S(1)} %collective-permute-done.1.refs_2_, bf16[16,2048]{1,0:T(8,128)(2,1)S(1)} %collective-permute-done.2.refs_3_, ...), custom_call_target="tpu_custom_call" | custom-call | flops 1610612736 | bytes 25165824 | tf_op jit(solution)/shard_map/gate_up/pallas_call | solution.py:94
  29.0 0.1 collective-permute-start.8
  29.1 1.1 %collective-permute-done.4.got = bf16[16,8192]{1,0:T(8,128)(2,1)S(1)} collective-permute-done((bf16[16,8192]{1,0:T(8,128)(2,1)S(1)}, bf16[16,8192]{1,0:T(8,128)(2,1)S(1)}, u32[]{:S(2)}, u32[]{:S(2)}) %collective-permute-start.4) | collective-permute-done | bytes 262176 | tf_op jit(solution)/shard_map/ppermute | solution.py:30
  30.2 0.1 activate.2.refs_0_
  30.3 1.0 %collective-permute-done.8.got = f32[32,6144]{1,0:T(8,128)S(1)} collective-permute-done((f32[32,6144]{1,0:T(8,128)S(1)}, f32[32,6144]{1,0:T(8,128)S(1)}, u32[]{:S(2)}, u32[]{:S(2)}) %collective-permute-start.8) | collective-permute-done | bytes 786464 | tf_op jit(solution)/shard_map/ppermute | solution.py:30
  31.3 0.1 fold.3
  31.4 0.6 collective-permute-start.9
  32.0 1.5 %collective-permute-start.6 = (bf16[16,4096]{1,0:T(8,128)(2,1)S(1)}, bf16[16,4096]{1,0:T(8,128)(2,1)S(1)}, u32[]{:S(2)}, u32[]{:S(2)}) collective-permute-start(bf16[16,4096]{1,0:T(8,128)(2,1)S(1)} %activate.2.refs_0_), channel_id=1, source_target_pairs={{0,2},{1,3},{2,0},{3,1},{4,6},{5,7},{6,4},{7,5},{8,10},{9,11},{10,... | collective-permute-start | bytes 393224 | tf_op jit(solution)/shard_map/ppermute | solution.py:30
  33.5 5.7 %collective-permute-done.9.got = bf16[16,6144]{1,0:T(8,128)(2,1)S(1)} collective-permute-done((bf16[16,6144]{1,0:T(8,128)(2,1)S(1)}, bf16[16,6144]{1,0:T(8,128)(2,1)S(1)}, u32[]{:S(2)}, u32[]{:S(2)}) %collective-permute-start.9) | collective-permute-done | bytes 196640 | tf_op jit(solution)/shard_map/ppermute | solution.py:30
  39.3 0.1 activate.3.refs_4_
  39.3 0.6 collective-permute-start.11
  39.9 2.1 %collective-permute-done.6.refs_2_ = bf16[16,4096]{1,0:T(8,128)(2,1)S(1)} collective-permute-done((bf16[16,4096]{1,0:T(8,128)(2,1)S(1)}, bf16[16,4096]{1,0:T(8,128)(2,1)S(1)}, u32[]{:S(2)}, u32[]{:S(2)}) %collective-permute-start.6) | collective-permute-done | bytes 131104 | tf_op jit(solution)/shard_map/ppermute | solution.py:30
  42.0 0.5 collective-permute-start.10
  42.5 1.5 %collective-permute-done.11.refs_6_ = bf16[16,3072]{1,0:T(8,128)(2,1)S(1)} collective-permute-done((bf16[16,3072]{1,0:T(8,128)(2,1)S(1)}, bf16[16,3072]{1,0:T(8,128)(2,1)S(1)}, u32[]{:S(2)}, u32[]{:S(2)}) %collective-permute-start.11) | collective-permute-done | bytes 98336 | tf_op jit(solution)/shard_map/ppermute | solution.py:30
  44.0 1.3 %collective-permute-done.12.refs_7_ = bf16[16,3072]{1,0:T(8,128)(2,1)S(1)} collective-permute-done((bf16[16,3072]{1,0:T(8,128)(2,1)S(1)}, bf16[16,3072]{1,0:T(8,128)(2,1)S(1)}, u32[]{:S(2)}, u32[]{:S(2)}) %collective-permute-start.12) | collective-permute-done | bytes 98336 | tf_op jit(solution)/shard_map/ppermute | solution.py:30
  45.4 5.3 %down.1 = (f32[16,2048]{1,0:T(8,128)S(1)}, bf16[16,2048]{1,0:T(8,128)(2,1)S(1)}, bf16[16,2048]{1,0:T(8,128)(2,1)S(1)}, bf16[16,2048]{1,0:T(8,128)(2,1)S(1)}) custom-call(bf16[16,4096]{1,0:T(8,128)(2,1)S(1)} %activate.2.refs_0_, bf16[16,4096]{1,0:T(8,128)(2,1)S(1)} %collective-permute-done.5.refs_1_, bf16[16,4096]{1,0:T(8,128)(2,1)S(1)} %collective-permute-done.6.refs_2_, ...), custom_call_target="tpu_custom_call" | custom-call | flops 1879048192 | bytes 29360128 | tf_op jit(solution)/shard_map/down/pallas_call | solution.py:163
  50.7 2.8 %collective-permute-start.13 = (bf16[16,2048]{1,0:T(8,128)(2,1)S(1)}, bf16[16,2048]{1,0:T(8,128)(2,1)S(1)}, u32[]{:S(2)}, u32[]{:S(2)}) collective-permute-start(bf16[16,2048]{1,0:T(8,128)(2,1)S(1)} %get-tuple-element.26), channel_id=1, source_target_pairs={{0,12},{4,8},{8,4},{12,0},{1,13},{5,9},{9,5},{13,1},{2,14},{6,10},... | collective-permute-start | bytes 196616 | tf_op jit(solution)/shard_map/ppermute | solution.py:30
  53.5 1.6 %collective-permute-start.15 = (bf16[16,2048]{1,0:T(8,128)(2,1)S(1)}, bf16[16,2048]{1,0:T(8,128)(2,1)S(1)}, u32[]{:S(2)}, u32[]{:S(2)}) collective-permute-start(bf16[16,2048]{1,0:T(8,128)(2,1)S(1)} %get-tuple-element.28), channel_id=1, source_target_pairs={{0,4},{4,0},{8,12},{12,8},{1,5},{5,1},{9,13},{13,9},{2,6},{6,2},{1... | collective-permute-start | bytes 196616 | tf_op jit(solution)/shard_map/ppermute | solution.py:30
  55.1 2.4 %collective-permute-done.13 = bf16[16,2048]{1,0:T(8,128)(2,1)S(1)} collective-permute-done((bf16[16,2048]{1,0:T(8,128)(2,1)S(1)}, bf16[16,2048]{1,0:T(8,128)(2,1)S(1)}, u32[]{:S(2)}, u32[]{:S(2)}) %collective-permute-start.13) | collective-permute-done | bytes 65568 | tf_op jit(solution)/shard_map/ppermute | solution.py:30
  57.5 2.2 %collective-permute-done.14 = bf16[16,2048]{1,0:T(8,128)(2,1)S(1)} collective-permute-done((bf16[16,2048]{1,0:T(8,128)(2,1)S(1)}, bf16[16,2048]{1,0:T(8,128)(2,1)S(1)}, u32[]{:S(2)}, u32[]{:S(2)}) %collective-permute-start.14) | collective-permute-done | bytes 65568 | tf_op jit(solution)/shard_map/ppermute | solution.py:30
  59.7 0.7 %add_convert_fusion = bf16[16,2048]{1,0:T(8,128)(2,1)} fusion(bf16[16,2048]{1,0:T(8,128)(2,1)S(1)} %collective-permute-done.15, bf16[16,2048]{1,0:T(8,128)(2,1)S(1)} %collective-permute-done.14, f32[16,2048]{1,0:T(8,128)S(1)} %get-tuple-element.25, bf16[16,2048]{1,0:T(8,128)(2,1)S(1)} %collective-permute-done.13), kind=kLoop, calls=%fused_computation | loop fusion | flops 229376 | bytes 393216 | tf_op jit(solution)/shard_map/convert_element_type | solution.py:216
  (28 shorter events, 0.1 us)
Async XLA Ops:
  0.0 11.7 %copy-start = (bf16[2048,7168]{1,0:T(8,128)(2,1)S(1)}, bf16[2048,7168]{1,0:T(8,128)(2,1)}, u32[]{:S(2)}) copy-start(bf16[2048,7168]{1,0:T(8,128)(2,1)} %refs_5_.3) | copy-start | bytes 88080384
  0.0 1.0 %copy-start.1 = (bf16[16,2048]{1,0:T(8,128)(2,1)S(1)}, bf16[16,2048]{1,0:T(8,128)(2,1)}, u32[]{:S(2)}) copy-start(bf16[16,2048]{1,0:T(8,128)(2,1)} %given.1) | copy-start | bytes 196612
  1.0 7.6 %collective-permute-start.2 = (bf16[16,2048]{1,0:T(8,128)(2,1)S(1)}, bf16[16,2048]{1,0:T(8,128)(2,1)S(1)}, u32[]{:S(2)}, u32[]{:S(2)}) collective-permute-start(bf16[16,2048]{1,0:T(8,128)(2,1)S(1)} %head.1.refs_0_), channel_id=1, source_target_pairs={{0,12},{4,8},{8,4},{12,0},{1,13},{5,9},{9,5},{13,1},{2,14},{6,10},... | collective-permute-start | bytes 196616 | tf_op jit(solution)/shard_map/ppermute | solution.py:30
  6.0 5.6 %collective-permute-start.1 = (bf16[16,2048]{1,0:T(8,128)(2,1)S(1)}, bf16[16,2048]{1,0:T(8,128)(2,1)S(1)}, u32[]{:S(2)}, u32[]{:S(2)}) collective-permute-start(bf16[16,2048]{1,0:T(8,128)(2,1)S(1)} %head.1.refs_0_), channel_id=1, source_target_pairs={{0,8},{4,12},{8,0},{12,4},{1,9},{5,13},{9,1},{13,5},{2,10},{6,14},... | collective-permute-start | bytes 196616 | tf_op jit(solution)/shard_map/ppermute | solution.py:30
  6.1 5.6 %collective-permute-start = (bf16[16,2048]{1,0:T(8,128)(2,1)S(1)}, bf16[16,2048]{1,0:T(8,128)(2,1)S(1)}, u32[]{:S(2)}, u32[]{:S(2)}) collective-permute-start(bf16[16,2048]{1,0:T(8,128)(2,1)S(1)} %head.1.refs_0_), channel_id=1, source_target_pairs={{0,4},{4,0},{8,12},{12,8},{1,5},{5,1},{9,13},{13,9},{2,6},{6,2},{1... | collective-permute-start | bytes 196616 | tf_op jit(solution)/shard_map/ppermute | solution.py:30
  19.0 2.7 %collective-permute-start.3 = (f32[32,8192]{1,0:T(8,128)S(1)}, f32[32,8192]{1,0:T(8,128)S(1)}, u32[]{:S(2)}, u32[]{:S(2)}) collective-permute-start(f32[32,8192]{1,0:T(8,128)S(1)} %get-tuple-element.18), channel_id=1, source_target_pairs={{0,1},{1,0},{2,3},{3,2},{4,5},{5,4},{6,7},{7,6},{8,9},{9,8},{10,11... | collective-permute-start | bytes 3145736 | tf_op jit(solution)/shard_map/ppermute | solution.py:30
  21.8 8.4 %collective-permute-start.4 = (bf16[16,8192]{1,0:T(8,128)(2,1)S(1)}, bf16[16,8192]{1,0:T(8,128)(2,1)S(1)}, u32[]{:S(2)}, u32[]{:S(2)}) collective-permute-start(bf16[16,8192]{1,0:T(8,128)(2,1)S(1)} %get-tuple-element.20.refs_4_), channel_id=1, source_target_pairs={{0,2},{1,3},{2,0},{3,1},{4,6},{5,7},{6,4},{7,5},{8,10},{9,11},{10,... | collective-permute-start | bytes 786440 | tf_op jit(solution)/shard_map/ppermute | solution.py:30
  29.0 2.4 %collective-permute-start.8 = (f32[32,6144]{1,0:T(8,128)S(1)}, f32[32,6144]{1,0:T(8,128)S(1)}, u32[]{:S(2)}, u32[]{:S(2)}) collective-permute-start(f32[32,6144]{1,0:T(8,128)S(1)} %get-tuple-element.22), channel_id=1, source_target_pairs={{0,1},{1,0},{2,3},{3,2},{4,5},{5,4},{6,7},{7,6},{8,9},{9,8},{10,11... | collective-permute-start | bytes 2359304 | tf_op jit(solution)/shard_map/ppermute | solution.py:30
  30.2 15.1 %slice-start = ((s8[29360128]{0:T(1024)(128)(4,1)}), s8[4194304]{0:T(1024)(128)(4,1)S(1)}, s32[]{:S(2)}) async-start(s8[29360128]{0:T(1024)(128)(4,1)} %bitcast), calls=%async_computation | async-start | bytes 8388608
  30.2 15.1 %slice-start.1 = ((s8[29360128]{0:T(1024)(128)(4,1)}), s8[4194304]{0:T(1024)(128)(4,1)S(1)}, s32[]{:S(2)}) async-start(s8[29360128]{0:T(1024)(128)(4,1)} %bitcast), calls=%async_computation.1 | async-start | bytes 8388608
  30.2 15.1 %slice-start.2 = ((s8[29360128]{0:T(1024)(128)(4,1)}), s8[4194304]{0:T(1024)(128)(4,1)S(1)}, s32[]{:S(2)}) async-start(s8[29360128]{0:T(1024)(128)(4,1)} %bitcast), calls=%async_computation.2 | async-start | bytes 8388608
  30.2 15.1 %slice-start.3 = ((s8[29360128]{0:T(1024)(128)(4,1)}), s8[4194304]{0:T(1024)(128)(4,1)S(1)}, s32[]{:S(2)}) async-start(s8[29360128]{0:T(1024)(128)(4,1)} %bitcast), calls=%async_computation.3 | async-start | bytes 8388608
  31.4 7.8 %collective-permute-start.9 = (bf16[16,6144]{1,0:T(8,128)(2,1)S(1)}, bf16[16,6144]{1,0:T(8,128)(2,1)S(1)}, u32[]{:S(2)}, u32[]{:S(2)}) collective-permute-start(bf16[16,6144]{1,0:T(8,128)(2,1)S(1)} %get-tuple-element.24), channel_id=1, source_target_pairs={{0,2},{1,3},{2,0},{3,1},{4,6},{5,7},{6,4},{7,5},{8,10},{9,11},{10,... | collective-permute-start | bytes 589832 | tf_op jit(solution)/shard_map/ppermute | solution.py:30
  32.0 10.0 %collective-permute-start.6 = (bf16[16,4096]{1,0:T(8,128)(2,1)S(1)}, bf16[16,4096]{1,0:T(8,128)(2,1)S(1)}, u32[]{:S(2)}, u32[]{:S(2)}) collective-permute-start(bf16[16,4096]{1,0:T(8,128)(2,1)S(1)} %activate.2.refs_0_), channel_id=1, source_target_pairs={{0,2},{1,3},{2,0},{3,1},{4,6},{5,7},{6,4},{7,5},{8,10},{9,11},{10,... | collective-permute-start | bytes 393224 | tf_op jit(solution)/shard_map/ppermute | solution.py:30
  39.3 6.1 %slice-start.4 = ((s8[29360128]{0:T(1024)(128)(4,1)}), s8[4194304]{0:T(1024)(128)(4,1)S(1)}, s32[]{:S(2)}) async-start(s8[29360128]{0:T(1024)(128)(4,1)} %bitcast), calls=%async_computation.4 | async-start | bytes 8388608
  39.3 6.1 %slice-start.5 = ((s8[29360128]{0:T(1024)(128)(4,1)}), s8[4194304]{0:T(1024)(128)(4,1)S(1)}, s32[]{:S(2)}) async-start(s8[29360128]{0:T(1024)(128)(4,1)} %bitcast), calls=%async_computation.5 | async-start | bytes 8388608
  39.3 6.1 %slice-start.6 = ((s8[29360128]{0:T(1024)(128)(4,1)}), s8[4194304]{0:T(1024)(128)(4,1)S(1)}, s32[]{:S(2)}) async-start(s8[29360128]{0:T(1024)(128)(4,1)} %bitcast), calls=%async_computation.6 | async-start | bytes 8388608
  39.3 4.7 %collective-permute-start.11 = (bf16[16,3072]{1,0:T(8,128)(2,1)S(1)}, bf16[16,3072]{1,0:T(8,128)(2,1)S(1)}, u32[]{:S(2)}, u32[]{:S(2)}) collective-permute-start(bf16[16,3072]{1,0:T(8,128)(2,1)S(1)} %activate.3.refs_4_), channel_id=1, source_target_pairs={{0,2},{1,3},{2,0},{3,1},{4,6},{5,7},{6,4},{7,5},{8,10},{9,11},{10,... | collective-permute-start | bytes 294920 | tf_op jit(solution)/shard_map/ppermute | solution.py:30
  39.9 4.1 %collective-permute-start.5 = (bf16[16,4096]{1,0:T(8,128)(2,1)S(1)}, bf16[16,4096]{1,0:T(8,128)(2,1)S(1)}, u32[]{:S(2)}, u32[]{:S(2)}) collective-permute-start(bf16[16,4096]{1,0:T(8,128)(2,1)S(1)} %activate.2.refs_0_), channel_id=1, source_target_pairs={{0,1},{1,0},{2,3},{3,2},{4,5},{5,4},{6,7},{7,6},{8,9},{9,8},{10,11... | collective-permute-start | bytes 393224 | tf_op jit(solution)/shard_map/ppermute | solution.py:30
  42.0 2.1 %collective-permute-start.7 = (bf16[16,4096]{1,0:T(8,128)(2,1)S(1)}, bf16[16,4096]{1,0:T(8,128)(2,1)S(1)}, u32[]{:S(2)}, u32[]{:S(2)}) collective-permute-start(bf16[16,4096]{1,0:T(8,128)(2,1)S(1)} %collective-permute-done.6.refs_2_), channel_id=1, source_target_pairs={{0,1},{1,0},{2,3},{3,2},{4,5},{5,4},{6,7},{7,6},{8,9},{9,8},{10,11... | collective-permute-start | bytes 393224 | tf_op jit(solution)/shard_map/ppermute | solution.py:30
  42.0 2.1 %collective-permute-start.10 = (bf16[16,3072]{1,0:T(8,128)(2,1)S(1)}, bf16[16,3072]{1,0:T(8,128)(2,1)S(1)}, u32[]{:S(2)}, u32[]{:S(2)}) collective-permute-start(bf16[16,3072]{1,0:T(8,128)(2,1)S(1)} %activate.3.refs_4_), channel_id=1, source_target_pairs={{0,1},{1,0},{2,3},{3,2},{4,5},{5,4},{6,7},{7,6},{8,9},{9,8},{10,11... | collective-permute-start | bytes 294920 | tf_op jit(solution)/shard_map/ppermute | solution.py:30
  44.0 1.3 %collective-permute-start.12 = (bf16[16,3072]{1,0:T(8,128)(2,1)S(1)}, bf16[16,3072]{1,0:T(8,128)(2,1)S(1)}, u32[]{:S(2)}, u32[]{:S(2)}) collective-permute-start(bf16[16,3072]{1,0:T(8,128)(2,1)S(1)} %collective-permute-done.11.refs_6_), channel_id=1, source_target_pairs={{0,1},{1,0},{2,3},{3,2},{4,5},{5,4},{6,7},{7,6},{8,9},{9,8},{10,11... | collective-permute-start | bytes 294920 | tf_op jit(solution)/shard_map/ppermute | solution.py:30
  50.7 6.8 %collective-permute-start.13 = (bf16[16,2048]{1,0:T(8,128)(2,1)S(1)}, bf16[16,2048]{1,0:T(8,128)(2,1)S(1)}, u32[]{:S(2)}, u32[]{:S(2)}) collective-permute-start(bf16[16,2048]{1,0:T(8,128)(2,1)S(1)} %get-tuple-element.26), channel_id=1, source_target_pairs={{0,12},{4,8},{8,4},{12,0},{1,13},{5,9},{9,5},{13,1},{2,14},{6,10},... | collective-permute-start | bytes 196616 | tf_op jit(solution)/shard_map/ppermute | solution.py:30
  53.5 6.2 %collective-permute-start.14 = (bf16[16,2048]{1,0:T(8,128)(2,1)S(1)}, bf16[16,2048]{1,0:T(8,128)(2,1)S(1)}, u32[]{:S(2)}, u32[]{:S(2)}) collective-permute-start(bf16[16,2048]{1,0:T(8,128)(2,1)S(1)} %get-tuple-element.27), channel_id=1, source_target_pairs={{0,8},{4,12},{8,0},{12,4},{1,9},{5,13},{9,1},{13,5},{2,10},{6,14},... | collective-permute-start | bytes 196616 | tf_op jit(solution)/shard_map/ppermute | solution.py:30
  53.5 6.2 %collective-permute-start.15 = (bf16[16,2048]{1,0:T(8,128)(2,1)S(1)}, bf16[16,2048]{1,0:T(8,128)(2,1)S(1)}, u32[]{:S(2)}, u32[]{:S(2)}) collective-permute-start(bf16[16,2048]{1,0:T(8,128)(2,1)S(1)} %get-tuple-element.28), channel_id=1, source_target_pairs={{0,4},{4,0},{8,12},{12,8},{1,5},{5,1},{9,13},{13,9},{2,6},{6,2},{1... | collective-permute-start | bytes 196616 | tf_op jit(solution)/shard_map/ppermute | solution.py:30

commit v4 on v3

--- a/solution.py
+++ b/solution.py
@@ -74,7 +74,7 @@
         keep[:, pl.ds(column, bn)] = part[:half]
         send[:, pl.ds(column, bn)] = part[half:]
 
-    lead = min(2, tiles)
+    lead = min(3, tiles)
     for step in range(tiles + lead):
         if step < tiles:
             weight = gate[:, pl.ds(start + step * bn, bn)]
@@ -90,7 +90,7 @@
 
 def gate_up(pieces, waits, gate, up, groups, start, n):
     slots, (block, depth) = len(pieces), pieces[0].shape
-    rows, bn, ring = slots * block, tile_of(n, 512), 4
+    rows, bn, ring = slots * block, tile_of(n, 512), 6
     return pl.pallas_call(
         functools.partial(gate_up_kernel, slots, groups, len(waits), start, n, bn),
         out_shape=[jax.ShapeDtypeStruct((rows // 2, 2 * n), F32)] * 2,
@@ -101,7 +101,7 @@
             pltpu.VMEM((ring, depth, bn), BF16),
             pltpu.SemaphoreType.DMA((ring,)),
         ],
-        compiler_params=pltpu.CompilerParams(vmem_limit_bytes=14 * MIB),
+        compiler_params=pltpu.CompilerParams(vmem_limit_bytes=18 * MIB),
         cost_estimate=pl.CostEstimate(
             flops=4 * rows * depth * n, bytes_accessed=4 * depth * n, transcendentals=0
         ),

time: 60.5 us -> 59.9 us (0.990)
    pallas_call x2, Pallas kernels: 12.9 us -> 12.3 us  [gate_up(): pl.pallas_call(functools.partial(gate_up_kernel, slots, groups, len(waits...]
  transfers between devices with their start and end apart: 16 -> 16, of which waited for: 11 -> 11; matrix products, arithmetic and copies ran while one was open for 0% -> 0% of each run, Pallas kernels for 10% -> 9%
where the time goes in v4:
time: 59.9 us; the launch traced here: 59.7 us
  waiting for transfers between devices  24.7 us (41%)
  Pallas kernels  17.9 us (30%)
  starting transfers between devices  15.3 us (26%)
  local copies, waits for them, and re-layouts  1.02 us (2%)
  other arithmetic  0.67 us (1%)
    ppermute x16, waiting for transfers between devices, swap(): return lax.ppermute(x, axis, [(i, i ^ bit) for i in range(count)])  24.7 us
    ppermute x16, starting transfers between devices, swap(): return lax.ppermute(x, axis, [(i, i ^ bit) for i in range(count)])  15.3 us
    pallas_call x2, Pallas kernels, gate_up(): pl.pallas_call(functools.partial(gate_up_kernel, slots, groups, len(waits...  12.3 us
    pallas_call x1, Pallas kernels, down_part(): pl.pallas_call(functools.partial(down_kernel, len(pieces), groups, start,...  5.26 us
  transfers between devices with their start and end apart: 16, of which 11 were waited for; matrix products, arithmetic and copies ran while one was open for 0% of the time, Pallas kernels for 9%

profile of v4, /device:TPU:0, one launch (start us, length us, event | category | flops | bytes accessed | tf_op | source)
XLA Modules:
  0.0 59.7 jit_solution(9594128184346967967)
XLA Ops:
  0.0 1.0 %copy-done.1 = bf16[16,2048]{1,0:T(8,128)(2,1)S(1)} copy-done((bf16[16,2048]{1,0:T(8,128)(2,1)S(1)}, bf16[16,2048]{1,0:T(8,128)(2,1)}, u32[]{:S(2)}) %copy-start.1) | copy-done | bytes 65560
  1.0 5.0 %collective-permute-start.2 = (bf16[16,2048]{1,0:T(8,128)(2,1)S(1)}, bf16[16,2048]{1,0:T(8,128)(2,1)S(1)}, u32[]{:S(2)}, u32[]{:S(2)}) collective-permute-start(bf16[16,2048]{1,0:T(8,128)(2,1)S(1)} %head.1.refs_0_), channel_id=1, source_target_pairs={{0,12},{4,8},{8,4},{12,0},{1,13},{5,9},{9,5},{13,1},{2,14},{6,10},... | collective-permute-start | bytes 196616 | tf_op jit(solution)/shard_map/ppermute | solution.py:30
  6.0 0.0 collective-permute-start.1
  6.1 0.6 %collective-permute-start = (bf16[16,2048]{1,0:T(8,128)(2,1)S(1)}, bf16[16,2048]{1,0:T(8,128)(2,1)S(1)}, u32[]{:S(2)}, u32[]{:S(2)}) collective-permute-start(bf16[16,2048]{1,0:T(8,128)(2,1)S(1)} %head.1.refs_0_), channel_id=1, source_target_pairs={{0,4},{4,0},{8,12},{12,8},{1,5},{5,1},{9,13},{13,9},{2,6},{6,2},{1... | collective-permute-start | bytes 196616 | tf_op jit(solution)/shard_map/ppermute | solution.py:30
  6.7 1.9 %collective-permute-done.2.refs_3_ = bf16[16,2048]{1,0:T(8,128)(2,1)S(1)} collective-permute-done((bf16[16,2048]{1,0:T(8,128)(2,1)S(1)}, bf16[16,2048]{1,0:T(8,128)(2,1)S(1)}, u32[]{:S(2)}, u32[]{:S(2)}) %collective-permute-start.2) | collective-permute-done | bytes 65568 | tf_op jit(solution)/shard_map/ppermute | solution.py:30
  8.6 3.0 %collective-permute-done.1.refs_2_ = bf16[16,2048]{1,0:T(8,128)(2,1)S(1)} collective-permute-done((bf16[16,2048]{1,0:T(8,128)(2,1)S(1)}, bf16[16,2048]{1,0:T(8,128)(2,1)S(1)}, u32[]{:S(2)}, u32[]{:S(2)}) %collective-permute-start.1) | collective-permute-done | bytes 65568 | tf_op jit(solution)/shard_map/ppermute | solution.py:30
  11.7 7.0 %gate_up.2 = (f32[32,8192]{1,0:T(8,128)S(1)}, f32[32,8192]{1,0:T(8,128)S(1)}) custom-call(bf16[16,2048]{1,0:T(8,128)(2,1)S(1)} %head.1.refs_0_, bf16[16,2048]{1,0:T(8,128)(2,1)S(1)} %collective-permute-done.refs_1_, bf16[16,2048]{1,0:T(8,128)(2,1)S(1)} %collective-permute-done.1.refs_2_, bf16[16,2048]{1,0:T(8,128)(2,1)S(1)} %collective-permute-done.2.refs_3_, ...), custom_call_target="tpu_custom_call" | custom-call | flops 2147483648 | bytes 33554432 | tf_op jit(solution)/shard_map/gate_up/pallas_call | solution.py:94
  18.6 0.1 collective-permute-start.3
  18.7 2.6 %collective-permute-done.3.got = f32[32,8192]{1,0:T(8,128)S(1)} collective-permute-done((f32[32,8192]{1,0:T(8,128)S(1)}, f32[32,8192]{1,0:T(8,128)S(1)}, u32[]{:S(2)}, u32[]{:S(2)}) %collective-permute-start.3) | collective-permute-done | bytes 1048608 | tf_op jit(solution)/shard_map/ppermute | solution.py:30
  21.4 0.1 fold.2
  21.5 1.6 %collective-permute-start.4 = (bf16[16,8192]{1,0:T(8,128)(2,1)S(1)}, bf16[16,8192]{1,0:T(8,128)(2,1)S(1)}, u32[]{:S(2)}, u32[]{:S(2)}) collective-permute-start(bf16[16,8192]{1,0:T(8,128)(2,1)S(1)} %get-tuple-element.20.refs_4_), channel_id=1, source_target_pairs={{0,2},{1,3},{2,0},{3,1},{4,6},{5,7},{6,4},{7,5},{8,10},{9,11},{10,... | collective-permute-start | bytes 786440 | tf_op jit(solution)/shard_map/ppermute | solution.py:30
  23.0 5.3 %gate_up.3 = (f32[32,6144]{1,0:T(8,128)S(1)}, f32[32,6144]{1,0:T(8,128)S(1)}) custom-call(bf16[16,2048]{1,0:T(8,128)(2,1)S(1)} %head.1.refs_0_, bf16[16,2048]{1,0:T(8,128)(2,1)S(1)} %collective-permute-done.refs_1_, bf16[16,2048]{1,0:T(8,128)(2,1)S(1)} %collective-permute-done.1.refs_2_, bf16[16,2048]{1,0:T(8,128)(2,1)S(1)} %collective-permute-done.2.refs_3_, ...), custom_call_target="tpu_custom_call" | custom-call | flops 1610612736 | bytes 25165824 | tf_op jit(solution)/shard_map/gate_up/pallas_call | solution.py:94
  28.3 0.1 collective-permute-start.8
  28.4 1.5 %collective-permute-done.4.got = bf16[16,8192]{1,0:T(8,128)(2,1)S(1)} collective-permute-done((bf16[16,8192]{1,0:T(8,128)(2,1)S(1)}, bf16[16,8192]{1,0:T(8,128)(2,1)S(1)}, u32[]{:S(2)}, u32[]{:S(2)}) %collective-permute-start.4) | collective-permute-done | bytes 262176 | tf_op jit(solution)/shard_map/ppermute | solution.py:30
  29.9 0.1 activate.2.refs_0_
  30.0 0.7 %collective-permute-done.8.got = f32[32,6144]{1,0:T(8,128)S(1)} collective-permute-done((f32[32,6144]{1,0:T(8,128)S(1)}, f32[32,6144]{1,0:T(8,128)S(1)}, u32[]{:S(2)}, u32[]{:S(2)}) %collective-permute-start.8) | collective-permute-done | bytes 786464 | tf_op jit(solution)/shard_map/ppermute | solution.py:30
  30.7 0.1 fold.3
  30.8 0.9 %collective-permute-start.9 = (bf16[16,6144]{1,0:T(8,128)(2,1)S(1)}, bf16[16,6144]{1,0:T(8,128)(2,1)S(1)}, u32[]{:S(2)}, u32[]{:S(2)}) collective-permute-start(bf16[16,6144]{1,0:T(8,128)(2,1)S(1)} %get-tuple-element.24), channel_id=1, source_target_pairs={{0,2},{1,3},{2,0},{3,1},{4,6},{5,7},{6,4},{7,5},{8,10},{9,11},{10,... | collective-permute-start | bytes 589832 | tf_op jit(solution)/shard_map/ppermute | solution.py:30
  31.6 1.3 %collective-permute-start.6 = (bf16[16,4096]{1,0:T(8,128)(2,1)S(1)}, bf16[16,4096]{1,0:T(8,128)(2,1)S(1)}, u32[]{:S(2)}, u32[]{:S(2)}) collective-permute-start(bf16[16,4096]{1,0:T(8,128)(2,1)S(1)} %activate.2.refs_0_), channel_id=1, source_target_pairs={{0,2},{1,3},{2,0},{3,1},{4,6},{5,7},{6,4},{7,5},{8,10},{9,11},{10,... | collective-permute-start | bytes 393224 | tf_op jit(solution)/shard_map/ppermute | solution.py:30
  32.9 5.7 %collective-permute-done.9.got = bf16[16,6144]{1,0:T(8,128)(2,1)S(1)} collective-permute-done((bf16[16,6144]{1,0:T(8,128)(2,1)S(1)}, bf16[16,6144]{1,0:T(8,128)(2,1)S(1)}, u32[]{:S(2)}, u32[]{:S(2)}) %collective-permute-start.9) | collective-permute-done | bytes 196640 | tf_op jit(solution)/shard_map/ppermute | solution.py:30
  38.6 0.1 activate.3.refs_4_
  38.7 0.9 %collective-permute-start.11 = (bf16[16,3072]{1,0:T(8,128)(2,1)S(1)}, bf16[16,3072]{1,0:T(8,128)(2,1)S(1)}, u32[]{:S(2)}, u32[]{:S(2)}) collective-permute-start(bf16[16,3072]{1,0:T(8,128)(2,1)S(1)} %activate.3.refs_4_), channel_id=1, source_target_pairs={{0,2},{1,3},{2,0},{3,1},{4,6},{5,7},{6,4},{7,5},{8,10},{9,11},{10,... | collective-permute-start | bytes 294920 | tf_op jit(solution)/shard_map/ppermute | solution.py:30
  39.6 1.8 %collective-permute-done.6.refs_2_ = bf16[16,4096]{1,0:T(8,128)(2,1)S(1)} collective-permute-done((bf16[16,4096]{1,0:T(8,128)(2,1)S(1)}, bf16[16,4096]{1,0:T(8,128)(2,1)S(1)}, u32[]{:S(2)}, u32[]{:S(2)}) %collective-permute-start.6) | collective-permute-done | bytes 131104 | tf_op jit(solution)/shard_map/ppermute | solution.py:30
  41.3 0.5 collective-permute-start.10
  41.8 1.5 %collective-permute-done.11.refs_6_ = bf16[16,3072]{1,0:T(8,128)(2,1)S(1)} collective-permute-done((bf16[16,3072]{1,0:T(8,128)(2,1)S(1)}, bf16[16,3072]{1,0:T(8,128)(2,1)S(1)}, u32[]{:S(2)}, u32[]{:S(2)}) %collective-permute-start.11) | collective-permute-done | bytes 98336 | tf_op jit(solution)/shard_map/ppermute | solution.py:30
  43.4 1.3 %collective-permute-done.12.refs_7_ = bf16[16,3072]{1,0:T(8,128)(2,1)S(1)} collective-permute-done((bf16[16,3072]{1,0:T(8,128)(2,1)S(1)}, bf16[16,3072]{1,0:T(8,128)(2,1)S(1)}, u32[]{:S(2)}, u32[]{:S(2)}) %collective-permute-start.12) | collective-permute-done | bytes 98336 | tf_op jit(solution)/shard_map/ppermute | solution.py:30
  44.7 5.3 %down.1 = (f32[16,2048]{1,0:T(8,128)S(1)}, bf16[16,2048]{1,0:T(8,128)(2,1)S(1)}, bf16[16,2048]{1,0:T(8,128)(2,1)S(1)}, bf16[16,2048]{1,0:T(8,128)(2,1)S(1)}) custom-call(bf16[16,4096]{1,0:T(8,128)(2,1)S(1)} %activate.2.refs_0_, bf16[16,4096]{1,0:T(8,128)(2,1)S(1)} %collective-permute-done.5.refs_1_, bf16[16,4096]{1,0:T(8,128)(2,1)S(1)} %collective-permute-done.6.refs_2_, ...), custom_call_target="tpu_custom_call" | custom-call | flops 1879048192 | bytes 29360128 | tf_op jit(solution)/shard_map/down/pallas_call | solution.py:163
  50.0 2.8 %collective-permute-start.13 = (bf16[16,2048]{1,0:T(8,128)(2,1)S(1)}, bf16[16,2048]{1,0:T(8,128)(2,1)S(1)}, u32[]{:S(2)}, u32[]{:S(2)}) collective-permute-start(bf16[16,2048]{1,0:T(8,128)(2,1)S(1)} %get-tuple-element.26), channel_id=1, source_target_pairs={{0,12},{4,8},{8,4},{12,0},{1,13},{5,9},{9,5},{13,1},{2,14},{6,10},... | collective-permute-start | bytes 196616 | tf_op jit(solution)/shard_map/ppermute | solution.py:30
  52.8 1.6 %collective-permute-start.15 = (bf16[16,2048]{1,0:T(8,128)(2,1)S(1)}, bf16[16,2048]{1,0:T(8,128)(2,1)S(1)}, u32[]{:S(2)}, u32[]{:S(2)}) collective-permute-start(bf16[16,2048]{1,0:T(8,128)(2,1)S(1)} %get-tuple-element.28), channel_id=1, source_target_pairs={{0,4},{4,0},{8,12},{12,8},{1,5},{5,1},{9,13},{13,9},{2,6},{6,2},{1... | collective-permute-start | bytes 196616 | tf_op jit(solution)/shard_map/ppermute | solution.py:30
  54.5 2.4 %collective-permute-done.13 = bf16[16,2048]{1,0:T(8,128)(2,1)S(1)} collective-permute-done((bf16[16,2048]{1,0:T(8,128)(2,1)S(1)}, bf16[16,2048]{1,0:T(8,128)(2,1)S(1)}, u32[]{:S(2)}, u32[]{:S(2)}) %collective-permute-start.13) | collective-permute-done | bytes 65568 | tf_op jit(solution)/shard_map/ppermute | solution.py:30
  56.8 2.2 %collective-permute-done.14 = bf16[16,2048]{1,0:T(8,128)(2,1)S(1)} collective-permute-done((bf16[16,2048]{1,0:T(8,128)(2,1)S(1)}, bf16[16,2048]{1,0:T(8,128)(2,1)S(1)}, u32[]{:S(2)}, u32[]{:S(2)}) %collective-permute-start.14) | collective-permute-done | bytes 65568 | tf_op jit(solution)/shard_map/ppermute | solution.py:30
  59.1 0.7 %add_convert_fusion = bf16[16,2048]{1,0:T(8,128)(2,1)} fusion(bf16[16,2048]{1,0:T(8,128)(2,1)S(1)} %collective-permute-done.15, bf16[16,2048]{1,0:T(8,128)(2,1)S(1)} %collective-permute-done.14, f32[16,2048]{1,0:T(8,128)S(1)} %get-tuple-element.25, bf16[16,2048]{1,0:T(8,128)(2,1)S(1)} %collective-permute-done.13), kind=kLoop, calls=%fused_computation | loop fusion | flops 229376 | bytes 393216 | tf_op jit(solution)/shard_map/convert_element_type | solution.py:216
  (28 shorter events, 0.1 us)
Async XLA Ops:
  0.0 11.7 %copy-start = (bf16[2048,7168]{1,0:T(8,128)(2,1)S(1)}, bf16[2048,7168]{1,0:T(8,128)(2,1)}, u32[]{:S(2)}) copy-start(bf16[2048,7168]{1,0:T(8,128)(2,1)} %refs_5_.3) | copy-start | bytes 88080384
  0.0 1.0 %copy-start.1 = (bf16[16,2048]{1,0:T(8,128)(2,1)S(1)}, bf16[16,2048]{1,0:T(8,128)(2,1)}, u32[]{:S(2)}) copy-start(bf16[16,2048]{1,0:T(8,128)(2,1)} %given.1) | copy-start | bytes 196612
  1.0 7.6 %collective-permute-start.2 = (bf16[16,2048]{1,0:T(8,128)(2,1)S(1)}, bf16[16,2048]{1,0:T(8,128)(2,1)S(1)}, u32[]{:S(2)}, u32[]{:S(2)}) collective-permute-start(bf16[16,2048]{1,0:T(8,128)(2,1)S(1)} %head.1.refs_0_), channel_id=1, source_target_pairs={{0,12},{4,8},{8,4},{12,0},{1,13},{5,9},{9,5},{13,1},{2,14},{6,10},... | collective-permute-start | bytes 196616 | tf_op jit(solution)/shard_map/ppermute | solution.py:30
  6.0 5.6 %collective-permute-start.1 = (bf16[16,2048]{1,0:T(8,128)(2,1)S(1)}, bf16[16,2048]{1,0:T(8,128)(2,1)S(1)}, u32[]{:S(2)}, u32[]{:S(2)}) collective-permute-start(bf16[16,2048]{1,0:T(8,128)(2,1)S(1)} %head.1.refs_0_), channel_id=1, source_target_pairs={{0,8},{4,12},{8,0},{12,4},{1,9},{5,13},{9,1},{13,5},{2,10},{6,14},... | collective-permute-start | bytes 196616 | tf_op jit(solution)/shard_map/ppermute | solution.py:30
  6.1 5.6 %collective-permute-start = (bf16[16,2048]{1,0:T(8,128)(2,1)S(1)}, bf16[16,2048]{1,0:T(8,128)(2,1)S(1)}, u32[]{:S(2)}, u32[]{:S(2)}) collective-permute-start(bf16[16,2048]{1,0:T(8,128)(2,1)S(1)} %head.1.refs_0_), channel_id=1, source_target_pairs={{0,4},{4,0},{8,12},{12,8},{1,5},{5,1},{9,13},{13,9},{2,6},{6,2},{1... | collective-permute-start | bytes 196616 | tf_op jit(solution)/shard_map/ppermute | solution.py:30
  18.6 2.7 %collective-permute-start.3 = (f32[32,8192]{1,0:T(8,128)S(1)}, f32[32,8192]{1,0:T(8,128)S(1)}, u32[]{:S(2)}, u32[]{:S(2)}) collective-permute-start(f32[32,8192]{1,0:T(8,128)S(1)} %get-tuple-element.18), channel_id=1, source_target_pairs={{0,1},{1,0},{2,3},{3,2},{4,5},{5,4},{6,7},{7,6},{8,9},{9,8},{10,11... | collective-permute-start | bytes 3145736 | tf_op jit(solution)/shard_map/ppermute | solution.py:30
  21.5 8.4 %collective-permute-start.4 = (bf16[16,8192]{1,0:T(8,128)(2,1)S(1)}, bf16[16,8192]{1,0:T(8,128)(2,1)S(1)}, u32[]{:S(2)}, u32[]{:S(2)}) collective-permute-start(bf16[16,8192]{1,0:T(8,128)(2,1)S(1)} %get-tuple-element.20.refs_4_), channel_id=1, source_target_pairs={{0,2},{1,3},{2,0},{3,1},{4,6},{5,7},{6,4},{7,5},{8,10},{9,11},{10,... | collective-permute-start | bytes 786440 | tf_op jit(solution)/shard_map/ppermute | solution.py:30
  28.3 2.4 %collective-permute-start.8 = (f32[32,6144]{1,0:T(8,128)S(1)}, f32[32,6144]{1,0:T(8,128)S(1)}, u32[]{:S(2)}, u32[]{:S(2)}) collective-permute-start(f32[32,6144]{1,0:T(8,128)S(1)} %get-tuple-element.22), channel_id=1, source_target_pairs={{0,1},{1,0},{2,3},{3,2},{4,5},{5,4},{6,7},{7,6},{8,9},{9,8},{10,11... | collective-permute-start | bytes 2359304 | tf_op jit(solution)/shard_map/ppermute | solution.py:30
  29.9 14.8 %slice-start = ((s8[29360128]{0:T(1024)(128)(4,1)}), s8[4194304]{0:T(1024)(128)(4,1)S(1)}, s32[]{:S(2)}) async-start(s8[29360128]{0:T(1024)(128)(4,1)} %bitcast), calls=%async_computation | async-start | bytes 8388608
  29.9 14.8 %slice-start.1 = ((s8[29360128]{0:T(1024)(128)(4,1)}), s8[4194304]{0:T(1024)(128)(4,1)S(1)}, s32[]{:S(2)}) async-start(s8[29360128]{0:T(1024)(128)(4,1)} %bitcast), calls=%async_computation.1 | async-start | bytes 8388608
  29.9 14.8 %slice-start.2 = ((s8[29360128]{0:T(1024)(128)(4,1)}), s8[4194304]{0:T(1024)(128)(4,1)S(1)}, s32[]{:S(2)}) async-start(s8[29360128]{0:T(1024)(128)(4,1)} %bitcast), calls=%async_computation.2 | async-start | bytes 8388608
  29.9 14.8 %slice-start.3 = ((s8[29360128]{0:T(1024)(128)(4,1)}), s8[4194304]{0:T(1024)(128)(4,1)S(1)}, s32[]{:S(2)}) async-start(s8[29360128]{0:T(1024)(128)(4,1)} %bitcast), calls=%async_computation.3 | async-start | bytes 8388608
  30.8 7.8 %collective-permute-start.9 = (bf16[16,6144]{1,0:T(8,128)(2,1)S(1)}, bf16[16,6144]{1,0:T(8,128)(2,1)S(1)}, u32[]{:S(2)}, u32[]{:S(2)}) collective-permute-start(bf16[16,6144]{1,0:T(8,128)(2,1)S(1)} %get-tuple-element.24), channel_id=1, source_target_pairs={{0,2},{1,3},{2,0},{3,1},{4,6},{5,7},{6,4},{7,5},{8,10},{9,11},{10,... | collective-permute-start | bytes 589832 | tf_op jit(solution)/shard_map/ppermute | solution.py:30
  31.6 9.7 %collective-permute-start.6 = (bf16[16,4096]{1,0:T(8,128)(2,1)S(1)}, bf16[16,4096]{1,0:T(8,128)(2,1)S(1)}, u32[]{:S(2)}, u32[]{:S(2)}) collective-permute-start(bf16[16,4096]{1,0:T(8,128)(2,1)S(1)} %activate.2.refs_0_), channel_id=1, source_target_pairs={{0,2},{1,3},{2,0},{3,1},{4,6},{5,7},{6,4},{7,5},{8,10},{9,11},{10,... | collective-permute-start | bytes 393224 | tf_op jit(solution)/shard_map/ppermute | solution.py:30
  38.6 6.1 %slice-start.4 = ((s8[29360128]{0:T(1024)(128)(4,1)}), s8[4194304]{0:T(1024)(128)(4,1)S(1)}, s32[]{:S(2)}) async-start(s8[29360128]{0:T(1024)(128)(4,1)} %bitcast), calls=%async_computation.4 | async-start | bytes 8388608
  38.6 6.1 %slice-start.5 = ((s8[29360128]{0:T(1024)(128)(4,1)}), s8[4194304]{0:T(1024)(128)(4,1)S(1)}, s32[]{:S(2)}) async-start(s8[29360128]{0:T(1024)(128)(4,1)} %bitcast), calls=%async_computation.5 | async-start | bytes 8388608
  38.6 6.1 %slice-start.6 = ((s8[29360128]{0:T(1024)(128)(4,1)}), s8[4194304]{0:T(1024)(128)(4,1)S(1)}, s32[]{:S(2)}) async-start(s8[29360128]{0:T(1024)(128)(4,1)} %bitcast), calls=%async_computation.6 | async-start | bytes 8388608
  38.7 4.7 %collective-permute-start.11 = (bf16[16,3072]{1,0:T(8,128)(2,1)S(1)}, bf16[16,3072]{1,0:T(8,128)(2,1)S(1)}, u32[]{:S(2)}, u32[]{:S(2)}) collective-permute-start(bf16[16,3072]{1,0:T(8,128)(2,1)S(1)} %activate.3.refs_4_), channel_id=1, source_target_pairs={{0,2},{1,3},{2,0},{3,1},{4,6},{5,7},{6,4},{7,5},{8,10},{9,11},{10,... | collective-permute-start | bytes 294920 | tf_op jit(solution)/shard_map/ppermute | solution.py:30
  39.5 3.8 %collective-permute-start.5 = (bf16[16,4096]{1,0:T(8,128)(2,1)S(1)}, bf16[16,4096]{1,0:T(8,128)(2,1)S(1)}, u32[]{:S(2)}, u32[]{:S(2)}) collective-permute-start(bf16[16,4096]{1,0:T(8,128)(2,1)S(1)} %activate.2.refs_0_), channel_id=1, source_target_pairs={{0,1},{1,0},{2,3},{3,2},{4,5},{5,4},{6,7},{7,6},{8,9},{9,8},{10,11... | collective-permute-start | bytes 393224 | tf_op jit(solution)/shard_map/ppermute | solution.py:30
  41.3 2.1 %collective-permute-start.7 = (bf16[16,4096]{1,0:T(8,128)(2,1)S(1)}, bf16[16,4096]{1,0:T(8,128)(2,1)S(1)}, u32[]{:S(2)}, u32[]{:S(2)}) collective-permute-start(bf16[16,4096]{1,0:T(8,128)(2,1)S(1)} %collective-permute-done.6.refs_2_), channel_id=1, source_target_pairs={{0,1},{1,0},{2,3},{3,2},{4,5},{5,4},{6,7},{7,6},{8,9},{9,8},{10,11... | collective-permute-start | bytes 393224 | tf_op jit(solution)/shard_map/ppermute | solution.py:30
  41.3 2.1 %collective-permute-start.10 = (bf16[16,3072]{1,0:T(8,128)(2,1)S(1)}, bf16[16,3072]{1,0:T(8,128)(2,1)S(1)}, u32[]{:S(2)}, u32[]{:S(2)}) collective-permute-start(bf16[16,3072]{1,0:T(8,128)(2,1)S(1)} %activate.3.refs_4_), channel_id=1, source_target_pairs={{0,1},{1,0},{2,3},{3,2},{4,5},{5,4},{6,7},{7,6},{8,9},{9,8},{10,11... | collective-permute-start | bytes 294920 | tf_op jit(solution)/shard_map/ppermute | solution.py:30
  43.4 1.3 %collective-permute-start.12 = (bf16[16,3072]{1,0:T(8,128)(2,1)S(1)}, bf16[16,3072]{1,0:T(8,128)(2,1)S(1)}, u32[]{:S(2)}, u32[]{:S(2)}) collective-permute-start(bf16[16,3072]{1,0:T(8,128)(2,1)S(1)} %collective-permute-done.11.refs_6_), channel_id=1, source_target_pairs={{0,1},{1,0},{2,3},{3,2},{4,5},{5,4},{6,7},{7,6},{8,9},{9,8},{10,11... | collective-permute-start | bytes 294920 | tf_op jit(solution)/shard_map/ppermute | solution.py:30
  50.0 6.8 %collective-permute-start.13 = (bf16[16,2048]{1,0:T(8,128)(2,1)S(1)}, bf16[16,2048]{1,0:T(8,128)(2,1)S(1)}, u32[]{:S(2)}, u32[]{:S(2)}) collective-permute-start(bf16[16,2048]{1,0:T(8,128)(2,1)S(1)} %get-tuple-element.26), channel_id=1, source_target_pairs={{0,12},{4,8},{8,4},{12,0},{1,13},{5,9},{9,5},{13,1},{2,14},{6,10},... | collective-permute-start | bytes 196616 | tf_op jit(solution)/shard_map/ppermute | solution.py:30
  52.8 6.2 %collective-permute-start.14 = (bf16[16,2048]{1,0:T(8,128)(2,1)S(1)}, bf16[16,2048]{1,0:T(8,128)(2,1)S(1)}, u32[]{:S(2)}, u32[]{:S(2)}) collective-permute-start(bf16[16,2048]{1,0:T(8,128)(2,1)S(1)} %get-tuple-element.27), channel_id=1, source_target_pairs={{0,8},{4,12},{8,0},{12,4},{1,9},{5,13},{9,1},{13,5},{2,10},{6,14},... | collective-permute-start | bytes 196616 | tf_op jit(solution)/shard_map/ppermute | solution.py:30
  52.8 6.2 %collective-permute-start.15 = (bf16[16,2048]{1,0:T(8,128)(2,1)S(1)}, bf16[16,2048]{1,0:T(8,128)(2,1)S(1)}, u32[]{:S(2)}, u32[]{:S(2)}) collective-permute-start(bf16[16,2048]{1,0:T(8,128)(2,1)S(1)} %get-tuple-element.28), channel_id=1, source_target_pairs={{0,4},{4,0},{8,12},{12,8},{1,5},{5,1},{9,13},{13,9},{2,6},{6,2},{1... | collective-permute-start | bytes 196616 | tf_op jit(solution)/shard_map/ppermute | solution.py:30

commit v5 on v4

--- a/solution.py
+++ b/solution.py
@@ -9,7 +9,7 @@
 
 BF16, F32 = jnp.bfloat16, jnp.float32
 MIB = 2**20
-SPLIT = (8, 6)
+SPLIT = (8, 1, 5)
 VMEM, ANY = pl.BlockSpec(memory_space=pltpu.VMEM), pl.BlockSpec(memory_space=pl.ANY)
 LONG = pl.CostEstimate(flops=20_000_000_000, bytes_accessed=1000, transcendentals=0)
 
@@ -109,16 +109,24 @@
     )(*pieces, *waits, gate, up)
 
 
-def fold(keep, got, waits, cost=None):
-    def kernel(keep, got, *refs):
+def fold(parts, waits):
+    rows, count = parts[0][0].shape[0], len(parts)
+    width = sum(keep.shape[1] for keep, _ in parts)
+
+    def kernel(*refs):
         own, away = refs[-2:]
-        quarter = own.shape[0]
-        own[...] = keep[:quarter] + got[:quarter]
-        away[...] = (keep[quarter:] + got[quarter:]).astype(BF16)
-
-    rows, width = keep.shape
+        quarter, at = own.shape[0], 0
+        for keep, got in zip(refs[:count], refs[count : 2 * count]):
+            n = keep.shape[1] // 2
+            for base, column in ((0, at), (n, width // 2 + at)):
+                here, there = pl.ds(base, n), pl.ds(column, n)
+                own[:, there] = keep[:quarter, here] + got[:quarter, here]
+                away[:, there] = (keep[quarter:, here] + got[quarter:, here]).astype(BF16)
+            at += n
+
     shape = (rows // 2, width)
-    return local(kernel, [(shape, F32), (shape, BF16)], keep, got, *([w] for w in waits), name="fold", cost=cost)
+    given = [keep for keep, _ in parts] + [got for _, got in parts]
+    return local(kernel, [(shape, F32), (shape, BF16)], *given, *([w] for w in waits), name="fold")
 
 
 def activate(own, got):
@@ -174,9 +182,24 @@
     )(*(q for p in pieces for q in p), down, *given)
 
 
+def take(x):
+    def kernel(given, out):
+        out[...] = given[...]
+
+    return local(kernel, [(x.shape, x.dtype)], x, name="take", limit=MIB)[0]
+
+
+def plus(total, got):
+    def kernel(total, got, out):
+        out[...] = total[...] + got[...].astype(F32)
+
+    return local(kernel, [(total.shape, F32)], total, got, name="plus", limit=2 * MIB)[0]
+
+
 def gather_tokens(tokens, count):
     if count <= 4:
-        return [tokens] + [swap(tokens, "blk", count, s) for s in range(1, count)]
+        pieces = [tokens] + [swap(tokens, "blk", count, s) for s in range(1, count)]
+        return pieces[:-1] + [take(pieces[-1])]
     pieces, bit = {0: tokens}, count // 2
     while bit:
         pieces.update({s | bit: swap(p, "blk", count, bit) for s, p in list(pieces.items())})
@@ -189,17 +212,25 @@
     gate = pltpu.with_memory_space_constraint(gate, pltpu.VMEM)
     up = pltpu.with_memory_space_constraint(up, pltpu.HBM)
     pieces = gather_tokens(head(tokens), slots)
-    unit = sum(SPLIT) * 128
-    sizes = [width // sum(SPLIT) * s for s in SPLIT] if width % unit == 0 else [width]
-    starts = [sum(sizes[:k]) for k in range(len(sizes))]
-    waits, mines = [], []
-    for k, (start, n) in enumerate(zip(starts, sizes)):
-        keep, send = gate_up(pieces, waits, gate, up, groups, start, n)
-        got = swap(send, "contract", groups, 1)
-        own, away = fold(keep, got, mines[-1:])
-        waits = [away]
-        mine = activate(own, swap(away, "contract", groups, 2))
-        mines.append(mine)
+    unit = width // sum(SPLIT) if width % (sum(SPLIT) * 128) == 0 else 0
+    sizes = [unit * n for n in SPLIT] if unit else [width]
+
+    def products(k, waits):
+        keep, send = gate_up(pieces, waits, gate, up, groups, sum(sizes[:k]), sizes[k])
+        return keep, swap(send, "contract", groups, 1)
+
+    def across_sum(own, away):
+        return activate(own, swap(away, "contract", groups, 2))
+
+    first = products(0, [])
+    if unit:
+        second = products(1, first[:1])
+        own, away = fold([first], second[:1])
+        mines = [across_sum(own, away)]
+        third = products(2, [away])
+        mines.append(across_sum(*fold([second, third], mines)))
+    else:
+        mines = [across_sum(*fold([first], []))]
     if slots <= 4:
         block = tokens.shape[0]
         places = [(reverse(s, slots) * block, block, BF16 if s else F32) for s in range(slots)]
@@ -213,7 +244,9 @@
     held = pltpu.with_memory_space_constraint(down, pltpu.VMEM)
     out = down_part(hiddens, held, None, 0, places)
     if slots <= 4:
-        return sum((swap(out[s], "blk", slots, s).astype(F32) for s in reversed(range(1, slots))), out[0]).astype(BF16)
+        got = [swap(out[s], "blk", slots, s) for s in range(1, slots)]
+        total = plus(out[0], got.pop())
+        return sum((g.astype(F32) for g in reversed(got)), total).astype(BF16)
     keep, send = out
     bit = 1
     while True:

time: 59.9 us -> 59.2 us (0.988)
  waiting for transfers between devices: 24.7 us -> 20.9 us
  Pallas kernels: 17.9 us -> 19.8 us
  starting transfers between devices: 15.3 us -> 16.5 us
    ppermute x16 -> x17, waiting for transfers between devices: 24.7 us -> 20.9 us  [swap(): return lax.ppermute(x, axis, [(i, i ^ bit) for i in range(count)])]
    pallas_call x2 -> x3, Pallas kernels: 12.3 us -> 14.1 us  [gate_up(): pl.pallas_call(functools.partial(gate_up_kernel, slots, groups, len(waits...]
    ppermute x16 -> x17, starting transfers between devices: 15.3 us -> 16.5 us  [swap(): return lax.ppermute(x, axis, [(i, i ^ bit) for i in range(count)])]
  transfers between devices with their start and end apart: 16 -> 17, of which waited for: 11 -> 12; matrix products, arithmetic and copies ran while one was open for 0% -> 0% of each run, Pallas kernels for 9% -> 12%
where the time goes in v5:
time: 59.2 us; the launch traced here: 59 us
  waiting for transfers between devices  20.9 us (35%)
  Pallas kernels  19.8 us (33%)
  starting transfers between devices  16.5 us (28%)
  local copies, waits for them, and re-layouts  1.02 us (2%)
  other arithmetic  0.65 us (1%)
    ppermute x17, waiting for transfers between devices, swap(): return lax.ppermute(x, axis, [(i, i ^ bit) for i in range(count)])  20.9 us
    ppermute x17, starting transfers between devices, swap(): return lax.ppermute(x, axis, [(i, i ^ bit) for i in range(count)])  16.5 us
    pallas_call x3, Pallas kernels, gate_up(): pl.pallas_call(functools.partial(gate_up_kernel, slots, groups, len(waits...  14.1 us
    pallas_call x1, Pallas kernels, down_part(): pl.pallas_call(functools.partial(down_kernel, len(pieces), groups, start,...  5.26 us
  transfers between devices with their start and end apart: 17, of which 12 were waited for; matrix products, arithmetic and copies ran while one was open for 0% of the time, Pallas kernels for 12%

profile of v5, /device:TPU:0, one launch (start us, length us, event | category | flops | bytes accessed | tf_op | source)
XLA Modules:
  0.0 59.0 jit_solution(7266213468270659367)
XLA Ops:
  0.0 1.0 %copy-done.1 = bf16[16,2048]{1,0:T(8,128)(2,1)S(1)} copy-done((bf16[16,2048]{1,0:T(8,128)(2,1)S(1)}, bf16[16,2048]{1,0:T(8,128)(2,1)}, u32[]{:S(2)}) %copy-start.1) | copy-done | bytes 65560
  1.0 5.0 %collective-permute-start.2 = (bf16[16,2048]{1,0:T(8,128)(2,1)S(1)}, bf16[16,2048]{1,0:T(8,128)(2,1)S(1)}, u32[]{:S(2)}, u32[]{:S(2)}) collective-permute-start(bf16[16,2048]{1,0:T(8,128)(2,1)S(1)} %head.1.refs_0_), channel_id=1, source_target_pairs={{0,12},{4,8},{8,4},{12,0},{1,13},{5,9},{9,5},{13,1},{2,14},{6,10},... | collective-permute-start | bytes 196616 | tf_op jit(solution)/shard_map/ppermute | solution.py:30
  6.1 0.6 %collective-permute-start.1 = (bf16[16,2048]{1,0:T(8,128)(2,1)S(1)}, bf16[16,2048]{1,0:T(8,128)(2,1)S(1)}, u32[]{:S(2)}, u32[]{:S(2)}) collective-permute-start(bf16[16,2048]{1,0:T(8,128)(2,1)S(1)} %head.1.refs_0_), channel_id=1, source_target_pairs={{0,8},{4,12},{8,0},{12,4},{1,9},{5,13},{9,1},{13,5},{2,10},{6,14},... | collective-permute-start | bytes 196616 | tf_op jit(solution)/shard_map/ppermute | solution.py:30
  6.7 2.3 %collective-permute-done.2.given = bf16[16,2048]{1,0:T(8,128)(2,1)S(1)} collective-permute-done((bf16[16,2048]{1,0:T(8,128)(2,1)S(1)}, bf16[16,2048]{1,0:T(8,128)(2,1)S(1)}, u32[]{:S(2)}, u32[]{:S(2)}) %collective-permute-start.2) | collective-permute-done | bytes 65568 | tf_op jit(solution)/shard_map/ppermute | solution.py:30
  8.9 1.8 %collective-permute-done.refs_1_ = bf16[16,2048]{1,0:T(8,128)(2,1)S(1)} collective-permute-done((bf16[16,2048]{1,0:T(8,128)(2,1)S(1)}, bf16[16,2048]{1,0:T(8,128)(2,1)S(1)}, u32[]{:S(2)}, u32[]{:S(2)}) %collective-permute-start) | collective-permute-done | bytes 65568 | tf_op jit(solution)/shard_map/ppermute | solution.py:30
  10.7 1.0 %collective-permute-done.1.refs_2_ = bf16[16,2048]{1,0:T(8,128)(2,1)S(1)} collective-permute-done((bf16[16,2048]{1,0:T(8,128)(2,1)S(1)}, bf16[16,2048]{1,0:T(8,128)(2,1)S(1)}, u32[]{:S(2)}, u32[]{:S(2)}) %collective-permute-start.1) | collective-permute-done | bytes 65568 | tf_op jit(solution)/shard_map/ppermute | solution.py:30
  11.7 7.0 %gate_up.3 = (f32[32,8192]{1,0:T(8,128)S(1)}, f32[32,8192]{1,0:T(8,128)S(1)}) custom-call(bf16[16,2048]{1,0:T(8,128)(2,1)S(1)} %head.1.refs_0_, bf16[16,2048]{1,0:T(8,128)(2,1)S(1)} %collective-permute-done.refs_1_, bf16[16,2048]{1,0:T(8,128)(2,1)S(1)} %collective-permute-done.1.refs_2_, bf16[16,2048]{1,0:T(8,128)(2,1)S(1)} %take.1.refs_3_, ...), custom_call_target="tpu_custom_call" | custom-call | flops 2147483648 | bytes 33554432 | tf_op jit(solution)/shard_map/gate_up/pallas_call | solution.py:94
  18.7 0.1 collective-permute-start.3
  18.7 2.5 %gate_up.4 = (f32[32,1024]{1,0:T(8,128)S(1)}, f32[32,1024]{1,0:T(8,128)S(1)}) custom-call(bf16[16,2048]{1,0:T(8,128)(2,1)S(1)} %head.1.refs_0_, bf16[16,2048]{1,0:T(8,128)(2,1)S(1)} %collective-permute-done.refs_1_, bf16[16,2048]{1,0:T(8,128)(2,1)S(1)} %collective-permute-done.1.refs_2_, bf16[16,2048]{1,0:T(8,128)(2,1)S(1)} %take.1.refs_3_, ...), custom_call_target="tpu_custom_call" | custom-call | flops 268435456 | bytes 4194304 | tf_op jit(solution)/shard_map/gate_up/pallas_call | solution.py:94
  21.2 0.2 collective-permute-done.3.refs_1_
  21.4 0.1 fold.2
  21.5 1.6 %collective-permute-start.4 = (bf16[16,8192]{1,0:T(8,128)(2,1)S(1)}, bf16[16,8192]{1,0:T(8,128)(2,1)S(1)}, u32[]{:S(2)}, u32[]{:S(2)}) collective-permute-start(bf16[16,8192]{1,0:T(8,128)(2,1)S(1)} %get-tuple-element.23.refs_4_), channel_id=1, source_target_pairs={{0,2},{1,3},{2,0},{3,1},{4,6},{5,7},{6,4},{7,5},{8,10},{9,11},{10,... | collective-permute-start | bytes 786440 | tf_op jit(solution)/shard_map/ppermute | solution.py:30
  23.1 4.7 %gate_up.5 = (f32[32,5120]{1,0:T(8,128)S(1)}, f32[32,5120]{1,0:T(8,128)S(1)}) custom-call(bf16[16,2048]{1,0:T(8,128)(2,1)S(1)} %head.1.refs_0_, bf16[16,2048]{1,0:T(8,128)(2,1)S(1)} %collective-permute-done.refs_1_, bf16[16,2048]{1,0:T(8,128)(2,1)S(1)} %collective-permute-done.1.refs_2_, bf16[16,2048]{1,0:T(8,128)(2,1)S(1)} %take.1.refs_3_, ...), custom_call_target="tpu_custom_call" | custom-call | flops 1342177280 | bytes 20971520 | tf_op jit(solution)/shard_map/gate_up/pallas_call | solution.py:94
  27.8 0.5 collective-permute-start.9
  28.3 1.8 %collective-permute-done.4.got = bf16[16,8192]{1,0:T(8,128)(2,1)S(1)} collective-permute-done((bf16[16,8192]{1,0:T(8,128)(2,1)S(1)}, bf16[16,8192]{1,0:T(8,128)(2,1)S(1)}, u32[]{:S(2)}, u32[]{:S(2)}) %collective-permute-start.4) | collective-permute-done | bytes 262176 | tf_op jit(solution)/shard_map/ppermute | solution.py:30
  30.1 0.1 activate.2.refs_4_.refs_0_
  30.2 0.1 fold.3
  30.3 1.6 %collective-permute-start.10 = (bf16[16,6144]{1,0:T(8,128)(2,1)S(1)}, bf16[16,6144]{1,0:T(8,128)(2,1)S(1)}, u32[]{:S(2)}, u32[]{:S(2)}) collective-permute-start(bf16[16,6144]{1,0:T(8,128)(2,1)S(1)} %get-tuple-element.28), channel_id=1, source_target_pairs={{0,2},{1,3},{2,0},{3,1},{4,6},{5,7},{6,4},{7,5},{8,10},{9,11},{10,... | collective-permute-start | bytes 589832 | tf_op jit(solution)/shard_map/ppermute | solution.py:30
  31.9 0.5 collective-permute-start.6
  32.4 5.7 %collective-permute-done.10.got = bf16[16,6144]{1,0:T(8,128)(2,1)S(1)} collective-permute-done((bf16[16,6144]{1,0:T(8,128)(2,1)S(1)}, bf16[16,6144]{1,0:T(8,128)(2,1)S(1)}, u32[]{:S(2)}, u32[]{:S(2)}) %collective-permute-start.10) | collective-permute-done | bytes 196640 | tf_op jit(solution)/shard_map/ppermute | solution.py:30
  38.2 1.6 %collective-permute-start.12 = (bf16[16,3072]{1,0:T(8,128)(2,1)S(1)}, bf16[16,3072]{1,0:T(8,128)(2,1)S(1)}, u32[]{:S(2)}, u32[]{:S(2)}) collective-permute-start(bf16[16,3072]{1,0:T(8,128)(2,1)S(1)} %activate.3.refs_4_), channel_id=1, source_target_pairs={{0,2},{1,3},{2,0},{3,1},{4,6},{5,7},{6,4},{7,5},{8,10},{9,11},{10,... | collective-permute-start | bytes 294920 | tf_op jit(solution)/shard_map/ppermute | solution.py:30
  39.8 1.1 %collective-permute-done.6.refs_2_ = bf16[16,4096]{1,0:T(8,128)(2,1)S(1)} collective-permute-done((bf16[16,4096]{1,0:T(8,128)(2,1)S(1)}, bf16[16,4096]{1,0:T(8,128)(2,1)S(1)}, u32[]{:S(2)}, u32[]{:S(2)}) %collective-permute-start.6) | collective-permute-done | bytes 131104 | tf_op jit(solution)/shard_map/ppermute | solution.py:30
  40.8 0.5 collective-permute-start.11
  41.3 1.5 %collective-permute-done.12.refs_6_ = bf16[16,3072]{1,0:T(8,128)(2,1)S(1)} collective-permute-done((bf16[16,3072]{1,0:T(8,128)(2,1)S(1)}, bf16[16,3072]{1,0:T(8,128)(2,1)S(1)}, u32[]{:S(2)}, u32[]{:S(2)}) %collective-permute-start.12) | collective-permute-done | bytes 98336 | tf_op jit(solution)/shard_map/ppermute | solution.py:30
  42.9 1.3 %collective-permute-done.13.refs_7_ = bf16[16,3072]{1,0:T(8,128)(2,1)S(1)} collective-permute-done((bf16[16,3072]{1,0:T(8,128)(2,1)S(1)}, bf16[16,3072]{1,0:T(8,128)(2,1)S(1)}, u32[]{:S(2)}, u32[]{:S(2)}) %collective-permute-start.13) | collective-permute-done | bytes 98336 | tf_op jit(solution)/shard_map/ppermute | solution.py:30
  44.2 5.3 %down.1 = (f32[16,2048]{1,0:T(8,128)S(1)}, bf16[16,2048]{1,0:T(8,128)(2,1)S(1)}, bf16[16,2048]{1,0:T(8,128)(2,1)S(1)}, bf16[16,2048]{1,0:T(8,128)(2,1)S(1)}) custom-call(bf16[16,4096]{1,0:T(8,128)(2,1)S(1)} %activate.2.refs_4_.refs_0_, bf16[16,4096]{1,0:T(8,128)(2,1)S(1)} %collective-permute-done.5.refs_1_, ...), custom_call_target="tpu_custom_call" | custom-call | flops 1879048192 | bytes 29360128 | tf_op jit(solution)/shard_map/down/pallas_call | solution.py:171
  49.5 2.8 %collective-permute-start.14 = (bf16[16,2048]{1,0:T(8,128)(2,1)S(1)}, bf16[16,2048]{1,0:T(8,128)(2,1)S(1)}, u32[]{:S(2)}, u32[]{:S(2)}) collective-permute-start(bf16[16,2048]{1,0:T(8,128)(2,1)S(1)} %get-tuple-element.30), channel_id=1, source_target_pairs={{0,12},{4,8},{8,4},{12,0},{1,13},{5,9},{9,5},{13,1},{2,14},{6,10},... | collective-permute-start | bytes 196616 | tf_op jit(solution)/shard_map/ppermute | solution.py:30
  52.3 1.6 %collective-permute-start.15 = (bf16[16,2048]{1,0:T(8,128)(2,1)S(1)}, bf16[16,2048]{1,0:T(8,128)(2,1)S(1)}, u32[]{:S(2)}, u32[]{:S(2)}) collective-permute-start(bf16[16,2048]{1,0:T(8,128)(2,1)S(1)} %get-tuple-element.31), channel_id=1, source_target_pairs={{0,8},{4,12},{8,0},{12,4},{1,9},{5,13},{9,1},{13,5},{2,10},{6,14},... | collective-permute-start | bytes 196616 | tf_op jit(solution)/shard_map/ppermute | solution.py:30
  54.0 2.3 %collective-permute-done.14.got = bf16[16,2048]{1,0:T(8,128)(2,1)S(1)} collective-permute-done((bf16[16,2048]{1,0:T(8,128)(2,1)S(1)}, bf16[16,2048]{1,0:T(8,128)(2,1)S(1)}, u32[]{:S(2)}, u32[]{:S(2)}) %collective-permute-start.14) | collective-permute-done | bytes 65568 | tf_op jit(solution)/shard_map/ppermute | solution.py:30
  56.2 1.6 %collective-permute-done.16 = bf16[16,2048]{1,0:T(8,128)(2,1)S(1)} collective-permute-done((bf16[16,2048]{1,0:T(8,128)(2,1)S(1)}, bf16[16,2048]{1,0:T(8,128)(2,1)S(1)}, u32[]{:S(2)}, u32[]{:S(2)}) %collective-permute-start.16) | collective-permute-done | bytes 65568 | tf_op jit(solution)/shard_map/ppermute | solution.py:30
  57.8 0.6 %collective-permute-done.15 = bf16[16,2048]{1,0:T(8,128)(2,1)S(1)} collective-permute-done((bf16[16,2048]{1,0:T(8,128)(2,1)S(1)}, bf16[16,2048]{1,0:T(8,128)(2,1)S(1)}, u32[]{:S(2)}, u32[]{:S(2)}) %collective-permute-start.15) | collective-permute-done | bytes 65568 | tf_op jit(solution)/shard_map/ppermute | solution.py:30
  58.4 0.7 %add_convert_fusion = bf16[16,2048]{1,0:T(8,128)(2,1)} fusion(bf16[16,2048]{1,0:T(8,128)(2,1)S(1)} %collective-permute-done.16, f32[16,2048]{1,0:T(8,128)S(1)} %plus.1, bf16[16,2048]{1,0:T(8,128)(2,1)S(1)} %collective-permute-done.15), kind=kLoop, calls=%fused_computation | loop fusion | flops 163840 | bytes 327680 | tf_op jit(solution)/shard_map/convert_element_type | solution.py:249
  (33 shorter events, 0.2 us)
Async XLA Ops:
  0.0 11.7 %copy-start = (bf16[2048,7168]{1,0:T(8,128)(2,1)S(1)}, bf16[2048,7168]{1,0:T(8,128)(2,1)}, u32[]{:S(2)}) copy-start(bf16[2048,7168]{1,0:T(8,128)(2,1)} %refs_5_.5) | copy-start | bytes 88080384
  0.0 1.0 %copy-start.1 = (bf16[16,2048]{1,0:T(8,128)(2,1)S(1)}, bf16[16,2048]{1,0:T(8,128)(2,1)}, u32[]{:S(2)}) copy-start(bf16[16,2048]{1,0:T(8,128)(2,1)} %given.1) | copy-start | bytes 196612
  1.0 7.9 %collective-permute-start.2 = (bf16[16,2048]{1,0:T(8,128)(2,1)S(1)}, bf16[16,2048]{1,0:T(8,128)(2,1)S(1)}, u32[]{:S(2)}, u32[]{:S(2)}) collective-permute-start(bf16[16,2048]{1,0:T(8,128)(2,1)S(1)} %head.1.refs_0_), channel_id=1, source_target_pairs={{0,12},{4,8},{8,4},{12,0},{1,13},{5,9},{9,5},{13,1},{2,14},{6,10},... | collective-permute-start | bytes 196616 | tf_op jit(solution)/shard_map/ppermute | solution.py:30
  6.0 4.7 %collective-permute-start = (bf16[16,2048]{1,0:T(8,128)(2,1)S(1)}, bf16[16,2048]{1,0:T(8,128)(2,1)S(1)}, u32[]{:S(2)}, u32[]{:S(2)}) collective-permute-start(bf16[16,2048]{1,0:T(8,128)(2,1)S(1)} %head.1.refs_0_), channel_id=1, source_target_pairs={{0,4},{4,0},{8,12},{12,8},{1,5},{5,1},{9,13},{13,9},{2,6},{6,2},{1... | collective-permute-start | bytes 196616 | tf_op jit(solution)/shard_map/ppermute | solution.py:30
  6.1 5.6 %collective-permute-start.1 = (bf16[16,2048]{1,0:T(8,128)(2,1)S(1)}, bf16[16,2048]{1,0:T(8,128)(2,1)S(1)}, u32[]{:S(2)}, u32[]{:S(2)}) collective-permute-start(bf16[16,2048]{1,0:T(8,128)(2,1)S(1)} %head.1.refs_0_), channel_id=1, source_target_pairs={{0,8},{4,12},{8,0},{12,4},{1,9},{5,13},{9,1},{13,5},{2,10},{6,14},... | collective-permute-start | bytes 196616 | tf_op jit(solution)/shard_map/ppermute | solution.py:30
  18.7 2.7 %collective-permute-start.3 = (f32[32,8192]{1,0:T(8,128)S(1)}, f32[32,8192]{1,0:T(8,128)S(1)}, u32[]{:S(2)}, u32[]{:S(2)}) collective-permute-start(f32[32,8192]{1,0:T(8,128)S(1)} %get-tuple-element.20), channel_id=1, source_target_pairs={{0,1},{1,0},{2,3},{3,2},{4,5},{5,4},{6,7},{7,6},{8,9},{9,8},{10,11... | collective-permute-start | bytes 3145736 | tf_op jit(solution)/shard_map/ppermute | solution.py:30
  21.5 8.6 %collective-permute-start.4 = (bf16[16,8192]{1,0:T(8,128)(2,1)S(1)}, bf16[16,8192]{1,0:T(8,128)(2,1)S(1)}, u32[]{:S(2)}, u32[]{:S(2)}) collective-permute-start(bf16[16,8192]{1,0:T(8,128)(2,1)S(1)} %get-tuple-element.23.refs_4_), channel_id=1, source_target_pairs={{0,2},{1,3},{2,0},{3,1},{4,6},{5,7},{6,4},{7,5},{8,10},{9,11},{10,... | collective-permute-start | bytes 786440 | tf_op jit(solution)/shard_map/ppermute | solution.py:30
  23.0 7.2 %collective-permute-start.8 = (f32[32,1024]{1,0:T(8,128)S(1)}, f32[32,1024]{1,0:T(8,128)S(1)}, u32[]{:S(2)}, u32[]{:S(2)}) collective-permute-start(f32[32,1024]{1,0:T(8,128)S(1)} %get-tuple-element.25), channel_id=1, source_target_pairs={{0,1},{1,0},{2,3},{3,2},{4,5},{5,4},{6,7},{7,6},{8,9},{9,8},{10,11... | collective-permute-start | bytes 393224 | tf_op jit(solution)/shard_map/ppermute | solution.py:30
  27.8 2.4 %collective-permute-start.9 = (f32[32,5120]{1,0:T(8,128)S(1)}, f32[32,5120]{1,0:T(8,128)S(1)}, u32[]{:S(2)}, u32[]{:S(2)}) collective-permute-start(f32[32,5120]{1,0:T(8,128)S(1)} %get-tuple-element.26), channel_id=1, source_target_pairs={{0,1},{1,0},{2,3},{3,2},{4,5},{5,4},{6,7},{7,6},{8,9},{9,8},{10,11... | collective-permute-start | bytes 1966088 | tf_op jit(solution)/shard_map/ppermute | solution.py:30
  30.1 14.1 %slice-start = ((s8[29360128]{0:T(1024)(128)(4,1)}), s8[4194304]{0:T(1024)(128)(4,1)S(1)}, s32[]{:S(2)}) async-start(s8[29360128]{0:T(1024)(128)(4,1)} %bitcast), calls=%async_computation | async-start | bytes 8388608
  30.1 14.1 %slice-start.1 = ((s8[29360128]{0:T(1024)(128)(4,1)}), s8[4194304]{0:T(1024)(128)(4,1)S(1)}, s32[]{:S(2)}) async-start(s8[29360128]{0:T(1024)(128)(4,1)} %bitcast), calls=%async_computation.1 | async-start | bytes 8388608
  30.1 14.1 %slice-start.2 = ((s8[29360128]{0:T(1024)(128)(4,1)}), s8[4194304]{0:T(1024)(128)(4,1)S(1)}, s32[]{:S(2)}) async-start(s8[29360128]{0:T(1024)(128)(4,1)} %bitcast), calls=%async_computation.2 | async-start | bytes 8388608
  30.1 14.1 %slice-start.3 = ((s8[29360128]{0:T(1024)(128)(4,1)}), s8[4194304]{0:T(1024)(128)(4,1)S(1)}, s32[]{:S(2)}) async-start(s8[29360128]{0:T(1024)(128)(4,1)} %bitcast), calls=%async_computation.3 | async-start | bytes 8388608
  30.3 7.8 %collective-permute-start.10 = (bf16[16,6144]{1,0:T(8,128)(2,1)S(1)}, bf16[16,6144]{1,0:T(8,128)(2,1)S(1)}, u32[]{:S(2)}, u32[]{:S(2)}) collective-permute-start(bf16[16,6144]{1,0:T(8,128)(2,1)S(1)} %get-tuple-element.28), channel_id=1, source_target_pairs={{0,2},{1,3},{2,0},{3,1},{4,6},{5,7},{6,4},{7,5},{8,10},{9,11},{10,... | collective-permute-start | bytes 589832 | tf_op jit(solution)/shard_map/ppermute | solution.py:30
  31.9 9.0 %collective-permute-start.6 = (bf16[16,4096]{1,0:T(8,128)(2,1)S(1)}, bf16[16,4096]{1,0:T(8,128)(2,1)S(1)}, u32[]{:S(2)}, u32[]{:S(2)}) collective-permute-start(bf16[16,4096]{1,0:T(8,128)(2,1)S(1)} %activate.2.refs_4_.refs_0_), channel_id=1, source_target_pairs={{0,2},{1,3},{2,0},{3,1},{4,6},{5,7},{6,4},{7,5},{8,10},{9,11},{10,... | collective-permute-start | bytes 393224 | tf_op jit(solution)/shard_map/ppermute | solution.py:30
  38.1 6.1 %slice-start.4 = ((s8[29360128]{0:T(1024)(128)(4,1)}), s8[4194304]{0:T(1024)(128)(4,1)S(1)}, s32[]{:S(2)}) async-start(s8[29360128]{0:T(1024)(128)(4,1)} %bitcast), calls=%async_computation.4 | async-start | bytes 8388608
  38.1 6.1 %slice-start.5 = ((s8[29360128]{0:T(1024)(128)(4,1)}), s8[4194304]{0:T(1024)(128)(4,1)S(1)}, s32[]{:S(2)}) async-start(s8[29360128]{0:T(1024)(128)(4,1)} %bitcast), calls=%async_computation.5 | async-start | bytes 8388608
  38.1 6.1 %slice-start.6 = ((s8[29360128]{0:T(1024)(128)(4,1)}), s8[4194304]{0:T(1024)(128)(4,1)S(1)}, s32[]{:S(2)}) async-start(s8[29360128]{0:T(1024)(128)(4,1)} %bitcast), calls=%async_computation.6 | async-start | bytes 8388608
  38.2 4.7 %collective-permute-start.12 = (bf16[16,3072]{1,0:T(8,128)(2,1)S(1)}, bf16[16,3072]{1,0:T(8,128)(2,1)S(1)}, u32[]{:S(2)}, u32[]{:S(2)}) collective-permute-start(bf16[16,3072]{1,0:T(8,128)(2,1)S(1)} %activate.3.refs_4_), channel_id=1, source_target_pairs={{0,2},{1,3},{2,0},{3,1},{4,6},{5,7},{6,4},{7,5},{8,10},{9,11},{10,... | collective-permute-start | bytes 294920 | tf_op jit(solution)/shard_map/ppermute | solution.py:30
  39.8 3.1 %collective-permute-start.5 = (bf16[16,4096]{1,0:T(8,128)(2,1)S(1)}, bf16[16,4096]{1,0:T(8,128)(2,1)S(1)}, u32[]{:S(2)}, u32[]{:S(2)}) collective-permute-start(bf16[16,4096]{1,0:T(8,128)(2,1)S(1)} %activate.2.refs_4_.refs_0_), channel_id=1, source_target_pairs={{0,1},{1,0},{2,3},{3,2},{4,5},{5,4},{6,7},{7,6},{8,9},{9,8},{10,11... | collective-permute-start | bytes 393224 | tf_op jit(solution)/shard_map/ppermute | solution.py:30
  40.8 2.1 %collective-permute-start.7 = (bf16[16,4096]{1,0:T(8,128)(2,1)S(1)}, bf16[16,4096]{1,0:T(8,128)(2,1)S(1)}, u32[]{:S(2)}, u32[]{:S(2)}) collective-permute-start(bf16[16,4096]{1,0:T(8,128)(2,1)S(1)} %collective-permute-done.6.refs_2_), channel_id=1, source_target_pairs={{0,1},{1,0},{2,3},{3,2},{4,5},{5,4},{6,7},{7,6},{8,9},{9,8},{10,11... | collective-permute-start | bytes 393224 | tf_op jit(solution)/shard_map/ppermute | solution.py:30
  40.8 2.1 %collective-permute-start.11 = (bf16[16,3072]{1,0:T(8,128)(2,1)S(1)}, bf16[16,3072]{1,0:T(8,128)(2,1)S(1)}, u32[]{:S(2)}, u32[]{:S(2)}) collective-permute-start(bf16[16,3072]{1,0:T(8,128)(2,1)S(1)} %activate.3.refs_4_), channel_id=1, source_target_pairs={{0,1},{1,0},{2,3},{3,2},{4,5},{5,4},{6,7},{7,6},{8,9},{9,8},{10,11... | collective-permute-start | bytes 294920 | tf_op jit(solution)/shard_map/ppermute | solution.py:30
  42.9 1.3 %collective-permute-start.13 = (bf16[16,3072]{1,0:T(8,128)(2,1)S(1)}, bf16[16,3072]{1,0:T(8,128)(2,1)S(1)}, u32[]{:S(2)}, u32[]{:S(2)}) collective-permute-start(bf16[16,3072]{1,0:T(8,128)(2,1)S(1)} %collective-permute-done.12.refs_6_), channel_id=1, source_target_pairs={{0,1},{1,0},{2,3},{3,2},{4,5},{5,4},{6,7},{7,6},{8,9},{9,8},{10,11... | collective-permute-start | bytes 294920 | tf_op jit(solution)/shard_map/ppermute | solution.py:30
  49.5 6.7 %collective-permute-start.14 = (bf16[16,2048]{1,0:T(8,128)(2,1)S(1)}, bf16[16,2048]{1,0:T(8,128)(2,1)S(1)}, u32[]{:S(2)}, u32[]{:S(2)}) collective-permute-start(bf16[16,2048]{1,0:T(8,128)(2,1)S(1)} %get-tuple-element.30), channel_id=1, source_target_pairs={{0,12},{4,8},{8,4},{12,0},{1,13},{5,9},{9,5},{13,1},{2,14},{6,10},... | collective-permute-start | bytes 196616 | tf_op jit(solution)/shard_map/ppermute | solution.py:30
  52.3 5.5 %collective-permute-start.16 = (bf16[16,2048]{1,0:T(8,128)(2,1)S(1)}, bf16[16,2048]{1,0:T(8,128)(2,1)S(1)}, u32[]{:S(2)}, u32[]{:S(2)}) collective-permute-start(bf16[16,2048]{1,0:T(8,128)(2,1)S(1)} %get-tuple-element.32), channel_id=1, source_target_pairs={{0,4},{4,0},{8,12},{12,8},{1,5},{5,1},{9,13},{13,9},{2,6},{6,2},{1... | collective-permute-start | bytes 196616 | tf_op jit(solution)/shard_map/ppermute | solution.py:30
  52.3 6.1 %collective-permute-start.15 = (bf16[16,2048]{1,0:T(8,128)(2,1)S(1)}, bf16[16,2048]{1,0:T(8,128)(2,1)S(1)}, u32[]{:S(2)}, u32[]{:S(2)}) collective-permute-start(bf16[16,2048]{1,0:T(8,128)(2,1)S(1)} %get-tuple-element.31), channel_id=1, source_target_pairs={{0,8},{4,12},{8,0},{12,4},{1,9},{5,13},{9,1},{13,5},{2,10},{6,14},... | collective-permute-start | bytes 196616 | tf_op jit(solution)/shard_map/ppermute | solution.py:30

commit v6 on v5

--- a/solution.py
+++ b/solution.py
@@ -74,7 +74,7 @@
         keep[:, pl.ds(column, bn)] = part[:half]
         send[:, pl.ds(column, bn)] = part[half:]
 
-    lead = min(3, tiles)
+    lead = min(4, tiles)
     for step in range(tiles + lead):
         if step < tiles:
             weight = gate[:, pl.ds(start + step * bn, bn)]
@@ -90,7 +90,7 @@
 
 def gate_up(pieces, waits, gate, up, groups, start, n):
     slots, (block, depth) = len(pieces), pieces[0].shape
-    rows, bn, ring = slots * block, tile_of(n, 512), 6
+    rows, bn, ring = slots * block, tile_of(n, 512), 8
     return pl.pallas_call(
         functools.partial(gate_up_kernel, slots, groups, len(waits), start, n, bn),
         out_shape=[jax.ShapeDtypeStruct((rows // 2, 2 * n), F32)] * 2,
@@ -101,7 +101,7 @@
             pltpu.VMEM((ring, depth, bn), BF16),
             pltpu.SemaphoreType.DMA((ring,)),
         ],
-        compiler_params=pltpu.CompilerParams(vmem_limit_bytes=18 * MIB),
+        compiler_params=pltpu.CompilerParams(vmem_limit_bytes=22 * MIB),
         cost_estimate=pl.CostEstimate(
             flops=4 * rows * depth * n, bytes_accessed=4 * depth * n, transcendentals=0
         ),
@@ -166,7 +166,7 @@
 
 def down_part(pieces, down, total, start, places):
     groups, share, n, width = len(pieces[0]), pieces[0][0].shape[0], sum(p[0].shape[1] for p in pieces), down.shape[1]
-    rows, bn = groups * share, tile_of(width, 512)
+    rows, bn = groups * share, tile_of(width, 1024)
     given = [] if total is None else [total]
     return pl.pallas_call(
         functools.partial(down_kernel, len(pieces), groups, start, bn, [p[:2] for p in places], bool(given)),

time: 59.2 us -> 59.2 us (level)
  no operation moved by 1% of the time
where the time goes in v6:
time: 59.2 us; the launch traced here: 59 us
  waiting for transfers between devices  20.9 us (35%)
  Pallas kernels  19.7 us (33%)
  starting transfers between devices  16.5 us (28%)
  local copies, waits for them, and re-layouts  1.02 us (2%)
  other arithmetic  0.65 us (1%)
    ppermute x17, waiting for transfers between devices, swap(): return lax.ppermute(x, axis, [(i, i ^ bit) for i in range(count)])  20.9 us
    ppermute x17, starting transfers between devices, swap(): return lax.ppermute(x, axis, [(i, i ^ bit) for i in range(count)])  16.5 us
    pallas_call x3, Pallas kernels, gate_up(): pl.pallas_call(functools.partial(gate_up_kernel, slots, groups, len(waits...  14.1 us
    pallas_call x1, Pallas kernels, down_part(): pl.pallas_call(functools.partial(down_kernel, len(pieces), groups, start,...  5.25 us
  transfers between devices with their start and end apart: 17, of which 12 were waited for; matrix products, arithmetic and copies ran while one was open for 0% of the time, Pallas kernels for 12%

profile of v6, /device:TPU:0, one launch (start us, length us, event | category | flops | bytes accessed | tf_op | source)
XLA Modules:
  0.0 59.0 jit_solution(9813589507939327302)
XLA Ops:
  0.0 1.0 %copy-done.1 = bf16[16,2048]{1,0:T(8,128)(2,1)S(1)} copy-done((bf16[16,2048]{1,0:T(8,128)(2,1)S(1)}, bf16[16,2048]{1,0:T(8,128)(2,1)}, u32[]{:S(2)}) %copy-start.1) | copy-done | bytes 65560
  1.0 5.0 %collective-permute-start.2 = (bf16[16,2048]{1,0:T(8,128)(2,1)S(1)}, bf16[16,2048]{1,0:T(8,128)(2,1)S(1)}, u32[]{:S(2)}, u32[]{:S(2)}) collective-permute-start(bf16[16,2048]{1,0:T(8,128)(2,1)S(1)} %head.1.refs_0_), channel_id=1, source_target_pairs={{0,12},{4,8},{8,4},{12,0},{1,13},{5,9},{9,5},{13,1},{2,14},{6,10},... | collective-permute-start | bytes 196616 | tf_op jit(solution)/shard_map/ppermute | solution.py:30
  6.1 0.6 %collective-permute-start.1 = (bf16[16,2048]{1,0:T(8,128)(2,1)S(1)}, bf16[16,2048]{1,0:T(8,128)(2,1)S(1)}, u32[]{:S(2)}, u32[]{:S(2)}) collective-permute-start(bf16[16,2048]{1,0:T(8,128)(2,1)S(1)} %head.1.refs_0_), channel_id=1, source_target_pairs={{0,8},{4,12},{8,0},{12,4},{1,9},{5,13},{9,1},{13,5},{2,10},{6,14},... | collective-permute-start | bytes 196616 | tf_op jit(solution)/shard_map/ppermute | solution.py:30
  6.7 2.3 %collective-permute-done.2.given = bf16[16,2048]{1,0:T(8,128)(2,1)S(1)} collective-permute-done((bf16[16,2048]{1,0:T(8,128)(2,1)S(1)}, bf16[16,2048]{1,0:T(8,128)(2,1)S(1)}, u32[]{:S(2)}, u32[]{:S(2)}) %collective-permute-start.2) | collective-permute-done | bytes 65568 | tf_op jit(solution)/shard_map/ppermute | solution.py:30
  8.9 1.8 %collective-permute-done.refs_1_ = bf16[16,2048]{1,0:T(8,128)(2,1)S(1)} collective-permute-done((bf16[16,2048]{1,0:T(8,128)(2,1)S(1)}, bf16[16,2048]{1,0:T(8,128)(2,1)S(1)}, u32[]{:S(2)}, u32[]{:S(2)}) %collective-permute-start) | collective-permute-done | bytes 65568 | tf_op jit(solution)/shard_map/ppermute | solution.py:30
  10.7 1.0 %collective-permute-done.1.refs_2_ = bf16[16,2048]{1,0:T(8,128)(2,1)S(1)} collective-permute-done((bf16[16,2048]{1,0:T(8,128)(2,1)S(1)}, bf16[16,2048]{1,0:T(8,128)(2,1)S(1)}, u32[]{:S(2)}, u32[]{:S(2)}) %collective-permute-start.1) | collective-permute-done | bytes 65568 | tf_op jit(solution)/shard_map/ppermute | solution.py:30
  11.7 6.9 %gate_up.3 = (f32[32,8192]{1,0:T(8,128)S(1)}, f32[32,8192]{1,0:T(8,128)S(1)}) custom-call(bf16[16,2048]{1,0:T(8,128)(2,1)S(1)} %head.1.refs_0_, bf16[16,2048]{1,0:T(8,128)(2,1)S(1)} %collective-permute-done.refs_1_, bf16[16,2048]{1,0:T(8,128)(2,1)S(1)} %collective-permute-done.1.refs_2_, bf16[16,2048]{1,0:T(8,128)(2,1)S(1)} %take.1.refs_3_, ...), custom_call_target="tpu_custom_call" | custom-call | flops 2147483648 | bytes 33554432 | tf_op jit(solution)/shard_map/gate_up/pallas_call | solution.py:94
  18.6 0.1 collective-permute-start.3
  18.7 2.5 %gate_up.4 = (f32[32,1024]{1,0:T(8,128)S(1)}, f32[32,1024]{1,0:T(8,128)S(1)}) custom-call(bf16[16,2048]{1,0:T(8,128)(2,1)S(1)} %head.1.refs_0_, bf16[16,2048]{1,0:T(8,128)(2,1)S(1)} %collective-permute-done.refs_1_, bf16[16,2048]{1,0:T(8,128)(2,1)S(1)} %collective-permute-done.1.refs_2_, bf16[16,2048]{1,0:T(8,128)(2,1)S(1)} %take.1.refs_3_, ...), custom_call_target="tpu_custom_call" | custom-call | flops 268435456 | bytes 4194304 | tf_op jit(solution)/shard_map/gate_up/pallas_call | solution.py:94
  21.2 0.1 collective-permute-done.3.refs_1_
  21.4 0.1 fold.2
  21.5 1.6 %collective-permute-start.4 = (bf16[16,8192]{1,0:T(8,128)(2,1)S(1)}, bf16[16,8192]{1,0:T(8,128)(2,1)S(1)}, u32[]{:S(2)}, u32[]{:S(2)}) collective-permute-start(bf16[16,8192]{1,0:T(8,128)(2,1)S(1)} %get-tuple-element.23.refs_4_), channel_id=1, source_target_pairs={{0,2},{1,3},{2,0},{3,1},{4,6},{5,7},{6,4},{7,5},{8,10},{9,11},{10,... | collective-permute-start | bytes 786440 | tf_op jit(solution)/shard_map/ppermute | solution.py:30
  23.1 4.7 %gate_up.5 = (f32[32,5120]{1,0:T(8,128)S(1)}, f32[32,5120]{1,0:T(8,128)S(1)}) custom-call(bf16[16,2048]{1,0:T(8,128)(2,1)S(1)} %head.1.refs_0_, bf16[16,2048]{1,0:T(8,128)(2,1)S(1)} %collective-permute-done.refs_1_, bf16[16,2048]{1,0:T(8,128)(2,1)S(1)} %collective-permute-done.1.refs_2_, bf16[16,2048]{1,0:T(8,128)(2,1)S(1)} %take.1.refs_3_, ...), custom_call_target="tpu_custom_call" | custom-call | flops 1342177280 | bytes 20971520 | tf_op jit(solution)/shard_map/gate_up/pallas_call | solution.py:94
  27.8 0.5 collective-permute-start.9
  28.3 1.8 %collective-permute-done.4.got = bf16[16,8192]{1,0:T(8,128)(2,1)S(1)} collective-permute-done((bf16[16,8192]{1,0:T(8,128)(2,1)S(1)}, bf16[16,8192]{1,0:T(8,128)(2,1)S(1)}, u32[]{:S(2)}, u32[]{:S(2)}) %collective-permute-start.4) | collective-permute-done | bytes 262176 | tf_op jit(solution)/shard_map/ppermute | solution.py:30
  30.1 0.1 activate.2.refs_4_.refs_0_
  30.2 0.1 fold.3
  30.3 1.6 %collective-permute-start.10 = (bf16[16,6144]{1,0:T(8,128)(2,1)S(1)}, bf16[16,6144]{1,0:T(8,128)(2,1)S(1)}, u32[]{:S(2)}, u32[]{:S(2)}) collective-permute-start(bf16[16,6144]{1,0:T(8,128)(2,1)S(1)} %get-tuple-element.28), channel_id=1, source_target_pairs={{0,2},{1,3},{2,0},{3,1},{4,6},{5,7},{6,4},{7,5},{8,10},{9,11},{10,... | collective-permute-start | bytes 589832 | tf_op jit(solution)/shard_map/ppermute | solution.py:30
  31.9 0.5 collective-permute-start.6
  32.4 5.7 %collective-permute-done.10.got = bf16[16,6144]{1,0:T(8,128)(2,1)S(1)} collective-permute-done((bf16[16,6144]{1,0:T(8,128)(2,1)S(1)}, bf16[16,6144]{1,0:T(8,128)(2,1)S(1)}, u32[]{:S(2)}, u32[]{:S(2)}) %collective-permute-start.10) | collective-permute-done | bytes 196640 | tf_op jit(solution)/shard_map/ppermute | solution.py:30
  38.2 1.6 %collective-permute-start.12 = (bf16[16,3072]{1,0:T(8,128)(2,1)S(1)}, bf16[16,3072]{1,0:T(8,128)(2,1)S(1)}, u32[]{:S(2)}, u32[]{:S(2)}) collective-permute-start(bf16[16,3072]{1,0:T(8,128)(2,1)S(1)} %activate.3.refs_4_), channel_id=1, source_target_pairs={{0,2},{1,3},{2,0},{3,1},{4,6},{5,7},{6,4},{7,5},{8,10},{9,11},{10,... | collective-permute-start | bytes 294920 | tf_op jit(solution)/shard_map/ppermute | solution.py:30
  39.8 1.1 %collective-permute-done.6.refs_2_ = bf16[16,4096]{1,0:T(8,128)(2,1)S(1)} collective-permute-done((bf16[16,4096]{1,0:T(8,128)(2,1)S(1)}, bf16[16,4096]{1,0:T(8,128)(2,1)S(1)}, u32[]{:S(2)}, u32[]{:S(2)}) %collective-permute-start.6) | collective-permute-done | bytes 131104 | tf_op jit(solution)/shard_map/ppermute | solution.py:30
  40.8 0.5 collective-permute-start.11
  41.3 1.5 %collective-permute-done.12.refs_6_ = bf16[16,3072]{1,0:T(8,128)(2,1)S(1)} collective-permute-done((bf16[16,3072]{1,0:T(8,128)(2,1)S(1)}, bf16[16,3072]{1,0:T(8,128)(2,1)S(1)}, u32[]{:S(2)}, u32[]{:S(2)}) %collective-permute-start.12) | collective-permute-done | bytes 98336 | tf_op jit(solution)/shard_map/ppermute | solution.py:30
  42.9 1.3 %collective-permute-done.13.refs_7_ = bf16[16,3072]{1,0:T(8,128)(2,1)S(1)} collective-permute-done((bf16[16,3072]{1,0:T(8,128)(2,1)S(1)}, bf16[16,3072]{1,0:T(8,128)(2,1)S(1)}, u32[]{:S(2)}, u32[]{:S(2)}) %collective-permute-start.13) | collective-permute-done | bytes 98336 | tf_op jit(solution)/shard_map/ppermute | solution.py:30
  44.2 5.2 %down.1 = (f32[16,2048]{1,0:T(8,128)S(1)}, bf16[16,2048]{1,0:T(8,128)(2,1)S(1)}, bf16[16,2048]{1,0:T(8,128)(2,1)S(1)}, bf16[16,2048]{1,0:T(8,128)(2,1)S(1)}) custom-call(bf16[16,4096]{1,0:T(8,128)(2,1)S(1)} %activate.2.refs_4_.refs_0_, bf16[16,4096]{1,0:T(8,128)(2,1)S(1)} %collective-permute-done.5.refs_1_, ...), custom_call_target="tpu_custom_call" | custom-call | flops 1879048192 | bytes 29360128 | tf_op jit(solution)/shard_map/down/pallas_call | solution.py:171
  49.5 2.8 %collective-permute-start.14 = (bf16[16,2048]{1,0:T(8,128)(2,1)S(1)}, bf16[16,2048]{1,0:T(8,128)(2,1)S(1)}, u32[]{:S(2)}, u32[]{:S(2)}) collective-permute-start(bf16[16,2048]{1,0:T(8,128)(2,1)S(1)} %get-tuple-element.30), channel_id=1, source_target_pairs={{0,12},{4,8},{8,4},{12,0},{1,13},{5,9},{9,5},{13,1},{2,14},{6,10},... | collective-permute-start | bytes 196616 | tf_op jit(solution)/shard_map/ppermute | solution.py:30
  52.3 1.6 %collective-permute-start.15 = (bf16[16,2048]{1,0:T(8,128)(2,1)S(1)}, bf16[16,2048]{1,0:T(8,128)(2,1)S(1)}, u32[]{:S(2)}, u32[]{:S(2)}) collective-permute-start(bf16[16,2048]{1,0:T(8,128)(2,1)S(1)} %get-tuple-element.31), channel_id=1, source_target_pairs={{0,8},{4,12},{8,0},{12,4},{1,9},{5,13},{9,1},{13,5},{2,10},{6,14},... | collective-permute-start | bytes 196616 | tf_op jit(solution)/shard_map/ppermute | solution.py:30
  53.9 2.3 %collective-permute-done.14.got = bf16[16,2048]{1,0:T(8,128)(2,1)S(1)} collective-permute-done((bf16[16,2048]{1,0:T(8,128)(2,1)S(1)}, bf16[16,2048]{1,0:T(8,128)(2,1)S(1)}, u32[]{:S(2)}, u32[]{:S(2)}) %collective-permute-start.14) | collective-permute-done | bytes 65568 | tf_op jit(solution)/shard_map/ppermute | solution.py:30
  56.2 1.6 %collective-permute-done.16 = bf16[16,2048]{1,0:T(8,128)(2,1)S(1)} collective-permute-done((bf16[16,2048]{1,0:T(8,128)(2,1)S(1)}, bf16[16,2048]{1,0:T(8,128)(2,1)S(1)}, u32[]{:S(2)}, u32[]{:S(2)}) %collective-permute-start.16) | collective-permute-done | bytes 65568 | tf_op jit(solution)/shard_map/ppermute | solution.py:30
  57.8 0.6 %collective-permute-done.15 = bf16[16,2048]{1,0:T(8,128)(2,1)S(1)} collective-permute-done((bf16[16,2048]{1,0:T(8,128)(2,1)S(1)}, bf16[16,2048]{1,0:T(8,128)(2,1)S(1)}, u32[]{:S(2)}, u32[]{:S(2)}) %collective-permute-start.15) | collective-permute-done | bytes 65568 | tf_op jit(solution)/shard_map/ppermute | solution.py:30
  58.4 0.7 %add_convert_fusion = bf16[16,2048]{1,0:T(8,128)(2,1)} fusion(bf16[16,2048]{1,0:T(8,128)(2,1)S(1)} %collective-permute-done.16, f32[16,2048]{1,0:T(8,128)S(1)} %plus.1, bf16[16,2048]{1,0:T(8,128)(2,1)S(1)} %collective-permute-done.15), kind=kLoop, calls=%fused_computation | loop fusion | flops 163840 | bytes 327680 | tf_op jit(solution)/shard_map/convert_element_type | solution.py:249
  (33 shorter events, 0.2 us)
Async XLA Ops:
  0.0 11.7 %copy-start = (bf16[2048,7168]{1,0:T(8,128)(2,1)S(1)}, bf16[2048,7168]{1,0:T(8,128)(2,1)}, u32[]{:S(2)}) copy-start(bf16[2048,7168]{1,0:T(8,128)(2,1)} %refs_5_.5) | copy-start | bytes 88080384
  0.0 1.0 %copy-start.1 = (bf16[16,2048]{1,0:T(8,128)(2,1)S(1)}, bf16[16,2048]{1,0:T(8,128)(2,1)}, u32[]{:S(2)}) copy-start(bf16[16,2048]{1,0:T(8,128)(2,1)} %given.1) | copy-start | bytes 196612
  1.0 7.9 %collective-permute-start.2 = (bf16[16,2048]{1,0:T(8,128)(2,1)S(1)}, bf16[16,2048]{1,0:T(8,128)(2,1)S(1)}, u32[]{:S(2)}, u32[]{:S(2)}) collective-permute-start(bf16[16,2048]{1,0:T(8,128)(2,1)S(1)} %head.1.refs_0_), channel_id=1, source_target_pairs={{0,12},{4,8},{8,4},{12,0},{1,13},{5,9},{9,5},{13,1},{2,14},{6,10},... | collective-permute-start | bytes 196616 | tf_op jit(solution)/shard_map/ppermute | solution.py:30
  6.0 4.7 %collective-permute-start = (bf16[16,2048]{1,0:T(8,128)(2,1)S(1)}, bf16[16,2048]{1,0:T(8,128)(2,1)S(1)}, u32[]{:S(2)}, u32[]{:S(2)}) collective-permute-start(bf16[16,2048]{1,0:T(8,128)(2,1)S(1)} %head.1.refs_0_), channel_id=1, source_target_pairs={{0,4},{4,0},{8,12},{12,8},{1,5},{5,1},{9,13},{13,9},{2,6},{6,2},{1... | collective-permute-start | bytes 196616 | tf_op jit(solution)/shard_map/ppermute | solution.py:30
  6.1 5.6 %collective-permute-start.1 = (bf16[16,2048]{1,0:T(8,128)(2,1)S(1)}, bf16[16,2048]{1,0:T(8,128)(2,1)S(1)}, u32[]{:S(2)}, u32[]{:S(2)}) collective-permute-start(bf16[16,2048]{1,0:T(8,128)(2,1)S(1)} %head.1.refs_0_), channel_id=1, source_target_pairs={{0,8},{4,12},{8,0},{12,4},{1,9},{5,13},{9,1},{13,5},{2,10},{6,14},... | collective-permute-start | bytes 196616 | tf_op jit(solution)/shard_map/ppermute | solution.py:30
  18.6 2.7 %collective-permute-start.3 = (f32[32,8192]{1,0:T(8,128)S(1)}, f32[32,8192]{1,0:T(8,128)S(1)}, u32[]{:S(2)}, u32[]{:S(2)}) collective-permute-start(f32[32,8192]{1,0:T(8,128)S(1)} %get-tuple-element.20), channel_id=1, source_target_pairs={{0,1},{1,0},{2,3},{3,2},{4,5},{5,4},{6,7},{7,6},{8,9},{9,8},{10,11... | collective-permute-start | bytes 3145736 | tf_op jit(solution)/shard_map/ppermute | solution.py:30
  21.5 8.6 %collective-permute-start.4 = (bf16[16,8192]{1,0:T(8,128)(2,1)S(1)}, bf16[16,8192]{1,0:T(8,128)(2,1)S(1)}, u32[]{:S(2)}, u32[]{:S(2)}) collective-permute-start(bf16[16,8192]{1,0:T(8,128)(2,1)S(1)} %get-tuple-element.23.refs_4_), channel_id=1, source_target_pairs={{0,2},{1,3},{2,0},{3,1},{4,6},{5,7},{6,4},{7,5},{8,10},{9,11},{10,... | collective-permute-start | bytes 786440 | tf_op jit(solution)/shard_map/ppermute | solution.py:30
  23.0 7.2 %collective-permute-start.8 = (f32[32,1024]{1,0:T(8,128)S(1)}, f32[32,1024]{1,0:T(8,128)S(1)}, u32[]{:S(2)}, u32[]{:S(2)}) collective-permute-start(f32[32,1024]{1,0:T(8,128)S(1)} %get-tuple-element.25), channel_id=1, source_target_pairs={{0,1},{1,0},{2,3},{3,2},{4,5},{5,4},{6,7},{7,6},{8,9},{9,8},{10,11... | collective-permute-start | bytes 393224 | tf_op jit(solution)/shard_map/ppermute | solution.py:30
  27.8 2.4 %collective-permute-start.9 = (f32[32,5120]{1,0:T(8,128)S(1)}, f32[32,5120]{1,0:T(8,128)S(1)}, u32[]{:S(2)}, u32[]{:S(2)}) collective-permute-start(f32[32,5120]{1,0:T(8,128)S(1)} %get-tuple-element.26), channel_id=1, source_target_pairs={{0,1},{1,0},{2,3},{3,2},{4,5},{5,4},{6,7},{7,6},{8,9},{9,8},{10,11... | collective-permute-start | bytes 1966088 | tf_op jit(solution)/shard_map/ppermute | solution.py:30
  30.1 14.1 %slice-start = ((s8[29360128]{0:T(1024)(128)(4,1)}), s8[4194304]{0:T(1024)(128)(4,1)S(1)}, s32[]{:S(2)}) async-start(s8[29360128]{0:T(1024)(128)(4,1)} %bitcast), calls=%async_computation | async-start | bytes 8388608
  30.1 14.1 %slice-start.1 = ((s8[29360128]{0:T(1024)(128)(4,1)}), s8[4194304]{0:T(1024)(128)(4,1)S(1)}, s32[]{:S(2)}) async-start(s8[29360128]{0:T(1024)(128)(4,1)} %bitcast), calls=%async_computation.1 | async-start | bytes 8388608
  30.1 14.1 %slice-start.2 = ((s8[29360128]{0:T(1024)(128)(4,1)}), s8[4194304]{0:T(1024)(128)(4,1)S(1)}, s32[]{:S(2)}) async-start(s8[29360128]{0:T(1024)(128)(4,1)} %bitcast), calls=%async_computation.2 | async-start | bytes 8388608
  30.1 14.1 %slice-start.3 = ((s8[29360128]{0:T(1024)(128)(4,1)}), s8[4194304]{0:T(1024)(128)(4,1)S(1)}, s32[]{:S(2)}) async-start(s8[29360128]{0:T(1024)(128)(4,1)} %bitcast), calls=%async_computation.3 | async-start | bytes 8388608
  30.3 7.8 %collective-permute-start.10 = (bf16[16,6144]{1,0:T(8,128)(2,1)S(1)}, bf16[16,6144]{1,0:T(8,128)(2,1)S(1)}, u32[]{:S(2)}, u32[]{:S(2)}) collective-permute-start(bf16[16,6144]{1,0:T(8,128)(2,1)S(1)} %get-tuple-element.28), channel_id=1, source_target_pairs={{0,2},{1,3},{2,0},{3,1},{4,6},{5,7},{6,4},{7,5},{8,10},{9,11},{10,... | collective-permute-start | bytes 589832 | tf_op jit(solution)/shard_map/ppermute | solution.py:30
  31.9 9.0 %collective-permute-start.6 = (bf16[16,4096]{1,0:T(8,128)(2,1)S(1)}, bf16[16,4096]{1,0:T(8,128)(2,1)S(1)}, u32[]{:S(2)}, u32[]{:S(2)}) collective-permute-start(bf16[16,4096]{1,0:T(8,128)(2,1)S(1)} %activate.2.refs_4_.refs_0_), channel_id=1, source_target_pairs={{0,2},{1,3},{2,0},{3,1},{4,6},{5,7},{6,4},{7,5},{8,10},{9,11},{10,... | collective-permute-start | bytes 393224 | tf_op jit(solution)/shard_map/ppermute | solution.py:30
  38.1 6.1 %slice-start.4 = ((s8[29360128]{0:T(1024)(128)(4,1)}), s8[4194304]{0:T(1024)(128)(4,1)S(1)}, s32[]{:S(2)}) async-start(s8[29360128]{0:T(1024)(128)(4,1)} %bitcast), calls=%async_computation.4 | async-start | bytes 8388608
  38.1 6.1 %slice-start.5 = ((s8[29360128]{0:T(1024)(128)(4,1)}), s8[4194304]{0:T(1024)(128)(4,1)S(1)}, s32[]{:S(2)}) async-start(s8[29360128]{0:T(1024)(128)(4,1)} %bitcast), calls=%async_computation.5 | async-start | bytes 8388608
  38.1 6.1 %slice-start.6 = ((s8[29360128]{0:T(1024)(128)(4,1)}), s8[4194304]{0:T(1024)(128)(4,1)S(1)}, s32[]{:S(2)}) async-start(s8[29360128]{0:T(1024)(128)(4,1)} %bitcast), calls=%async_computation.6 | async-start | bytes 8388608
  38.2 4.7 %collective-permute-start.12 = (bf16[16,3072]{1,0:T(8,128)(2,1)S(1)}, bf16[16,3072]{1,0:T(8,128)(2,1)S(1)}, u32[]{:S(2)}, u32[]{:S(2)}) collective-permute-start(bf16[16,3072]{1,0:T(8,128)(2,1)S(1)} %activate.3.refs_4_), channel_id=1, source_target_pairs={{0,2},{1,3},{2,0},{3,1},{4,6},{5,7},{6,4},{7,5},{8,10},{9,11},{10,... | collective-permute-start | bytes 294920 | tf_op jit(solution)/shard_map/ppermute | solution.py:30
  39.8 3.1 %collective-permute-start.5 = (bf16[16,4096]{1,0:T(8,128)(2,1)S(1)}, bf16[16,4096]{1,0:T(8,128)(2,1)S(1)}, u32[]{:S(2)}, u32[]{:S(2)}) collective-permute-start(bf16[16,4096]{1,0:T(8,128)(2,1)S(1)} %activate.2.refs_4_.refs_0_), channel_id=1, source_target_pairs={{0,1},{1,0},{2,3},{3,2},{4,5},{5,4},{6,7},{7,6},{8,9},{9,8},{10,11... | collective-permute-start | bytes 393224 | tf_op jit(solution)/shard_map/ppermute | solution.py:30
  40.8 2.1 %collective-permute-start.7 = (bf16[16,4096]{1,0:T(8,128)(2,1)S(1)}, bf16[16,4096]{1,0:T(8,128)(2,1)S(1)}, u32[]{:S(2)}, u32[]{:S(2)}) collective-permute-start(bf16[16,4096]{1,0:T(8,128)(2,1)S(1)} %collective-permute-done.6.refs_2_), channel_id=1, source_target_pairs={{0,1},{1,0},{2,3},{3,2},{4,5},{5,4},{6,7},{7,6},{8,9},{9,8},{10,11... | collective-permute-start | bytes 393224 | tf_op jit(solution)/shard_map/ppermute | solution.py:30
  40.8 2.1 %collective-permute-start.11 = (bf16[16,3072]{1,0:T(8,128)(2,1)S(1)}, bf16[16,3072]{1,0:T(8,128)(2,1)S(1)}, u32[]{:S(2)}, u32[]{:S(2)}) collective-permute-start(bf16[16,3072]{1,0:T(8,128)(2,1)S(1)} %activate.3.refs_4_), channel_id=1, source_target_pairs={{0,1},{1,0},{2,3},{3,2},{4,5},{5,4},{6,7},{7,6},{8,9},{9,8},{10,11... | collective-permute-start | bytes 294920 | tf_op jit(solution)/shard_map/ppermute | solution.py:30
  42.9 1.3 %collective-permute-start.13 = (bf16[16,3072]{1,0:T(8,128)(2,1)S(1)}, bf16[16,3072]{1,0:T(8,128)(2,1)S(1)}, u32[]{:S(2)}, u32[]{:S(2)}) collective-permute-start(bf16[16,3072]{1,0:T(8,128)(2,1)S(1)} %collective-permute-done.12.refs_6_), channel_id=1, source_target_pairs={{0,1},{1,0},{2,3},{3,2},{4,5},{5,4},{6,7},{7,6},{8,9},{9,8},{10,11... | collective-permute-start | bytes 294920 | tf_op jit(solution)/shard_map/ppermute | solution.py:30
  49.5 6.7 %collective-permute-start.14 = (bf16[16,2048]{1,0:T(8,128)(2,1)S(1)}, bf16[16,2048]{1,0:T(8,128)(2,1)S(1)}, u32[]{:S(2)}, u32[]{:S(2)}) collective-permute-start(bf16[16,2048]{1,0:T(8,128)(2,1)S(1)} %get-tuple-element.30), channel_id=1, source_target_pairs={{0,12},{4,8},{8,4},{12,0},{1,13},{5,9},{9,5},{13,1},{2,14},{6,10},... | collective-permute-start | bytes 196616 | tf_op jit(solution)/shard_map/ppermute | solution.py:30
  52.3 5.5 %collective-permute-start.16 = (bf16[16,2048]{1,0:T(8,128)(2,1)S(1)}, bf16[16,2048]{1,0:T(8,128)(2,1)S(1)}, u32[]{:S(2)}, u32[]{:S(2)}) collective-permute-start(bf16[16,2048]{1,0:T(8,128)(2,1)S(1)} %get-tuple-element.32), channel_id=1, source_target_pairs={{0,4},{4,0},{8,12},{12,8},{1,5},{5,1},{9,13},{13,9},{2,6},{6,2},{1... | collective-permute-start | bytes 196616 | tf_op jit(solution)/shard_map/ppermute | solution.py:30
  52.3 6.1 %collective-permute-start.15 = (bf16[16,2048]{1,0:T(8,128)(2,1)S(1)}, bf16[16,2048]{1,0:T(8,128)(2,1)S(1)}, u32[]{:S(2)}, u32[]{:S(2)}) collective-permute-start(bf16[16,2048]{1,0:T(8,128)(2,1)S(1)} %get-tuple-element.31), channel_id=1, source_target_pairs={{0,8},{4,12},{8,0},{12,4},{1,9},{5,13},{9,1},{13,5},{2,10},{6,14},... | collective-permute-start | bytes 196616 | tf_op jit(solution)/shard_map/ppermute | solution.py:30
